TPU v7x, 512 devices: a whole 4x8x8 slice. The times are simulated.
512 devices in a mesh: guide: 2 (over core), seq: 32 (over z, x), rep: 8 (over y).
Axes of the slice: x: 4, y: 8, z: 8, core: 2. Of those that a mesh axis runs over, the one named last changes fastest.
Arguments:
- queries: bfloat16 [2, 32768, 1536], P('guide', ('rep', 'seq')), parts along dimension 1, may hold values from -125 to 125
- keys: bfloat16 [2, 32768, 1536], P('guide', ('rep', 'seq')), parts along dimension 1, may hold values from -4.5 to 4.5
- values: bfloat16 [2, 32768, 1536], P('guide', ('rep', 'seq')), parts along dimension 1, may hold values from -6 to 6
- hidden_in: bfloat16 [2, 32768, 3072], P(None, ('rep', 'seq'), 'guide'), parts along dimension 1, may hold values from -6 to 6
- out_weight: bfloat16 [1536, 3072], P(None, ('guide', 'seq')), may hold values from -0.15625 to 0.15625
- final_weight: bfloat16 [3072, 64], replicated, may hold values from -0.109375 to 0.109375
- gate_mod: bfloat16 [2, 40, 3072], P(None, 'rep'), parts along dimension 1, may hold values from -4 to 4
- span_tiles: int32 [40], P('rep'), parts along dimension 0, may hold values from 1 to 8, 32 in all
- text_len: int32 [2, 40], P(None, 'rep'), parts along dimension 1, may hold values from 1 to 128
- guide_on: int32 [40], P('rep'), parts along dimension 0, may hold values 0 or 1
- guide_scale: float32 [40], P('rep'), parts along dimension 0, may hold values from 2 to 7
- step_size: float32 [40], P('rep'), parts along dimension 0, may hold values from -0.6 to -0.1
- latent: float32 [32768, 64], P(('rep', 'seq')), parts along dimension 0, may hold values from -6 to 6
Outputs:
- latent_next: float32 [32768, 64], P(('rep', 'seq')), parts along dimension 0
There are 8 independent parts, one for each index of `rep`. A program takes and returns all parts, laid end to end along the dimension named above; an argument that names none is the same for every part. Nothing has to cross between parts.
Inputs may be any that keep to these rules, and one draw needn't show every extreme that they name: `span_tiles`: some request spans exactly 8 tiles.
All inputs are finite; a program needn't handle non-finite values.
Results may differ from a plain program's by a relative error of at most 0.0011.
Values may be sent and summed in bfloat16 or wider, within the bound.
No kernel may reach another device: no remote copies, remote signals or barrier semaphores. Data moves between devices by JAX's collectives and lax.ppermute only.
A program may use at most 128 MiB of HBM per device.

v0:
```python
import jax
import jax.numpy as jnp
from jax import lax
from jax.sharding import PartitionSpec as P

HEAD_WIDTH = 128
TILE = 128
SPAN_MOST = 8


def from_behind(value, axis, by):
    count = lax.axis_size(axis)
    pairs = [(i, i + by) for i in range(count) if 0 <= i + by < count]
    return lax.ppermute(value, axis, pairs)


def swapped(value, axis, stride):
    mask = 2**stride
    pairs = [(source, source ^ mask) for source in range(lax.axis_size(axis))]
    return lax.ppermute(value, axis, pairs)


def layout(positions, span_tiles, text_lens, total):
    ends = jnp.cumsum(span_tiles)
    starts = ends - span_tiles
    tile_of = positions // TILE
    inside = (positions >= 0) & (positions < total)
    member = (
        (tile_of[:, None] >= starts[None, :]) & (tile_of[:, None] < ends[None, :]) & inside[:, None]
    )
    first = jnp.sum(jnp.where(member, starts[None, :], 0), axis=1) * TILE
    tlen = jnp.sum(jnp.where(member, text_lens[None, :], 0), axis=1)
    offset = positions - first
    live = jnp.any(member, axis=1) & ((offset >= TILE) | (offset < tlen))
    return (member, live)


def attend(query, key_rows, value_rows, allowed):
    count = query.shape[0]
    width = key_rows.shape[0]
    query_heads = query.reshape(count, -1, HEAD_WIDTH).transpose(1, 0, 2)
    key_heads = key_rows.reshape(width, -1, HEAD_WIDTH).transpose(1, 0, 2)
    value_heads = value_rows.reshape(width, -1, HEAD_WIDTH).transpose(1, 0, 2)

    def one_head(trio):
        attention_score = jnp.dot(
            trio[0], trio[1].T, preferred_element_type=jnp.float32
        ) * HEAD_WIDTH ** (-0.5)
        attention_score = jnp.where(allowed, attention_score, -jnp.inf)
        top = jnp.max(attention_score, axis=-1, keepdims=True)
        weight = jnp.exp(attention_score - top)
        total = jnp.sum(weight, axis=-1, keepdims=True)
        mixed_output = jnp.dot(
            weight.astype(jnp.bfloat16), trio[2], preferred_element_type=jnp.float32
        )
        return mixed_output / total

    heads_out = lax.map(one_head, (query_heads, key_heads, value_heads))
    return heads_out.transpose(1, 0, 2).reshape(count, -1).astype(jnp.bfloat16)


def guide_mix(cond, uncond, switch, factor):
    blend = jnp.where(switch > 0, uncond + factor * (cond - uncond), cond)
    upper = jnp.sqrt(jnp.mean(cond * cond, axis=-1, keepdims=True) + 1e-06)
    lower = jnp.sqrt(jnp.mean(blend * blend, axis=-1, keepdims=True) + 1e-06)
    return blend * (upper / lower)


def per_token(member, table):
    return jnp.sum(jnp.where(member, table[None, :], jnp.zeros_like(table)[None, :]), axis=1)[
        :, None
    ]


def fetch_direct(stacked, distance):
    return from_behind(stacked, "seq", distance)


def shards(
    queries,
    keys,
    values,
    hidden_in,
    out_weight,
    final_weight,
    gate_mod,
    span_tiles,
    text_len,
    guide_on,
    guide_scale,
    step_size,
    latent,
):
    rows = queries.shape[1]
    local = queries.shape[0]
    guides = lax.axis_size("guide")
    total = rows * lax.axis_size("seq")
    place = lax.axis_index("seq")
    half = lax.axis_index("guide")
    width = hidden_in.shape[2]
    tiles_dev = rows // TILE
    reach = (SPAN_MOST + tiles_dev - 2) // tiles_dev
    own = jnp.stack([keys, values])
    pieces = [own]
    anchors = [place]
    for distance in range(1, reach + 1):
        pieces.append(fetch_direct(own, distance))
        anchors.append(place - distance)
        pieces.append(fetch_direct(own, -distance))
        anchors.append(place + distance)
    store = jnp.concatenate(pieces, axis=2)
    steps_in = jnp.arange(rows, dtype=jnp.int32)
    key_pos = jnp.concatenate([anchor * rows + steps_in for anchor in anchors])
    query_pos = place * rows + steps_in
    member_q = None
    text_lens = lax.dynamic_index_in_dim(text_len, half * local + 0, 0, keepdims=False)
    member_q, live_q = layout(query_pos, span_tiles, text_lens, total)
    member_k, live_k = layout(key_pos, span_tiles, text_lens, total)
    same = (
        jnp.dot(
            member_q.astype(jnp.float32),
            member_k.astype(jnp.float32).T,
            precision=lax.Precision.HIGHEST,
        )
        > 0.5
    )
    allowed = same & live_k[None, :]
    attn_list = attend(queries[0], store[0, 0], store[1, 0], allowed)
    partner = swapped(attn_list, "guide", 0)
    first = jnp.where(half == 0, attn_list, partner)
    second = jnp.where(half == 0, partner, attn_list)
    both = jnp.concatenate([first, second], axis=0)
    mixed_output = jnp.dot(
        both,
        lax.all_gather(out_weight, "seq", axis=1, tiled=True),
        preferred_element_type=jnp.float32,
    ).reshape(2, rows, width)
    columns = lax.dynamic_slice_in_dim(gate_mod, half * width, width, 2).astype(jnp.float32)
    member_f = member_q.astype(jnp.float32)
    gate_rows = jnp.stack(
        [
            jnp.dot(member_f, columns[0], precision=lax.Precision.HIGHEST),
            jnp.dot(member_f, columns[1], precision=lax.Precision.HIGHEST),
        ]
    )
    state = hidden_in.astype(jnp.float32) + gate_rows * mixed_output
    full_width = guides * width
    sums = lax.psum(jnp.sum(state, axis=-1), "guide")
    centre = state - (sums / full_width)[:, :, None]
    squares = lax.psum(jnp.sum(centre * centre, axis=-1), "guide")
    normed = (centre * lax.rsqrt(squares / full_width + 1e-06)[:, :, None]).astype(jnp.bfloat16)
    weight_rows = lax.dynamic_slice_in_dim(final_weight, half * width, width, 0)
    partial_speed = jnp.einsum(
        "gnd,dc->gnc", normed, weight_rows, preferred_element_type=jnp.float32
    )
    switch = per_token(member_q, guide_on)
    factor = per_token(member_q, guide_scale)
    stride = per_token(member_q, step_size)
    speeds = lax.psum(partial_speed, "guide")
    return latent + stride * guide_mix(speeds[0], speeds[1], switch, factor)


def solution(mesh):
    in_specs = (
        P("guide", ("rep", "seq"), None),
        P("guide", ("rep", "seq"), None),
        P("guide", ("rep", "seq"), None),
        P(None, ("rep", "seq"), "guide"),
        P(None, ("guide", "seq")),
        P(),
        P(None, "rep", None),
        P("rep"),
        P(None, "rep"),
        P("rep"),
        P("rep"),
        P("rep"),
        P(("rep", "seq"), None),
    )
    out_specs = P(("rep", "seq"), None)
    return jax.shard_map(shards, mesh=mesh, in_specs=in_specs, out_specs=out_specs, check_vma=False)
```

profile of v0, /device:TPU:1, one launch (start us, length us, event | category | flops | bytes accessed | tf_op | source)
XLA Modules:
  0.0 357.0 jit_solution(14683461238505986990)
XLA Ops:
  10.5 4.8 %collective-permute-start = (bf16[2,1,128,1536]{2,3,1,0:T(8,128)(2,1)}, bf16[2,1,128,1536]{2,3,1,0:T(8,128)(2,1)}, u32[]{:S(2)}, u32[]{:S(2)}) collective-permute-start(bf16[2,1,128,1536]{2,3,1,0:T(8,128)(2,1)} %get-tuple-element.78), channel_id=1, source_target_pairs={{0,8},{8,16},{16,24},{24,32},{32,40},{40,48},{48,56},{56,64},{64,7... | collective-permute-start | bytes 2359304 | tf_op jit(solution)/shard_map/ppermute | solution.py:14
  16.6 4.7 %collective-permute-start.2 = (bf16[2,1,128,1536]{2,3,1,0:T(8,128)(2,1)}, bf16[2,1,128,1536]{2,3,1,0:T(8,128)(2,1)S(1)}, u32[]{:S(2)}, u32[]{:S(2)}) collective-permute-start(bf16[2,1,128,1536]{2,3,1,0:T(8,128)(2,1)} %get-tuple-element.78), channel_id=1, source_target_pairs={{0,16},{8,24},{16,32},{24,40},{32,48},{40,56},{48,64},{56,72},{64,... | collective-permute-start | bytes 2359304 | tf_op jit(solution)/shard_map/ppermute | solution.py:14
  22.6 5.8 %collective-permute-start.4 = (bf16[2,1,128,1536]{2,3,1,0:T(8,128)(2,1)}, bf16[2,1,128,1536]{2,3,1,0:T(8,128)(2,1)S(1)}, u32[]{:S(2)}, u32[]{:S(2)}) collective-permute-start(bf16[2,1,128,1536]{2,3,1,0:T(8,128)(2,1)} %get-tuple-element.78), channel_id=1, source_target_pairs={{0,24},{8,32},{16,40},{24,48},{32,56},{40,64},{48,72},{56,80},{64,... | collective-permute-start | bytes 2359304 | tf_op jit(solution)/shard_map/ppermute | solution.py:14
  35.9 2.2 constant_dynamic-update-slice_fusion.14
  38.1 35.1 %collective-permute-start.6 = (bf16[2,1,128,1536]{2,3,1,0:T(8,128)(2,1)}, bf16[2,1,128,1536]{2,3,1,0:T(8,128)(2,1)S(1)}, u32[]{:S(2)}, u32[]{:S(2)}) collective-permute-start(bf16[2,1,128,1536]{2,3,1,0:T(8,128)(2,1)} %get-tuple-element.78), channel_id=1, source_target_pairs={{0,32},{8,40},{16,48},{24,56},{32,64},{40,72},{48,80},{56,88},{64,... | collective-permute-start | bytes 2359304 | tf_op jit(solution)/shard_map/ppermute | solution.py:14
  73.2 2.2 constant_dynamic-update-slice_fusion.13
  77.8 23.4 %collective-permute-start.8 = (bf16[2,1,128,1536]{2,3,1,0:T(8,128)(2,1)}, bf16[2,1,128,1536]{2,3,1,0:T(8,128)(2,1)S(1)}, u32[]{:S(2)}, u32[]{:S(2)}) collective-permute-start(bf16[2,1,128,1536]{2,3,1,0:T(8,128)(2,1)} %get-tuple-element.78), channel_id=1, source_target_pairs={{0,40},{8,48},{16,56},{24,64},{32,72},{40,80},{48,88},{56,96},{64,... | collective-permute-start | bytes 2359304 | tf_op jit(solution)/shard_map/ppermute | solution.py:14
  104.5 4.3 %collective-permute-start.10 = (bf16[2,1,128,1536]{2,3,1,0:T(8,128)(2,1)}, bf16[2,1,128,1536]{2,3,1,0:T(8,128)(2,1)S(1)}, u32[]{:S(2)}, u32[]{:S(2)}) collective-permute-start(bf16[2,1,128,1536]{2,3,1,0:T(8,128)(2,1)} %get-tuple-element.78), channel_id=1, source_target_pairs={{0,48},{8,56},{16,64},{24,72},{32,80},{40,88},{48,96},{56,104},{64... | collective-permute-start | bytes 2359304 | tf_op jit(solution)/shard_map/ppermute | solution.py:14
  112.2 10.2 %collective-permute-start.12 = (bf16[2,1,128,1536]{2,3,1,0:T(8,128)(2,1)}, bf16[2,1,128,1536]{2,3,1,0:T(8,128)(2,1)S(1)}, u32[]{:S(2)}, u32[]{:S(2)}) collective-permute-start(bf16[2,1,128,1536]{2,3,1,0:T(8,128)(2,1)} %get-tuple-element.78), channel_id=1, source_target_pairs={{0,56},{8,64},{16,72},{24,80},{32,88},{40,96},{48,104},{56,112},{6... | collective-permute-start | bytes 2359304 | tf_op jit(solution)/shard_map/ppermute | solution.py:14
  127.0 8.5 %collective-permute-done.10 = bf16[2,1,128,1536]{2,3,1,0:T(8,128)(2,1)S(1)} collective-permute-done((bf16[2,1,128,1536]{2,3,1,0:T(8,128)(2,1)}, bf16[2,1,128,1536]{2,3,1,0:T(8,128)(2,1)S(1)}, u32[]{:S(2)}, u32[]{:S(2)}) %collective-permute-start.10) | collective-permute-done | bytes 786464 | tf_op jit(solution)/shard_map/ppermute | solution.py:14
  136.6 8.8 %collective-permute-done.11 = bf16[2,1,128,1536]{2,3,1,0:T(8,128)(2,1)S(1)} collective-permute-done((bf16[2,1,128,1536]{2,3,1,0:T(8,128)(2,1)}, bf16[2,1,128,1536]{2,3,1,0:T(8,128)(2,1)S(1)}, u32[]{:S(2)}, u32[]{:S(2)}) %collective-permute-start.11) | collective-permute-done | bytes 786464 | tf_op jit(solution)/shard_map/ppermute | solution.py:14
  146.4 21.9 %collective-permute-done.12 = bf16[2,1,128,1536]{2,3,1,0:T(8,128)(2,1)S(1)} collective-permute-done((bf16[2,1,128,1536]{2,3,1,0:T(8,128)(2,1)}, bf16[2,1,128,1536]{2,3,1,0:T(8,128)(2,1)S(1)}, u32[]{:S(2)}, u32[]{:S(2)}) %collective-permute-start.12) | collective-permute-done | bytes 786464 | tf_op jit(solution)/shard_map/ppermute | solution.py:14
  169.3 10.9 %collective-permute-done.13 = bf16[2,1,128,1536]{2,3,1,0:T(8,128)(2,1)S(1)} collective-permute-done((bf16[2,1,128,1536]{2,3,1,0:T(8,128)(2,1)}, bf16[2,1,128,1536]{2,3,1,0:T(8,128)(2,1)S(1)}, u32[]{:S(2)}, u32[]{:S(2)}) %collective-permute-start.13) | collective-permute-done | bytes 786464 | tf_op jit(solution)/shard_map/ppermute | solution.py:14
  181.3 9.8 %fusion.34 = (bf16[1,1,1920,1536]{2,3,1,0:T(8,128)(2,1)}, bf16[1,1,1920,1536]{2,3,1,0:T(8,128)(2,1)}) fusion(bf16[2,1,1920,1536]{2,3,1,0:T(8,128)(2,1)} %constant_dynamic-update-slice_fusion.1), kind=kLoop, calls=%fused_computation.112 | loop fusion | bytes 23592960 | tf_op jit(solution)/shard_map/slice | solution.py:128
  191.1 39.7 %while.10 = (s32[]{:T(128)}, bf16[12,128,128]{1,2,0:T(8,128)(2,1)S(1)}, bf16[12,128,128]{1,2,0:T(8,128)(2,1)S(1)}, bf16[12,1920,128]{1,2,0:T(8,128)(2,1)}, pred[...) while((s32[]{:T(128)}, bf16[12,128,128]{1,2,0:T(8,128)(2,1)S(1)}, ...), condition=%wide.region_9.10_spmd, body=%wide.region_6.9_spmd.sunk | while | flops 127581952 | bytes 4378705 | solution.py:58
  191.1 1.5 fusion.46
  194.4 1.5 fusion.46
  197.7 1.5 fusion.46
  201.1 1.5 fusion.46
  204.4 1.5 fusion.46
  207.7 1.5 fusion.46
  211.0 1.5 fusion.46
  214.3 1.5 fusion.46
  217.6 1.5 fusion.46
  220.9 1.5 fusion.46
  224.2 1.5 fusion.46
  227.5 1.4 fusion.46
  230.8 9.6 %collective-permute-start.14 = (bf16[128,1536]{0,1:T(8,128)(2,1)S(1)}, bf16[128,1536]{0,1:T(8,128)(2,1)S(1)}, u32[]{:S(2)}, u32[]{:S(2)}) collective-permute-start(bf16[128,1536]{0,1:T(8,128)(2,1)S(1)} %bitcast.89), channel_id=1, source_target_pairs={{0,256},{256,0},{1,257},{257,1},{2,258},{258,2},{3,259},{259,3},{4... | collective-permute-start | bytes 1179656 | tf_op jit(solution)/shard_map/ppermute | solution.py:20
  241.9 3.8 %fusion.17 = f32[256,1536]{1,0:T(8,128)S(1)} fusion(bf16[1536,1536]{0,1:T(8,128)(2,1)} %all-gather.2.cloned.1.call-done, bf16[128,1536]{0,1:T(8,128)(2,1)S(1)} %get-tuple-element.77, bf16[128,1536]{0,1:T(8,128)(2,1)S(1)} %get-tuple-element.76), kind=kOutput, calls=%fused_computation.27 | convolution fusion | flops 1209532416 | bytes 7077888 | tf_op jit(solution)/shard_map/dot_general | solution.py:133
  247.1 2.5 psum.21
  249.9 2.5 psum.22
  254.2 93.7 %all-reduce.2.cloned.1.call-done = f32[2,128,64]{1,2,0:T(8,128)} async-done(((f32[2,128,64]{1,2,0:T(8,128)}), f32[2,128,64]{1,2,0:T(8,128)}) %all-reduce.2.cloned.1.call-update) | async-done | bytes 65552 | tf_op jit(solution)/shard_map/psum | solution.py:159
  (135 shorter events, 60.6 us)
Async XLA Ops:
  6.5 245.8 %copy-start = (bf16[3072,64]{0,1:T(8,128)(2,1)S(1)}, bf16[3072,64]{0,1:T(8,128)(2,1)}, u32[]{:S(2)}) copy-start(bf16[3072,64]{0,1:T(8,128)(2,1)} %param.20) | copy-start | bytes 1179652
  6.5 235.3 %all-gather.2.cloned.1.call-start = ((), (), s32[]{:S(2)}) async-start(), calls=%async_computation | async-start | bytes 4866048 | tf_op jit(solution)/shard_map/all_gather | solution.py:135
  10.5 24.2 %collective-permute-start = (bf16[2,1,128,1536]{2,3,1,0:T(8,128)(2,1)}, bf16[2,1,128,1536]{2,3,1,0:T(8,128)(2,1)}, u32[]{:S(2)}, u32[]{:S(2)}) collective-permute-start(bf16[2,1,128,1536]{2,3,1,0:T(8,128)(2,1)} %get-tuple-element.78), channel_id=1, source_target_pairs={{0,8},{8,16},{16,24},{24,32},{32,40},{40,48},{48,56},{56,64},{64,7... | collective-permute-start | bytes 2359304 | tf_op jit(solution)/shard_map/ppermute | solution.py:14
  15.3 22.8 %collective-permute-start.1 = (bf16[2,1,128,1536]{2,3,1,0:T(8,128)(2,1)}, bf16[2,1,128,1536]{2,3,1,0:T(8,128)(2,1)}, u32[]{:S(2)}, u32[]{:S(2)}) collective-permute-start(bf16[2,1,128,1536]{2,3,1,0:T(8,128)(2,1)} %get-tuple-element.78), channel_id=1, source_target_pairs={{8,0},{16,8},{24,16},{32,24},{40,32},{48,40},{56,48},{64,56},{72,6... | collective-permute-start | bytes 2359304 | tf_op jit(solution)/shard_map/ppermute | solution.py:14
  16.6 58.9 %collective-permute-start.2 = (bf16[2,1,128,1536]{2,3,1,0:T(8,128)(2,1)}, bf16[2,1,128,1536]{2,3,1,0:T(8,128)(2,1)S(1)}, u32[]{:S(2)}, u32[]{:S(2)}) collective-permute-start(bf16[2,1,128,1536]{2,3,1,0:T(8,128)(2,1)} %get-tuple-element.78), channel_id=1, source_target_pairs={{0,16},{8,24},{16,32},{24,40},{32,48},{40,56},{48,64},{56,72},{64,... | collective-permute-start | bytes 2359304 | tf_op jit(solution)/shard_map/ppermute | solution.py:14
  21.3 56.5 %collective-permute-start.3 = (bf16[2,1,128,1536]{2,3,1,0:T(8,128)(2,1)}, bf16[2,1,128,1536]{2,3,1,0:T(8,128)(2,1)S(1)}, u32[]{:S(2)}, u32[]{:S(2)}) collective-permute-start(bf16[2,1,128,1536]{2,3,1,0:T(8,128)(2,1)} %get-tuple-element.78), channel_id=1, source_target_pairs={{16,0},{24,8},{32,16},{40,24},{48,32},{56,40},{64,48},{72,56},{80,... | collective-permute-start | bytes 2359304 | tf_op jit(solution)/shard_map/ppermute | solution.py:14
  22.6 79.6 %collective-permute-start.4 = (bf16[2,1,128,1536]{2,3,1,0:T(8,128)(2,1)}, bf16[2,1,128,1536]{2,3,1,0:T(8,128)(2,1)S(1)}, u32[]{:S(2)}, u32[]{:S(2)}) collective-permute-start(bf16[2,1,128,1536]{2,3,1,0:T(8,128)(2,1)} %get-tuple-element.78), channel_id=1, source_target_pairs={{0,24},{8,32},{16,40},{24,48},{32,56},{40,64},{48,72},{56,80},{64,... | collective-permute-start | bytes 2359304 | tf_op jit(solution)/shard_map/ppermute | solution.py:14
  28.4 319.5 %all-reduce.2.cloned.1.call-start = ((), (), s32[]{:S(2)}) async-start(), calls=%async_computation.1 | async-start | bytes 131072 | tf_op jit(solution)/shard_map/psum | solution.py:159
  34.6 69.9 %collective-permute-start.5 = (bf16[2,1,128,1536]{2,3,1,0:T(8,128)(2,1)}, bf16[2,1,128,1536]{2,3,1,0:T(8,128)(2,1)S(1)}, u32[]{:S(2)}, u32[]{:S(2)}) collective-permute-start(bf16[2,1,128,1536]{2,3,1,0:T(8,128)(2,1)} %get-tuple-element.78), channel_id=1, source_target_pairs={{24,0},{32,8},{40,16},{48,24},{56,32},{64,40},{72,48},{80,56},{88,... | collective-permute-start | bytes 2359304 | tf_op jit(solution)/shard_map/ppermute | solution.py:14
  38.1 71.8 %collective-permute-start.6 = (bf16[2,1,128,1536]{2,3,1,0:T(8,128)(2,1)}, bf16[2,1,128,1536]{2,3,1,0:T(8,128)(2,1)S(1)}, u32[]{:S(2)}, u32[]{:S(2)}) collective-permute-start(bf16[2,1,128,1536]{2,3,1,0:T(8,128)(2,1)} %get-tuple-element.78), channel_id=1, source_target_pairs={{0,32},{8,40},{16,48},{24,56},{32,64},{40,72},{48,80},{56,88},{64,... | collective-permute-start | bytes 2359304 | tf_op jit(solution)/shard_map/ppermute | solution.py:14
  75.4 36.8 %collective-permute-start.7 = (bf16[2,1,128,1536]{2,3,1,0:T(8,128)(2,1)}, bf16[2,1,128,1536]{2,3,1,0:T(8,128)(2,1)S(1)}, u32[]{:S(2)}, u32[]{:S(2)}) collective-permute-start(bf16[2,1,128,1536]{2,3,1,0:T(8,128)(2,1)} %get-tuple-element.78), channel_id=1, source_target_pairs={{32,0},{40,8},{48,16},{56,24},{64,32},{72,40},{80,48},{88,56},{96,... | collective-permute-start | bytes 2359304 | tf_op jit(solution)/shard_map/ppermute | solution.py:14
  77.8 45.7 %collective-permute-start.8 = (bf16[2,1,128,1536]{2,3,1,0:T(8,128)(2,1)}, bf16[2,1,128,1536]{2,3,1,0:T(8,128)(2,1)S(1)}, u32[]{:S(2)}, u32[]{:S(2)}) collective-permute-start(bf16[2,1,128,1536]{2,3,1,0:T(8,128)(2,1)} %get-tuple-element.78), channel_id=1, source_target_pairs={{0,40},{8,48},{16,56},{24,64},{32,72},{40,80},{48,88},{56,96},{64,... | collective-permute-start | bytes 2359304 | tf_op jit(solution)/shard_map/ppermute | solution.py:14
  102.2 23.8 %collective-permute-start.9 = (bf16[2,1,128,1536]{2,3,1,0:T(8,128)(2,1)}, bf16[2,1,128,1536]{2,3,1,0:T(8,128)(2,1)S(1)}, u32[]{:S(2)}, u32[]{:S(2)}) collective-permute-start(bf16[2,1,128,1536]{2,3,1,0:T(8,128)(2,1)} %get-tuple-element.78), channel_id=1, source_target_pairs={{40,0},{48,8},{56,16},{64,24},{72,32},{80,40},{88,48},{96,56},{104... | collective-permute-start | bytes 2359304 | tf_op jit(solution)/shard_map/ppermute | solution.py:14
  104.5 31.1 %collective-permute-start.10 = (bf16[2,1,128,1536]{2,3,1,0:T(8,128)(2,1)}, bf16[2,1,128,1536]{2,3,1,0:T(8,128)(2,1)S(1)}, u32[]{:S(2)}, u32[]{:S(2)}) collective-permute-start(bf16[2,1,128,1536]{2,3,1,0:T(8,128)(2,1)} %get-tuple-element.78), channel_id=1, source_target_pairs={{0,48},{8,56},{16,64},{24,72},{32,80},{40,88},{48,96},{56,104},{64... | collective-permute-start | bytes 2359304 | tf_op jit(solution)/shard_map/ppermute | solution.py:14
  109.9 35.4 %collective-permute-start.11 = (bf16[2,1,128,1536]{2,3,1,0:T(8,128)(2,1)}, bf16[2,1,128,1536]{2,3,1,0:T(8,128)(2,1)S(1)}, u32[]{:S(2)}, u32[]{:S(2)}) collective-permute-start(bf16[2,1,128,1536]{2,3,1,0:T(8,128)(2,1)} %get-tuple-element.78), channel_id=1, source_target_pairs={{48,0},{56,8},{64,16},{72,24},{80,32},{88,40},{96,48},{104,56},{11... | collective-permute-start | bytes 2359304 | tf_op jit(solution)/shard_map/ppermute | solution.py:14
  112.2 56.0 %collective-permute-start.12 = (bf16[2,1,128,1536]{2,3,1,0:T(8,128)(2,1)}, bf16[2,1,128,1536]{2,3,1,0:T(8,128)(2,1)S(1)}, u32[]{:S(2)}, u32[]{:S(2)}) collective-permute-start(bf16[2,1,128,1536]{2,3,1,0:T(8,128)(2,1)} %get-tuple-element.78), channel_id=1, source_target_pairs={{0,56},{8,64},{16,72},{24,80},{32,88},{40,96},{48,104},{56,112},{6... | collective-permute-start | bytes 2359304 | tf_op jit(solution)/shard_map/ppermute | solution.py:14
  123.5 56.8 %collective-permute-start.13 = (bf16[2,1,128,1536]{2,3,1,0:T(8,128)(2,1)}, bf16[2,1,128,1536]{2,3,1,0:T(8,128)(2,1)S(1)}, u32[]{:S(2)}, u32[]{:S(2)}) collective-permute-start(bf16[2,1,128,1536]{2,3,1,0:T(8,128)(2,1)} %get-tuple-element.78), channel_id=1, source_target_pairs={{56,0},{64,8},{72,16},{80,24},{88,32},{96,40},{104,48},{112,56},{1... | collective-permute-start | bytes 2359304 | tf_op jit(solution)/shard_map/ppermute | solution.py:14
  181.3 9.8 %copy-start.1 = (bf16[12,128,128]{1,2,0:T(8,128)(2,1)S(1)}, bf16[12,128,128]{1,2,0:T(8,128)(2,1)}, u32[]{:S(2)}) copy-start(bf16[12,128,128]{1,2,0:T(8,128)(2,1)} %custom-call.2) | copy-start | bytes 1179652
  230.8 22.7 %copy-start.2 = (f32[5]{0:T(128)S(1)}, f32[5]{0:T(128)}, u32[]{:S(2)}) copy-start(f32[5]{0:T(128)} %param.26) | copy-start | bytes 64
  230.8 11.0 %collective-permute-start.14 = (bf16[128,1536]{0,1:T(8,128)(2,1)S(1)}, bf16[128,1536]{0,1:T(8,128)(2,1)S(1)}, u32[]{:S(2)}, u32[]{:S(2)}) collective-permute-start(bf16[128,1536]{0,1:T(8,128)(2,1)S(1)} %bitcast.89), channel_id=1, source_target_pairs={{0,256},{256,0},{1,257},{257,1},{2,258},{258,2},{3,259},{259,3},{4... | collective-permute-start | bytes 1179656 | tf_op jit(solution)/shard_map/ppermute | solution.py:20
Sparse Core Ops, SparseCore 0:
  28.6 204.3 all-gather.1
  253.6 94.3 all-reduce.1
where the time goes:
time: 359 us; the launch traced here: 357 us
  waiting for transfers between devices  145 us (40%)
  starting transfers between devices  107 us (30%)
  matrix products  40.2 us (11%)
  local copies, waits for them, and re-layouts  33.5 us (9%)
  between operations  13.9 us (4%)
  other arithmetic  12.4 us (3%)
  blocking collectives  4.97 us (1%)
    ppermute x14, starting transfers between devices, from_behind(): return lax.ppermute(value, axis, pairs)  97.4 us
    psum x1, waiting for transfers between devices, shards(): speeds = lax.psum(partial_speed, 'guide')  93.7 us
    ppermute x14, waiting for transfers between devices, from_behind(): return lax.ppermute(value, axis, pairs)  50.3 us
    unnamed x22, local copies, waits for them, and re-layouts  19.6 us
    dot_general x12, matrix products, one_head(): jnp.dot(trio[0], trio[1].T, preferred_element_type=jnp.float32)  17.5 us
    dot_general x12, matrix products, one_head(): jnp.dot(weight.astype(jnp.bfloat16), trio[2], preferred_element_type=jnp....  16.7 us
    slice x1, local copies, waits for them, and re-layouts, shards(): attn_list = attend(queries[0], store[0, 0], store[1, 0], allowed)  9.76 us
    ppermute x1, starting transfers between devices, swapped(): return lax.ppermute(value, axis, pairs)  9.62 us
  transfers between devices with their start and end apart: 17, of which 7 were waited for; matrix products, arithmetic and copies ran while one was open for 21% of the time, Pallas kernels for 0%

commit v1 on v0

v1 whole, which is shorter than its diff:
```python
import jax
import jax.numpy as jnp
from jax import lax
from jax.experimental import pallas as pl
from jax.experimental.pallas import tpu as pltpu
from jax.sharding import PartitionSpec as P

HEAD_WIDTH = 128
TILE = 128
SPAN_MOST = 8
FULL_WIDTH = 3072
ROW = 4
LOG2E = 1.4426950408889634
NT = (((1,), (1,)), ((), ()))


def swapped(value):
    return lax.ppermute(value, "guide", [(0, 1), (1, 0)])


def along_z(value, by):
    count = lax.axis_size("seq")
    step = by * ROW
    pairs = [(i, i + step) for i in range(count) if 0 <= i + step < count]
    return lax.ppermute(value, "seq", pairs)


def spread(value):
    count = lax.axis_size("seq")
    groups = [[z * ROW + x for x in range(ROW)] for z in range(count // ROW)]
    return lax.all_to_all(value, "seq", 0, 0, axis_index_groups=groups)


def by_features(value):
    rows, width = value.shape
    return value.reshape(rows, ROW, width // ROW).transpose(1, 0, 2)


def request_of(tile, spans, tables):
    start = jnp.int32(0)
    found = [jnp.int32(0) for _ in range(len(tables) + 3)]
    for r in range(spans.shape[0]):
        span = spans[r]
        here = (tile >= start) & (tile < start + span)
        row = [start, span, jnp.int32(r)] + [table(r) for table in tables]
        found = [jnp.where(here, new, old) for new, old in zip(row, found)]
        start = start + span
    return found


def attend_kernel(
    where, spans, text_len, q_ref, far_l, near_l, own, near_r, far_r, o_ref, k_all, v_all
):
    place, half = where[0], where[1]
    first = (place // ROW) * ROW
    heads = q_ref.shape[2] // HEAD_WIDTH
    at = 0
    for ref in (far_l, near_l, own, near_r, far_r):
        for i in range(ref.shape[0]):
            k_all[at * TILE : (at + 1) * TILE, :] = ref[i, 0]
            v_all[at * TILE : (at + 1) * TILE, :] = ref[i, 1]
            at += 1
    keys = SPAN_MOST * TILE
    column = lax.broadcasted_iota(jnp.int32, (1, keys), 1)
    factor = HEAD_WIDTH**-0.5 * LOG2E
    for t in range(ROW):
        start, span, _, live = request_of(first + t, spans, [lambda r: text_len[half, r]])
        begin = jnp.clip(start - (first - (SPAN_MOST - 1)), 0, SPAN_MOST + ROW - 2)
        begin = pl.multiple_of(begin * TILE, TILE)
        allowed = ((column < live) | (column >= TILE)) & (column < span * TILE)
        bias = jnp.where(allowed, 0.0, -1e30)
        for h in range(heads):
            lanes = slice(h * HEAD_WIDTH, (h + 1) * HEAD_WIDTH)
            key = k_all[pl.ds(begin, keys), lanes]
            value = v_all[pl.ds(begin, keys), lanes]
            score = lax.dot_general(
                q_ref[t, :, lanes], key, NT, preferred_element_type=jnp.float32
            )
            score = score + bias
            top = jnp.max(score, axis=-1, keepdims=True)
            weight = jnp.exp2((score - top) * factor)
            total = jnp.sum(weight, axis=-1, keepdims=True)
            mixed = jnp.dot(weight.astype(jnp.bfloat16), value, preferred_element_type=jnp.float32)
            o_ref[t, :, lanes] = (mixed / total).astype(jnp.bfloat16)


def attend(where, spans, text_len, q, far_l, near_l, own, near_r, far_r):
    rows = (SPAN_MOST * 2 + ROW - 2) * TILE
    width = q.shape[2]
    smem = pl.BlockSpec(memory_space=pltpu.SMEM)
    vmem = pl.BlockSpec(memory_space=pltpu.VMEM)
    pairs = ROW * TILE * SPAN_MOST * TILE * (width // HEAD_WIDTH)
    return pl.pallas_call(
        attend_kernel,
        out_shape=jax.ShapeDtypeStruct(q.shape, jnp.bfloat16),
        in_specs=[smem] * 3 + [vmem] * 6,
        out_specs=vmem,
        scratch_shapes=[
            pltpu.VMEM((rows, width), jnp.bfloat16),
            pltpu.VMEM((rows, width), jnp.bfloat16),
        ],
        compiler_params=pltpu.CompilerParams(vmem_limit_bytes=40 << 20),
        cost_estimate=pl.CostEstimate(
            flops=4 * pairs * HEAD_WIDTH, bytes_accessed=8 << 20, transcendentals=pairs
        ),
        name="attend",
    )(where, spans, text_len, q, far_l, near_l, own, near_r, far_r)


def project_kernel(
    where, spans, mine, theirs, w_ref, hidden, gate, final_t, sums, colsum, state
):
    step = pl.program_id(0)
    place, half = where[0], where[1]
    _, _, request = request_of(place, spans, [])
    block = w_ref.shape[0]
    width = state.shape[2]
    here = pl.multiple_of(half * width + step * block, 128)
    groups, _, depth = mine.shape
    for side, source in enumerate((mine, theirs)):
        which = half if side == 0 else 1 - half
        total = jnp.zeros((TILE, block), jnp.float32)
        for j in range(groups):
            total += lax.dot_general(
                source[j],
                w_ref[:, j * depth : (j + 1) * depth],
                NT,
                preferred_element_type=jnp.float32,
            )
        scale = jnp.zeros((1, block), jnp.float32)
        for r in range(gate.shape[1]):
            row = gate[which, r : r + 1, pl.ds(here, block)].astype(jnp.float32)
            scale = jnp.where(request == r, row, scale)
        state[which, :, pl.ds(pl.multiple_of(step * block, 128), block)] = (
            hidden[which].astype(jnp.float32) + scale * total
        )

    @pl.when(step == 0)
    def _():
        ones = jnp.ones((8, width), jnp.bfloat16)
        other = pl.multiple_of((1 - half) * width, 128)
        base = pl.multiple_of(half * width, 128)
        mine_sum = lax.dot_general(
            ones, final_t[:, pl.ds(base, width)], NT, preferred_element_type=jnp.float32
        )
        other_sum = lax.dot_general(
            ones, final_t[:, pl.ds(other, width)], NT, preferred_element_type=jnp.float32
        )
        colsum[...] = mine_sum - other_sum

    @pl.when(step == pl.num_programs(0) - 1)
    def _():
        weights = final_t[:, pl.ds(pl.multiple_of(half * width, 128), width)]
        channels = weights.shape[0]
        lane = lax.broadcasted_iota(jnp.int32, (TILE, sums.shape[2] - channels), 1)
        for which in range(2):
            rows = state[which]
            mean = jnp.mean(rows, axis=-1, keepdims=True)
            centre = rows - mean
            squares = jnp.sum(centre * centre, axis=-1, keepdims=True)
            high = centre.astype(jnp.bfloat16)
            low = (centre - high.astype(jnp.float32)).astype(jnp.bfloat16)
            speed = lax.dot_general(high, weights, NT, preferred_element_type=jnp.float32)
            speed += lax.dot_general(low, weights, NT, preferred_element_type=jnp.float32)
            sums[which, :, :channels] = speed
            sums[which, :, channels:] = jnp.where(
                lane == 0, mean, jnp.where(lane == 1, squares, 0.0)
            )


def project(where, spans, mine, theirs, weight_t, hidden, gate, final_t):
    steps = 4
    depth, width = weight_t.shape[1], weight_t.shape[0]
    block = width // steps
    channels = final_t.shape[0]
    smem = pl.BlockSpec(memory_space=pltpu.SMEM)
    vmem = pl.BlockSpec(memory_space=pltpu.VMEM)
    return pl.pallas_call(
        project_kernel,
        grid=(steps,),
        out_shape=(
            jax.ShapeDtypeStruct((2, TILE, 2 * channels), jnp.float32),
            jax.ShapeDtypeStruct((8, channels), jnp.float32),
        ),
        in_specs=[
            smem,
            smem,
            vmem,
            vmem,
            pl.BlockSpec((block, depth), lambda i: (i, 0)),
            pl.BlockSpec((2, TILE, block), lambda i: (0, 0, i)),
            vmem,
            vmem,
        ],
        out_specs=(vmem, vmem),
        scratch_shapes=[pltpu.VMEM((2, TILE, width), jnp.float32)],
        compiler_params=pltpu.CompilerParams(vmem_limit_bytes=40 << 20),
        cost_estimate=pl.CostEstimate(
            flops=4 * TILE * depth * width, bytes_accessed=8 << 20, transcendentals=0
        ),
        name="project",
    )(where, spans, mine, theirs, weight_t, hidden, gate, final_t)


def finish_kernel(where, spans, on, scales, strides, mine, theirs, colsum, latent_t, out_t):
    _, _, _, switch, factor, stride = request_of(
        where[0], spans, [lambda r: on[r], lambda r: scales[r], lambda r: strides[r]]
    )
    channels = latent_t.shape[0]
    full = FULL_WIDTH
    speeds = []
    for which in range(2):
        a, b = mine[which], theirs[which]
        gap = a[:, channels : channels + 1] - b[:, channels : channels + 1]
        squares = a[:, channels + 1 : channels + 2] + b[:, channels + 1 : channels + 2]
        spread_of = squares + gap * gap * (full / 4)
        raw = a[:, :channels] + b[:, :channels] + (0.5 * gap) * colsum[0:1, :]
        speeds.append(raw * lax.rsqrt(spread_of / full + 1e-06))
    cond, uncond = speeds
    blend = jnp.where(switch > 0, uncond + factor * (cond - uncond), cond)
    upper = jnp.sqrt(jnp.mean(cond * cond, axis=-1, keepdims=True) + 1e-06)
    lower = jnp.sqrt(jnp.mean(blend * blend, axis=-1, keepdims=True) + 1e-06)
    out_t[...] = latent_t[...] + (stride * (blend * (upper / lower))).T


def finish(where, spans, on, scales, strides, mine, theirs, colsum, latent_t):
    smem = pl.BlockSpec(memory_space=pltpu.SMEM)
    vmem = pl.BlockSpec(memory_space=pltpu.VMEM)
    return pl.pallas_call(
        finish_kernel,
        out_shape=jax.ShapeDtypeStruct(latent_t.shape, jnp.float32),
        in_specs=[smem] * 5 + [vmem] * 4,
        out_specs=vmem,
        name="finish",
    )(where, spans, on, scales, strides, mine, theirs, colsum, latent_t)


def shards(
    queries,
    keys,
    values,
    hidden_in,
    out_weight,
    final_weight,
    gate_mod,
    span_tiles,
    text_len,
    guide_on,
    guide_scale,
    step_size,
    latent,
):
    place = lax.axis_index("seq")
    half = lax.axis_index("guide")
    where = jnp.stack([place, half]).astype(jnp.int32)
    weight_t = lax.all_gather(out_weight.T, "seq", axis=0, tiled=True)

    own = spread(jnp.stack([by_features(keys[0]), by_features(values[0])], axis=1))
    near_l = along_z(own, 1)
    near_r = along_z(own, -1)
    q_sent, _ = lax.optimization_barrier((by_features(queries[0]), own))
    q = spread(q_sent)
    far_l = along_z(near_l[1:], 1)
    far_r = along_z(near_r[:-1], -1)
    attn = spread(attend(where, span_tiles, text_len, q, far_l, near_l, own, near_r, far_r))
    theirs = swapped(attn)
    sums, colsum = project(
        where, span_tiles, attn, theirs, weight_t, hidden_in, gate_mod, final_weight.T
    )
    out_t = finish(
        where, span_tiles, guide_on, guide_scale, step_size, sums, swapped(sums), colsum, latent.T
    )
    return out_t.T


def solution(mesh):
    in_specs = (
        P("guide", ("rep", "seq"), None),
        P("guide", ("rep", "seq"), None),
        P("guide", ("rep", "seq"), None),
        P(None, ("rep", "seq"), "guide"),
        P(None, ("guide", "seq")),
        P(),
        P(None, "rep", None),
        P("rep"),
        P(None, "rep"),
        P("rep"),
        P("rep"),
        P("rep"),
        P(("rep", "seq"), None),
    )
    out_specs = P(("rep", "seq"), None)
    return jax.shard_map(shards, mesh=mesh, in_specs=in_specs, out_specs=out_specs, check_vma=False)
```

time: 359 us -> 133 us (0.37)
  waiting for transfers between devices: 145 us -> 39.8 us
  starting transfers between devices: 107 us -> 27.5 us
  matrix products: 40.2 us -> 0 us
  local copies, waits for them, and re-layouts: 33.5 us -> 11.4 us
  blocking collectives: 4.97 us -> 26.6 us
  Pallas kernels: 0 us -> 13.2 us
  other arithmetic: 12.4 us -> 0.17 us
    psum x1 -> x0, waiting for transfers between devices: 93.7 us -> none  [shards(): speeds = lax.psum(partial_speed, 'guide')]
    ppermute x15 -> x6, starting transfers between devices: 107 us -> 24.1 us  [the longest x4 15.7 us: along_z(): return lax.ppermute(value, 'seq', pairs)]
    dot_general x29 -> x0, matrix products: 40.2 us -> none  [the longest x12 17.5 us: one_head(): jnp.dot(trio[0], trio[1].T, preferred_element_type=jnp.float32)]
    ppermute x15 -> x6, waiting for transfers between devices: 50.9 us -> 21.2 us  [the longest x4 19 us: along_z(): return lax.ppermute(value, 'seq', pairs)]
    all_to_all x0 -> x2, blocking collectives: none -> 26.6 us  [spread(): return lax.all_to_all(value, 'seq', 0, 0, axis_index_groups=groups)]
    pallas_call x0 -> x3, Pallas kernels: none -> 13.2 us  [the longest x1 5.81 us: attend(): pl.pallas_call(attend_kernel, out_shape=jax.ShapeDtypeStruct(q.shape, jnp...]
    all_gather x1, waiting for transfers between devices: 0.02 us -> 11.8 us  [shards(): weight_t = lax.all_gather(out_weight.T, 'seq', axis=0, tiled=True)]
    unnamed x22 -> x24, local copies, waits for them, and re-layouts: 19.6 us -> 8.27 us
  transfers between devices with their start and end apart: 17 -> 8, of which waited for: 7 -> 6; matrix products, arithmetic and copies ran while one was open for 21% -> 5% of each run, Pallas kernels for 0% -> 4%
where the time goes in v1:
time: 133 us; the launch traced here: 132 us
  waiting for transfers between devices  39.8 us (30%)
  starting transfers between devices  27.5 us (21%)
  blocking collectives  26.6 us (20%)
  between operations  13.6 us (10%)
  Pallas kernels  13.2 us (10%)
  local copies, waits for them, and re-layouts  11.4 us (9%)
    all_to_all x2, blocking collectives, spread(): return lax.all_to_all(value, 'seq', 0, 0, axis_index_groups=groups)  26.6 us
    ppermute x4, waiting for transfers between devices, along_z(): return lax.ppermute(value, 'seq', pairs)  19 us
    ppermute x4, starting transfers between devices, along_z(): return lax.ppermute(value, 'seq', pairs)  15.7 us
    all_gather x1, waiting for transfers between devices, shards(): weight_t = lax.all_gather(out_weight.T, 'seq', axis=0, tiled=True)  11.8 us
    ppermute x2, starting transfers between devices, swapped(): return lax.ppermute(value, 'guide', [(0, 1), (1, 0)])  8.37 us
    unnamed x24, local copies, waits for them, and re-layouts  8.27 us
    all_to_all x1, waiting for transfers between devices, spread(): return lax.all_to_all(value, 'seq', 0, 0, axis_index_groups=groups)  6.11 us
    pallas_call x1, Pallas kernels, attend(): pl.pallas_call(attend_kernel, out_shape=jax.ShapeDtypeStruct(q.shape, jnp...  5.81 us
  transfers between devices with their start and end apart: 8, of which 6 were waited for; matrix products, arithmetic and copies ran while one was open for 5% of the time, Pallas kernels for 4%

profile of v1, /device:TPU:1, one launch (start us, length us, event | category | flops | bytes accessed | tf_op | source)
XLA Modules:
  0.0 132.3 jit_solution(13742275860672787096)
XLA Ops:
  6.5 0.7 all-gather.2.cloned.1.call-update
  7.3 1.2 copy.17
  8.5 0.2 copy.18
  8.7 1.2 copy.19
  10.0 0.2 copy.20
  10.2 0.1 pad_maximum_fusion
  10.3 13.0 %all_to_all.15.own = bf16[4,2,128,384]{3,2,1,0:T(8,128)(2,1)S(1)} all-to-all(bf16[4,2,128,384]{3,2,1,0:T(8,128)(2,1)S(1)} %pad_maximum_fusion), channel_id=1, replica_groups={{0,8,16,24},{32,40,48,56},{64,72,80,88},{96,104,112,120},{128,136,144,1..., dimensions={0} | all-to-all | bytes 1572864 | tf_op jit(solution)/shard_map/all_to_all | solution.py:31
  23.3 7.2 %collective-permute-start = (bf16[4,2,128,384]{3,2,1,0:T(8,128)(2,1)S(1)}, bf16[4,2,128,384]{3,2,1,0:T(8,128)(2,1)S(1)}, u32[]{:S(2)}, u32[]{:S(2)}) collective-permute-start(bf16[4,2,128,384]{3,2,1,0:T(8,128)(2,1)S(1)} %all_to_all.15.own), channel_id=1, source_target_pairs={{0,32},{8,40},{16,48},{24,56},{32,64},{40,72},{48,80},{56,88},{64,... | collective-permute-start | bytes 2359304 | tf_op jit(solution)/shard_map/ppermute | solution.py:25
  30.5 1.3 collective-permute-start.2
  31.8 17.6 %collective-permute-done.near_l = bf16[4,2,128,384]{3,2,1,0:T(8,128)(2,1)S(1)} collective-permute-done((bf16[4,2,128,384]{3,2,1,0:T(8,128)(2,1)S(1)}, bf16[4,2,128,384]{3,2,1,0:T(8,128)(2,1)S(1)}, u32[]{:S(2)}, u32[]{:S(2)}) %collective-permute-start) | collective-permute-done | bytes 786464 | tf_op jit(solution)/shard_map/ppermute | solution.py:25
  49.4 0.9 slice.8
  50.3 5.9 %collective-permute-start.1 = (bf16[3,2,128,384]{3,2,1,0:T(8,128)(2,1)}, bf16[3,2,128,384]{3,2,1,0:T(8,128)(2,1)}, u32[]{:S(2)}, u32[]{:S(2)}) collective-permute-start(bf16[3,2,128,384]{3,2,1,0:T(8,128)(2,1)} %slice.8), channel_id=1, source_target_pairs={{0,32},{8,40},{16,48},{24,56},{32,64},{40,72},{48,80},{56,88},{64,... | collective-permute-start | bytes 1769480 | tf_op jit(solution)/shard_map/ppermute | solution.py:25
  56.2 0.9 slice.9
  57.1 1.3 collective-permute-start.3
  58.3 1.2 copy.15
  59.6 0.9 copy.16
  60.5 3.5 %all-to-all-start.1 = ((bf16[4,128,384]{2,1,0:T(8,128)(2,1)}), bf16[4,128,384]{2,1,0:T(8,128)(2,1)S(1)}, u32[]{:S(2)}, u32[]{:S(2)}) async-start(bf16[4,128,384]{2,1,0:T(8,128)(2,1)} %bitcast.17), calls=%async_computation.1 | async-start | bytes 786432 | tf_op jit(solution)/shard_map/all_to_all | solution.py:31
  64.1 6.1 %all-to-all-done.1.q_ref = bf16[4,128,384]{2,1,0:T(8,128)(2,1)S(1)} async-done(((bf16[4,128,384]{2,1,0:T(8,128)(2,1)}), bf16[4,128,384]{2,1,0:T(8,128)(2,1)S(1)}, u32[]{:S(2)}, u32[]{:S(2)}) %all-to-all-start.1) | async-done | bytes 393248 | tf_op jit(solution)/shard_map/all_to_all | solution.py:31
  70.2 1.4 %collective-permute-done.3.far_r = bf16[3,2,128,384]{3,2,1,0:T(8,128)(2,1)} collective-permute-done((bf16[3,2,128,384]{3,2,1,0:T(8,128)(2,1)}, bf16[3,2,128,384]{3,2,1,0:T(8,128)(2,1)}, u32[]{:S(2)}, u32[]{:S(2)}) %collective-permute-start.3) | collective-permute-done | bytes 589856 | tf_op jit(solution)/shard_map/ppermute | solution.py:25
  71.6 5.8 %attend.1 = bf16[4,128,384]{2,1,0:T(8,128)(2,1)S(1)} custom-call(s32[2]{0:T(128)S(1)} %pad_add_fusion.where, s32[5]{0:T(128)S(1)} %copy-done.4, s32[2,5]{1,0:T(2,128)S(1)} %copy-done.7, bf16[4,128,384]{2,1,0:T(8,128)(2,1)S(1)} %all-to-all-done.1.q_ref, bf16[3,2,128,384]{3,2,1,0:T(8,128)(2,1)} %collective-permute-done.1.far_l, ...), custom_call_target="tpu_custom_call" | custom-call | flops 805306368 | bytes 8388608 | tf_op jit(solution)/shard_map/attend/pallas_call | solution.py:93
  77.4 13.6 %all_to_all.16.mine = bf16[4,128,384]{2,1,0:T(8,128)(2,1)S(1)} all-to-all(bf16[4,128,384]{2,1,0:T(8,128)(2,1)S(1)} %attend.1), channel_id=1, replica_groups={{0,8,16,24},{32,40,48,56},{64,72,80,88},{96,104,112,120},{128,136,144,1..., dimensions={0} | all-to-all | bytes 786432 | tf_op jit(solution)/shard_map/all_to_all | solution.py:31
  91.0 5.4 %collective-permute-start.4 = (bf16[4,128,384]{2,1,0:T(8,128)(2,1)S(1)}, bf16[4,128,384]{2,1,0:T(8,128)(2,1)S(1)}, u32[]{:S(2)}, u32[]{:S(2)}) collective-permute-start(bf16[4,128,384]{2,1,0:T(8,128)(2,1)S(1)} %all_to_all.16.mine), channel_id=1, source_target_pairs={{0,256},{256,0},{1,257},{257,1},{2,258},{258,2},{3,259},{259,3},{4... | collective-permute-start | bytes 1179656 | tf_op jit(solution)/shard_map/ppermute | solution.py:18
  96.4 1.3 collective-permute-done.4.theirs
  97.7 11.8 %all-gather.2.cloned.1.call-done.w_ref = bf16[1536,1536]{1,0:T(8,128)(2,1)} async-done(((bf16[48,1536]{1,0:T(8,128)(2,1)}), bf16[1536,1536]{1,0:T(8,128)(2,1)}) %all-gather.2.cloned.1.call-update) | async-done | bytes 4718608 | tf_op jit(solution)/shard_map/all_gather | solution.py:256
  109.5 2.3 %copy-done = bf16[1536,1536]{1,0:T(8,128)(2,1)S(1)} copy-done((bf16[1536,1536]{1,0:T(8,128)(2,1)S(1)}, bf16[1536,1536]{1,0:T(8,128)(2,1)}, u32[]{:S(2)}) %copy-start) | copy-done | bytes 4718616
  111.8 1.0 copy-done.2
  112.8 5.4 %project.1 = (f32[2,128,128]{2,1,0:T(8,128)S(1)}, f32[8,64]{1,0:T(8,128)S(1)}) custom-call(s32[2]{0:T(128)S(1)} %pad_add_fusion.where, s32[5]{0:T(128)S(1)} %copy-done.4, bf16[4,128,384]{2,1,0:T(8,128)(2,1)S(1)} %all_to_all.16.mine, bf16[4,128,384]{2,1,0:T(8,128)(2,1)S(1)} %collective-permute-done.4.theirs, bf16[1536,1536]{1,0:T(8,128)(2,1)S(1)} %copy-done, ...), custom_call_target="tpu_custom_call" | custom-call | flops 1207959552 | bytes 8388608 | tf_op jit(solution)/shard_map/project/pallas_call | solution.py:178
  118.3 0.6 copy-done.6
  118.9 3.0 %collective-permute-start.5 = (f32[2,128,128]{2,1,0:T(8,128)S(1)}, f32[2,128,128]{2,1,0:T(8,128)S(1)}, u32[]{:S(2)}, u32[]{:S(2)}) collective-permute-start(f32[2,128,128]{2,1,0:T(8,128)S(1)} %get-tuple-element.9.mine), channel_id=1, source_target_pairs={{0,256},{256,0},{1,257},{257,1},{2,258},{258,2},{3,259},{259,3},{4... | collective-permute-start | bytes 393224 | tf_op jit(solution)/shard_map/ppermute | solution.py:18
  121.8 1.0 collective-permute-done.5.theirs
  122.8 0.6 copy-done.8
  123.5 2.0 %finish.1 = f32[64,128]{1,0:T(8,128)} custom-call(s32[2]{0:T(128)} %copy-done.5, s32[5]{0:T(128)} %spans.5, s32[5]{0:T(128)} %on.1, f32[5]{0:T(128)} %scales.1, f32[5]{0:T(128)} %strides.1, f32[2,128,128]{2,1,0:T(8,128)} %copy-done.3, f32[2,128,128]{2,1,0:T(8,128)} %copy-done.8, f32[8,64]{1,0:T(8,128)} %copy-done.6, f32[64,128]{1,0:T(8,128)} %bitcast.24), custom_call_target="tpu_custom_call" | custom-call | tf_op jit(solution)/shard_map/finish/pallas_call | solution.py:229
  (21 shorter events, 0.1 us)
Async XLA Ops:
  6.5 103.0 %all-gather.2.cloned.1.call-start = ((), (), s32[]{:S(2)}) async-start(), calls=%async_computation.3 | async-start | bytes 4866048 | tf_op jit(solution)/shard_map/all_gather | solution.py:256
  8.7 62.9 %copy-start.4 = (s32[5]{0:T(128)S(1)}, s32[5]{0:T(128)}, u32[]{:S(2)}) copy-start(s32[5]{0:T(128)} %spans.5) | copy-start | bytes 64
  8.7 62.9 %copy-start.7 = (s32[2,5]{1,0:T(2,128)S(1)}, s32[2,5]{1,0:T(2,128)}, u32[]{:S(2)}) copy-start(s32[2,5]{1,0:T(2,128)} %text_len.1) | copy-start | bytes 124
  23.3 86.2 %copy-start.1 = (bf16[2,128,1536]{2,1,0:T(8,128)(2,1)S(1)}, bf16[2,128,1536]{2,1,0:T(8,128)(2,1)}, u32[]{:S(2)}) copy-start(bf16[2,128,1536]{2,1,0:T(8,128)(2,1)} %hidden.1) | copy-start | bytes 2359300
  23.3 26.1 %collective-permute-start = (bf16[4,2,128,384]{3,2,1,0:T(8,128)(2,1)S(1)}, bf16[4,2,128,384]{3,2,1,0:T(8,128)(2,1)S(1)}, u32[]{:S(2)}, u32[]{:S(2)}) collective-permute-start(bf16[4,2,128,384]{3,2,1,0:T(8,128)(2,1)S(1)} %all_to_all.15.own), channel_id=1, source_target_pairs={{0,32},{8,40},{16,48},{24,56},{32,64},{40,72},{48,80},{56,88},{64,... | collective-permute-start | bytes 2359304 | tf_op jit(solution)/shard_map/ppermute | solution.py:25
  30.5 25.7 %collective-permute-start.2 = (bf16[4,2,128,384]{3,2,1,0:T(8,128)(2,1)S(1)}, bf16[4,2,128,384]{3,2,1,0:T(8,128)(2,1)S(1)}, u32[]{:S(2)}, u32[]{:S(2)}) collective-permute-start(bf16[4,2,128,384]{3,2,1,0:T(8,128)(2,1)S(1)} %all_to_all.15.own), channel_id=1, source_target_pairs={{32,0},{40,8},{48,16},{56,24},{64,32},{72,40},{80,48},{88,56},{96,... | collective-permute-start | bytes 2359304 | tf_op jit(solution)/shard_map/ppermute | solution.py:25
  50.3 19.9 %collective-permute-start.1 = (bf16[3,2,128,384]{3,2,1,0:T(8,128)(2,1)}, bf16[3,2,128,384]{3,2,1,0:T(8,128)(2,1)}, u32[]{:S(2)}, u32[]{:S(2)}) collective-permute-start(bf16[3,2,128,384]{3,2,1,0:T(8,128)(2,1)} %slice.8), channel_id=1, source_target_pairs={{0,32},{8,40},{16,48},{24,56},{32,64},{40,72},{48,80},{56,88},{64,... | collective-permute-start | bytes 1769480 | tf_op jit(solution)/shard_map/ppermute | solution.py:25
  57.1 14.5 %collective-permute-start.3 = (bf16[3,2,128,384]{3,2,1,0:T(8,128)(2,1)}, bf16[3,2,128,384]{3,2,1,0:T(8,128)(2,1)}, u32[]{:S(2)}, u32[]{:S(2)}) collective-permute-start(bf16[3,2,128,384]{3,2,1,0:T(8,128)(2,1)} %slice.9), channel_id=1, source_target_pairs={{32,0},{40,8},{48,16},{56,24},{64,32},{72,40},{80,48},{88,56},{96,... | collective-permute-start | bytes 1769480 | tf_op jit(solution)/shard_map/ppermute | solution.py:25
  60.5 9.7 %all-to-all-start.1 = ((bf16[4,128,384]{2,1,0:T(8,128)(2,1)}), bf16[4,128,384]{2,1,0:T(8,128)(2,1)S(1)}, u32[]{:S(2)}, u32[]{:S(2)}) async-start(bf16[4,128,384]{2,1,0:T(8,128)(2,1)} %bitcast.17), calls=%async_computation.1 | async-start | bytes 786432 | tf_op jit(solution)/shard_map/all_to_all | solution.py:31
  64.1 54.2 %copy-start.5 = (s32[2]{0:T(128)}, s32[2]{0:T(128)S(1)}, u32[]{:S(2)}) copy-start(s32[2]{0:T(128)S(1)} %pad_add_fusion.where) | copy-start | bytes 28
  70.2 26.2 %copy-start.9 = (bf16[2,5,3072]{2,0,1:T(2,128)(2,1)S(1)}, bf16[2,5,3072]{2,0,1:T(2,128)(2,1)}, u32[]{:S(2)}) copy-start(bf16[2,5,3072]{2,0,1:T(2,128)(2,1)} %param.19) | copy-start | bytes 184324
  91.0 6.7 %collective-permute-start.4 = (bf16[4,128,384]{2,1,0:T(8,128)(2,1)S(1)}, bf16[4,128,384]{2,1,0:T(8,128)(2,1)S(1)}, u32[]{:S(2)}, u32[]{:S(2)}) collective-permute-start(bf16[4,128,384]{2,1,0:T(8,128)(2,1)S(1)} %all_to_all.16.mine), channel_id=1, source_target_pairs={{0,256},{256,0},{1,257},{257,1},{2,258},{258,2},{3,259},{259,3},{4... | collective-permute-start | bytes 1179656 | tf_op jit(solution)/shard_map/ppermute | solution.py:18
  109.5 2.3 %copy-start = (bf16[1536,1536]{1,0:T(8,128)(2,1)S(1)}, bf16[1536,1536]{1,0:T(8,128)(2,1)}, u32[]{:S(2)}) copy-start(bf16[1536,1536]{1,0:T(8,128)(2,1)} %all-gather.2.cloned.1.call-done.w_ref) | copy-start | bytes 14155780
  111.8 1.0 copy-start.2
  118.3 0.6 copy-start.6
  118.9 4.0 %copy-start.3 = (f32[2,128,128]{2,1,0:T(8,128)}, f32[2,128,128]{2,1,0:T(8,128)S(1)}, u32[]{:S(2)}) copy-start(f32[2,128,128]{2,1,0:T(8,128)S(1)} %get-tuple-element.9.mine) | copy-start | bytes 393220
  118.9 4.0 %collective-permute-start.5 = (f32[2,128,128]{2,1,0:T(8,128)S(1)}, f32[2,128,128]{2,1,0:T(8,128)S(1)}, u32[]{:S(2)}, u32[]{:S(2)}) collective-permute-start(f32[2,128,128]{2,1,0:T(8,128)S(1)} %get-tuple-element.9.mine), channel_id=1, source_target_pairs={{0,256},{256,0},{1,257},{257,1},{2,258},{258,2},{3,259},{259,3},{4... | collective-permute-start | bytes 393224 | tf_op jit(solution)/shard_map/ppermute | solution.py:18
  122.8 0.6 copy-start.8
Sparse Core Ops, SparseCore 0:
  10.5 98.9 all-gather.1

commit v2 on v1

--- a/solution.py
+++ b/solution.py
@@ -10,6 +10,7 @@
 SPAN_MOST = 8
 FULL_WIDTH = 3072
 ROW = 4
+STEPS = 6
 LOG2E = 1.4426950408889634
 NT = (((1,), (1,)), ((), ()))
 
@@ -31,9 +32,29 @@
     return lax.all_to_all(value, "seq", 0, 0, axis_index_groups=groups)
 
 
-def by_features(value):
-    rows, width = value.shape
-    return value.reshape(rows, ROW, width // ROW).transpose(1, 0, 2)
+def pack_kernel(k_ref, v_ref, q_ref, kv_out, q_out):
+    width = q_out.shape[2]
+    for j in range(ROW):
+        lanes = slice(j * width, (j + 1) * width)
+        kv_out[j, 0] = k_ref[0, :, lanes]
+        kv_out[j, 1] = v_ref[0, :, lanes]
+        q_out[j] = q_ref[0, :, lanes]
+
+
+def pack(keys, values, queries):
+    _, rows, width = keys.shape
+    vmem = pl.BlockSpec(memory_space=pltpu.VMEM)
+    return pl.pallas_call(
+        pack_kernel,
+        out_shape=(
+            jax.ShapeDtypeStruct((ROW, 2, rows, width // ROW), keys.dtype),
+            jax.ShapeDtypeStruct((ROW, rows, width // ROW), queries.dtype),
+        ),
+        in_specs=[vmem] * 3,
+        out_specs=(vmem, vmem),
+        compiler_params=pltpu.CompilerParams(vmem_limit_bytes=8 << 20),
+        name="pack",
+    )(keys, values, queries)
 
 
 def request_of(tile, spans, tables):
@@ -108,93 +129,87 @@
 
 
 def project_kernel(
-    where, spans, mine, theirs, w_ref, hidden, gate, final_t, sums, colsum, state
+    where, spans, mine, theirs, w_ref, hidden, gate, final_t, sums, colsum, weight, state, arrived
 ):
-    step = pl.program_id(0)
     place, half = where[0], where[1]
+    width = weight.shape[0]
+    block = width // STEPS
+    copies = [
+        pltpu.make_async_copy(
+            w_ref.at[pl.ds(c * block, block)], weight.at[pl.ds(c * block, block)], arrived.at[c]
+        )
+        for c in range(STEPS)
+    ]
+    for copy in copies:
+        copy.start()
+
     _, _, request = request_of(place, spans, [])
-    block = w_ref.shape[0]
-    width = state.shape[2]
-    here = pl.multiple_of(half * width + step * block, 128)
-    groups, _, depth = mine.shape
-    for side, source in enumerate((mine, theirs)):
-        which = half if side == 0 else 1 - half
-        total = jnp.zeros((TILE, block), jnp.float32)
-        for j in range(groups):
-            total += lax.dot_general(
-                source[j],
-                w_ref[:, j * depth : (j + 1) * depth],
-                NT,
-                preferred_element_type=jnp.float32,
+    base = pl.multiple_of(half * width, 128)
+    groups = mine.shape[0]
+    attn = jnp.concatenate(
+        [jnp.concatenate([source[j] for j in range(groups)], axis=1) for source in (mine, theirs)],
+        axis=0,
+    )
+    weights = final_t[:, pl.ds(base, width)]
+    others = final_t[:, pl.ds(pl.multiple_of((1 - half) * width, 128), width)]
+    ones = jnp.ones((8, width), jnp.bfloat16)
+    colsum[...] = lax.dot_general(
+        ones, weights, NT, preferred_element_type=jnp.float32
+    ) - lax.dot_general(ones, others, NT, preferred_element_type=jnp.float32)
+    scales = []
+    for which in (half, 1 - half):
+        scale = jnp.zeros((1, width), jnp.float32)
+        for r in range(gate.shape[1]):
+            row = gate[which, r : r + 1, pl.ds(base, width)].astype(jnp.float32)
+            scale = jnp.where(request == r, row, scale)
+        scales.append(scale)
+
+    for c in range(STEPS):
+        copies[c].wait()
+        here = slice(c * block, (c + 1) * block)
+        total = lax.dot_general(attn, weight[here, :], NT, preferred_element_type=jnp.float32)
+        for side, which in enumerate((half, 1 - half)):
+            state[side, :, here] = (
+                hidden[which, :, here].astype(jnp.float32)
+                + scales[side][:, here] * total[side * TILE : (side + 1) * TILE]
             )
-        scale = jnp.zeros((1, block), jnp.float32)
-        for r in range(gate.shape[1]):
-            row = gate[which, r : r + 1, pl.ds(here, block)].astype(jnp.float32)
-            scale = jnp.where(request == r, row, scale)
-        state[which, :, pl.ds(pl.multiple_of(step * block, 128), block)] = (
-            hidden[which].astype(jnp.float32) + scale * total
+
+    channels = weights.shape[0]
+    lane = lax.broadcasted_iota(jnp.int32, (TILE, sums.shape[2] - channels), 1)
+    for side, which in enumerate((half, 1 - half)):
+        rows = state[side]
+        mean = jnp.mean(rows, axis=-1, keepdims=True)
+        centre = rows - mean
+        squares = jnp.sum(centre * centre, axis=-1, keepdims=True)
+        high = centre.astype(jnp.bfloat16)
+        low = (centre - high.astype(jnp.float32)).astype(jnp.bfloat16)
+        speed = lax.dot_general(high, weights, NT, preferred_element_type=jnp.float32)
+        speed += lax.dot_general(low, weights, NT, preferred_element_type=jnp.float32)
+        sums[which, :, :channels] = speed
+        sums[which, :, channels:] = jnp.where(
+            lane == 0, mean, jnp.where(lane == 1, squares, 0.0)
         )
 
-    @pl.when(step == 0)
-    def _():
-        ones = jnp.ones((8, width), jnp.bfloat16)
-        other = pl.multiple_of((1 - half) * width, 128)
-        base = pl.multiple_of(half * width, 128)
-        mine_sum = lax.dot_general(
-            ones, final_t[:, pl.ds(base, width)], NT, preferred_element_type=jnp.float32
-        )
-        other_sum = lax.dot_general(
-            ones, final_t[:, pl.ds(other, width)], NT, preferred_element_type=jnp.float32
-        )
-        colsum[...] = mine_sum - other_sum
-
-    @pl.when(step == pl.num_programs(0) - 1)
-    def _():
-        weights = final_t[:, pl.ds(pl.multiple_of(half * width, 128), width)]
-        channels = weights.shape[0]
-        lane = lax.broadcasted_iota(jnp.int32, (TILE, sums.shape[2] - channels), 1)
-        for which in range(2):
-            rows = state[which]
-            mean = jnp.mean(rows, axis=-1, keepdims=True)
-            centre = rows - mean
-            squares = jnp.sum(centre * centre, axis=-1, keepdims=True)
-            high = centre.astype(jnp.bfloat16)
-            low = (centre - high.astype(jnp.float32)).astype(jnp.bfloat16)
-            speed = lax.dot_general(high, weights, NT, preferred_element_type=jnp.float32)
-            speed += lax.dot_general(low, weights, NT, preferred_element_type=jnp.float32)
-            sums[which, :, :channels] = speed
-            sums[which, :, channels:] = jnp.where(
-                lane == 0, mean, jnp.where(lane == 1, squares, 0.0)
-            )
-
 
 def project(where, spans, mine, theirs, weight_t, hidden, gate, final_t):
-    steps = 4
     depth, width = weight_t.shape[1], weight_t.shape[0]
-    block = width // steps
     channels = final_t.shape[0]
     smem = pl.BlockSpec(memory_space=pltpu.SMEM)
     vmem = pl.BlockSpec(memory_space=pltpu.VMEM)
     return pl.pallas_call(
         project_kernel,
-        grid=(steps,),
         out_shape=(
             jax.ShapeDtypeStruct((2, TILE, 2 * channels), jnp.float32),
             jax.ShapeDtypeStruct((8, channels), jnp.float32),
         ),
-        in_specs=[
-            smem,
-            smem,
-            vmem,
-            vmem,
-            pl.BlockSpec((block, depth), lambda i: (i, 0)),
-            pl.BlockSpec((2, TILE, block), lambda i: (0, 0, i)),
-            vmem,
-            vmem,
+        in_specs=[smem, smem, vmem, vmem, pl.BlockSpec(memory_space=pl.ANY), vmem, vmem, vmem],
+        out_specs=(vmem, vmem),
+        scratch_shapes=[
+            pltpu.VMEM((width, depth), jnp.bfloat16),
+            pltpu.VMEM((2, TILE, width), jnp.float32),
+            pltpu.SemaphoreType.DMA((STEPS,)),
         ],
-        out_specs=(vmem, vmem),
-        scratch_shapes=[pltpu.VMEM((2, TILE, width), jnp.float32)],
-        compiler_params=pltpu.CompilerParams(vmem_limit_bytes=40 << 20),
+        compiler_params=pltpu.CompilerParams(vmem_limit_bytes=56 << 20),
         cost_estimate=pl.CostEstimate(
             flops=4 * TILE * depth * width, bytes_accessed=8 << 20, transcendentals=0
         ),
@@ -231,6 +246,7 @@
         out_shape=jax.ShapeDtypeStruct(latent_t.shape, jnp.float32),
         in_specs=[smem] * 5 + [vmem] * 4,
         out_specs=vmem,
+        compiler_params=pltpu.CompilerParams(vmem_limit_bytes=4 << 20),
         name="finish",
     )(where, spans, on, scales, strides, mine, theirs, colsum, latent_t)
 
@@ -255,10 +271,11 @@
     where = jnp.stack([place, half]).astype(jnp.int32)
     weight_t = lax.all_gather(out_weight.T, "seq", axis=0, tiled=True)
 
-    own = spread(jnp.stack([by_features(keys[0]), by_features(values[0])], axis=1))
+    kv_sent, q_sent = pack(keys, values, queries)
+    own = spread(kv_sent)
     near_l = along_z(own, 1)
     near_r = along_z(own, -1)
-    q_sent, _ = lax.optimization_barrier((by_features(queries[0]), own))
+    q_sent, _ = lax.optimization_barrier((q_sent, own))
     q = spread(q_sent)
     far_l = along_z(near_l[1:], 1)
     far_r = along_z(near_r[:-1], -1)

time: 133 us -> 132 us (level)
  local copies, waits for them, and re-layouts: 11.4 us -> 7.75 us
  Pallas kernels: 13.2 us -> 15 us
    ppermute x4, waiting for transfers between devices: 19 us -> 22.1 us  [along_z(): return lax.ppermute(value, 'seq', pairs)]
    pallas_call x1 -> x2, Pallas kernels: 5.42 us -> 7.84 us  [the longest x1 7.74 us: project(): pl.pallas_call(project_kernel, out_shape=(jax.ShapeDtypeStruct((2, TILE,...]
    unnamed x24 -> x37, local copies, waits for them, and re-layouts: 8.27 us -> 5.96 us
    all_gather x1, waiting for transfers between devices: 11.8 us -> 10 us  [shards(): weight_t = lax.all_gather(out_weight.T, 'seq', axis=0, tiled=True)]
    another operation x3 -> x0, local copies, waits for them, and re-layouts: 1.39 us -> none  [by_features(): return value.reshape(rows, ROW, width // ROW).transpose(1, 0, 2)]
  transfers between devices with their start and end apart: 8 -> 8, of which waited for: 6 -> 6; matrix products, arithmetic and copies ran while one was open for 5% -> 2% of each run, Pallas kernels for 4% -> 4%
where the time goes in v2:
time: 132 us; the launch traced here: 131 us
  waiting for transfers between devices  40.8 us (31%)
  starting transfers between devices  27.5 us (21%)
  blocking collectives  26.7 us (20%)
  Pallas kernels  15 us (11%)
  between operations  13.6 us (10%)
  local copies, waits for them, and re-layouts  7.75 us (6%)
    all_to_all x2, blocking collectives, spread(): return lax.all_to_all(value, 'seq', 0, 0, axis_index_groups=groups)  26.7 us
    ppermute x4, waiting for transfers between devices, along_z(): return lax.ppermute(value, 'seq', pairs)  22.1 us
    ppermute x4, starting transfers between devices, along_z(): return lax.ppermute(value, 'seq', pairs)  14.8 us
    all_gather x1, waiting for transfers between devices, shards(): weight_t = lax.all_gather(out_weight.T, 'seq', axis=0, tiled=True)  10 us
    ppermute x2, starting transfers between devices, swapped(): return lax.ppermute(value, 'guide', [(0, 1), (1, 0)])  9.24 us
    pallas_call x1, Pallas kernels, project(): pl.pallas_call(project_kernel, out_shape=(jax.ShapeDtypeStruct((2, TILE,...  7.74 us
    all_to_all x1, waiting for transfers between devices, spread(): return lax.all_to_all(value, 'seq', 0, 0, axis_index_groups=groups)  6.11 us
    unnamed x37, local copies, waits for them, and re-layouts  5.96 us
  transfers between devices with their start and end apart: 8, of which 6 were waited for; matrix products, arithmetic and copies ran while one was open for 2% of the time, Pallas kernels for 4%

profile of v2, /device:TPU:1, one launch (start us, length us, event | category | flops | bytes accessed | tf_op | source)
XLA Modules:
  0.0 131.4 jit_solution(802490798349840633)
XLA Ops:
  6.5 0.7 all-gather.2.cloned.1.call-update
  7.3 1.0 copy-done.1
  8.3 1.0 copy-done.2
  9.3 1.0 copy-done.3
  10.2 0.1 pack.1
  10.4 0.0 copy-start.17
  10.4 13.1 %all_to_all.15.own = bf16[4,2,128,384]{3,2,1,0:T(8,128)(2,1)S(1)} all-to-all(bf16[4,2,128,384]{3,2,1,0:T(8,128)(2,1)S(1)} %get-tuple-element.11), channel_id=1, replica_groups={{0,8,16,24},{32,40,48,56},{64,72,80,88},{96,104,112,120},{128,136,144,1..., dimensions={0} | all-to-all | bytes 1572864 | tf_op jit(solution)/shard_map/all_to_all | solution.py:32
  23.5 7.1 %collective-permute-start = (bf16[4,2,128,384]{3,2,1,0:T(8,128)(2,1)S(1)}, bf16[4,2,128,384]{3,2,1,0:T(8,128)(2,1)S(1)}, u32[]{:S(2)}, u32[]{:S(2)}) collective-permute-start(bf16[4,2,128,384]{3,2,1,0:T(8,128)(2,1)S(1)} %all_to_all.15.own), channel_id=1, source_target_pairs={{0,32},{8,40},{16,48},{24,56},{32,64},{40,72},{48,80},{56,88},{64,... | collective-permute-start | bytes 2359304 | tf_op jit(solution)/shard_map/ppermute | solution.py:26
  30.6 1.3 collective-permute-start.2
  31.9 17.5 %collective-permute-done.near_l = bf16[4,2,128,384]{3,2,1,0:T(8,128)(2,1)S(1)} collective-permute-done((bf16[4,2,128,384]{3,2,1,0:T(8,128)(2,1)S(1)}, bf16[4,2,128,384]{3,2,1,0:T(8,128)(2,1)S(1)}, u32[]{:S(2)}, u32[]{:S(2)}) %collective-permute-start) | collective-permute-done | bytes 786464 | tf_op jit(solution)/shard_map/ppermute | solution.py:26
  49.4 0.9 slice.8
  50.3 5.1 %collective-permute-start.1 = (bf16[3,2,128,384]{3,2,1,0:T(8,128)(2,1)}, bf16[3,2,128,384]{3,2,1,0:T(8,128)(2,1)S(1)}, u32[]{:S(2)}, u32[]{:S(2)}) collective-permute-start(bf16[3,2,128,384]{3,2,1,0:T(8,128)(2,1)} %slice.8), channel_id=1, source_target_pairs={{0,32},{8,40},{16,48},{24,56},{32,64},{40,72},{48,80},{56,88},{64,... | collective-permute-start | bytes 1769480 | tf_op jit(solution)/shard_map/ppermute | solution.py:26
  55.5 0.9 slice.9
  56.3 1.3 collective-permute-start.3
  57.6 3.5 %all-to-all-start.1 = ((bf16[4,128,384]{2,1,0:T(8,128)(2,1)}), bf16[4,128,384]{2,1,0:T(8,128)(2,1)S(1)}, u32[]{:S(2)}, u32[]{:S(2)}) async-start(bf16[4,128,384]{2,1,0:T(8,128)(2,1)} %copy-done), calls=%async_computation.1 | async-start | bytes 786432 | tf_op jit(solution)/shard_map/all_to_all | solution.py:32
  61.1 0.1 pad_add_fusion.where
  61.2 6.1 %all-to-all-done.1.q_ref = bf16[4,128,384]{2,1,0:T(8,128)(2,1)S(1)} async-done(((bf16[4,128,384]{2,1,0:T(8,128)(2,1)}), bf16[4,128,384]{2,1,0:T(8,128)(2,1)S(1)}, u32[]{:S(2)}, u32[]{:S(2)}) %all-to-all-start.1) | async-done | bytes 393248 | tf_op jit(solution)/shard_map/all_to_all | solution.py:32
  67.3 4.6 %collective-permute-done.3.far_r = bf16[3,2,128,384]{3,2,1,0:T(8,128)(2,1)} collective-permute-done((bf16[3,2,128,384]{3,2,1,0:T(8,128)(2,1)}, bf16[3,2,128,384]{3,2,1,0:T(8,128)(2,1)}, u32[]{:S(2)}, u32[]{:S(2)}) %collective-permute-start.3) | collective-permute-done | bytes 589856 | tf_op jit(solution)/shard_map/ppermute | solution.py:26
  71.9 5.6 %attend.1 = bf16[4,128,384]{2,1,0:T(8,128)(2,1)S(1)} custom-call(s32[2]{0:T(128)S(1)} %pad_add_fusion.where, s32[5]{0:T(128)S(1)} %copy-done.6, s32[2,5]{1,0:T(2,128)S(1)} %copy-done.11, bf16[4,128,384]{2,1,0:T(8,128)(2,1)S(1)} %all-to-all-done.1.q_ref, bf16[3,2,128,384]{3,2,1,0:T(8,128)(2,1)S(1)} %collective-permute-done.1.far_l, ...), custom_call_target="tpu_custom_call" | custom-call | flops 805306368 | bytes 8388608 | tf_op jit(solution)/shard_map/attend/pallas_call | solution.py:114
  77.5 0.0 copy-start.5
  77.6 13.6 %all_to_all.16.mine = bf16[4,128,384]{2,1,0:T(8,128)(2,1)S(1)} all-to-all(bf16[4,128,384]{2,1,0:T(8,128)(2,1)S(1)} %attend.1), channel_id=1, replica_groups={{0,8,16,24},{32,40,48,56},{64,72,80,88},{96,104,112,120},{128,136,144,1..., dimensions={0} | all-to-all | bytes 786432 | tf_op jit(solution)/shard_map/all_to_all | solution.py:32
  91.2 6.5 %collective-permute-start.4 = (bf16[4,128,384]{2,1,0:T(8,128)(2,1)S(1)}, bf16[4,128,384]{2,1,0:T(8,128)(2,1)S(1)}, u32[]{:S(2)}, u32[]{:S(2)}) collective-permute-start(bf16[4,128,384]{2,1,0:T(8,128)(2,1)S(1)} %all_to_all.16.mine), channel_id=1, source_target_pairs={{0,256},{256,0},{1,257},{257,1},{2,258},{258,2},{3,259},{259,3},{4... | collective-permute-start | bytes 1179656 | tf_op jit(solution)/shard_map/ppermute | solution.py:19
  97.7 0.7 copy.14.gate
  98.4 0.6 collective-permute-done.4.theirs
  99.0 10.0 %all-gather.2.cloned.1.call-done.w_ref = bf16[1536,1536]{1,0:T(8,128)(2,1)} async-done(((bf16[48,1536]{1,0:T(8,128)(2,1)}), bf16[1536,1536]{1,0:T(8,128)(2,1)}) %all-gather.2.cloned.1.call-update) | async-done | bytes 4718608 | tf_op jit(solution)/shard_map/all_gather | solution.py:272
  109.0 7.7 %project.1 = (f32[2,128,128]{2,1,0:T(8,128)}, f32[8,64]{1,0:T(8,128)}) custom-call(s32[2]{0:T(128)} %copy-done.8, s32[5]{0:T(128)} %spans.5, bf16[4,128,384]{2,1,0:T(8,128)(2,1)} %copy-done.15, bf16[4,128,384]{2,1,0:T(8,128)(2,1)} %copy-done.16, bf16[1536,1536]{1,0:T(8,128)(2,1)} %all-gather.2.cloned.1.call-done.w_ref, bf16[2,128,1536]{2,1,0:T(8,128)(2,1)} %hidden.1, ...), custom_call_target="tpu_custom_call" | custom-call | flops 1207959552 | bytes 8388608 | tf_op jit(solution)/shard_map/project/pallas_call | solution.py:199
  116.8 2.7 %collective-permute-start.5 = (f32[2,128,128]{2,1,0:T(8,128)}, f32[2,128,128]{2,1,0:T(8,128)S(1)}, u32[]{:S(2)}, u32[]{:S(2)}) collective-permute-start(f32[2,128,128]{2,1,0:T(8,128)} %get-tuple-element.13.mine), channel_id=1, source_target_pairs={{0,256},{256,0},{1,257},{257,1},{2,258},{258,2},{3,259},{259,3},{4... | collective-permute-start | bytes 393224 | tf_op jit(solution)/shard_map/ppermute | solution.py:19
  119.5 1.2 collective-permute-done.5.theirs
  120.7 0.9 copy-done.4
  121.6 0.7 copy-done.9
  122.3 0.7 copy-done.10
  123.0 1.6 %finish.1 = f32[64,128]{1,0:T(8,128)} custom-call(s32[2]{0:T(128)S(1)} %copy-done.9, s32[5]{0:T(128)S(1)} %copy-done.7, s32[5]{0:T(128)S(1)} %copy-done.12, f32[5]{0:T(128)S(1)} %copy-done.13, f32[5]{0:T(128)S(1)} %copy-done.14, f32[2,128,128]{2,1,0:T(8,128)S(1)} %copy-done.4, f32[2,128,128]{2,1,0:T(8,128)S(1)} %collective-permute-done.5.theirs, ...), custom_call_target="tpu_custom_call" | custom-call | tf_op jit(solution)/shard_map/finish/pallas_call | solution.py:244
  (31 shorter events, 0.1 us)
Async XLA Ops:
  6.5 65.3 %copy-start.6 = (s32[5]{0:T(128)S(1)}, s32[5]{0:T(128)}, u32[]{:S(2)}) copy-start(s32[5]{0:T(128)} %spans.5) | copy-start | bytes 64
  6.5 65.3 %copy-start.11 = (s32[2,5]{1,0:T(2,128)S(1)}, s32[2,5]{1,0:T(2,128)}, u32[]{:S(2)}) copy-start(s32[2,5]{1,0:T(2,128)} %text_len.1) | copy-start | bytes 124
  6.5 102.5 %all-gather.2.cloned.1.call-start = ((), (), s32[]{:S(2)}) async-start(), calls=%async_computation.3 | async-start | bytes 4866048 | tf_op jit(solution)/shard_map/all_gather | solution.py:272
  7.3 1.0 copy-start.1
  8.3 1.0 copy-start.2
  9.3 1.0 copy-start.3
  10.4 20.2 %copy-start = (bf16[4,128,384]{2,1,0:T(8,128)(2,1)}, bf16[4,128,384]{2,1,0:T(8,128)(2,1)S(1)}, u32[]{:S(2)}) copy-start(bf16[4,128,384]{2,1,0:T(8,128)(2,1)S(1)} %get-tuple-element.12) | copy-start | bytes 1179652
  10.4 87.3 %copy-start.17 = (bf16[2,5,3072]{2,0,1:T(2,128)(2,1)S(1)}, bf16[2,5,3072]{2,0,1:T(2,128)(2,1)}, u32[]{:S(2)}) copy-start(bf16[2,5,3072]{2,0,1:T(2,128)(2,1)} %param.19) | copy-start | bytes 184324
  23.5 25.9 %collective-permute-start = (bf16[4,2,128,384]{3,2,1,0:T(8,128)(2,1)S(1)}, bf16[4,2,128,384]{3,2,1,0:T(8,128)(2,1)S(1)}, u32[]{:S(2)}, u32[]{:S(2)}) collective-permute-start(bf16[4,2,128,384]{3,2,1,0:T(8,128)(2,1)S(1)} %all_to_all.15.own), channel_id=1, source_target_pairs={{0,32},{8,40},{16,48},{24,56},{32,64},{40,72},{48,80},{56,88},{64,... | collective-permute-start | bytes 2359304 | tf_op jit(solution)/shard_map/ppermute | solution.py:26
  30.6 24.9 %collective-permute-start.2 = (bf16[4,2,128,384]{3,2,1,0:T(8,128)(2,1)S(1)}, bf16[4,2,128,384]{3,2,1,0:T(8,128)(2,1)S(1)}, u32[]{:S(2)}, u32[]{:S(2)}) collective-permute-start(bf16[4,2,128,384]{3,2,1,0:T(8,128)(2,1)S(1)} %all_to_all.15.own), channel_id=1, source_target_pairs={{32,0},{40,8},{48,16},{56,24},{64,32},{72,40},{80,48},{88,56},{96,... | collective-permute-start | bytes 2359304 | tf_op jit(solution)/shard_map/ppermute | solution.py:26
  50.3 17.0 %collective-permute-start.1 = (bf16[3,2,128,384]{3,2,1,0:T(8,128)(2,1)}, bf16[3,2,128,384]{3,2,1,0:T(8,128)(2,1)S(1)}, u32[]{:S(2)}, u32[]{:S(2)}) collective-permute-start(bf16[3,2,128,384]{3,2,1,0:T(8,128)(2,1)} %slice.8), channel_id=1, source_target_pairs={{0,32},{8,40},{16,48},{24,56},{32,64},{40,72},{48,80},{56,88},{64,... | collective-permute-start | bytes 1769480 | tf_op jit(solution)/shard_map/ppermute | solution.py:26
  56.3 15.5 %collective-permute-start.3 = (bf16[3,2,128,384]{3,2,1,0:T(8,128)(2,1)}, bf16[3,2,128,384]{3,2,1,0:T(8,128)(2,1)}, u32[]{:S(2)}, u32[]{:S(2)}) collective-permute-start(bf16[3,2,128,384]{3,2,1,0:T(8,128)(2,1)} %slice.9), channel_id=1, source_target_pairs={{32,0},{40,8},{48,16},{56,24},{64,32},{72,40},{80,48},{88,56},{96,... | collective-permute-start | bytes 1769480 | tf_op jit(solution)/shard_map/ppermute | solution.py:26
  57.6 9.7 %all-to-all-start.1 = ((bf16[4,128,384]{2,1,0:T(8,128)(2,1)}), bf16[4,128,384]{2,1,0:T(8,128)(2,1)S(1)}, u32[]{:S(2)}, u32[]{:S(2)}) async-start(bf16[4,128,384]{2,1,0:T(8,128)(2,1)} %copy-done), calls=%async_computation.1 | async-start | bytes 786432 | tf_op jit(solution)/shard_map/all_to_all | solution.py:32
  61.2 47.8 %copy-start.8 = (s32[2]{0:T(128)}, s32[2]{0:T(128)S(1)}, u32[]{:S(2)}) copy-start(s32[2]{0:T(128)S(1)} %pad_add_fusion.where) | copy-start | bytes 28
  77.5 43.2 %copy-start.5 = (f32[128,64]{0,1:T(8,128)S(1)}, f32[128,64]{0,1:T(8,128)}, u32[]{:S(2)}) copy-start(f32[128,64]{0,1:T(8,128)} %param.25) | copy-start | bytes 98308
  77.5 43.2 %copy-start.7 = (s32[5]{0:T(128)S(1)}, s32[5]{0:T(128)}, u32[]{:S(2)}) copy-start(s32[5]{0:T(128)} %spans.5) | copy-start | bytes 64
  77.5 43.2 %copy-start.12 = (s32[5]{0:T(128)S(1)}, s32[5]{0:T(128)}, u32[]{:S(2)}) copy-start(s32[5]{0:T(128)} %on.1) | copy-start | bytes 64
  77.5 43.2 %copy-start.13 = (f32[5]{0:T(128)S(1)}, f32[5]{0:T(128)}, u32[]{:S(2)}) copy-start(f32[5]{0:T(128)} %scales.1) | copy-start | bytes 64
  77.6 43.2 %copy-start.14 = (f32[5]{0:T(128)S(1)}, f32[5]{0:T(128)}, u32[]{:S(2)}) copy-start(f32[5]{0:T(128)} %strides.1) | copy-start | bytes 64
  91.2 17.9 %copy-start.15 = (bf16[4,128,384]{2,1,0:T(8,128)(2,1)}, bf16[4,128,384]{2,1,0:T(8,128)(2,1)S(1)}, u32[]{:S(2)}) copy-start(bf16[4,128,384]{2,1,0:T(8,128)(2,1)S(1)} %all_to_all.16.mine) | copy-start | bytes 1179652
  91.2 7.8 %collective-permute-start.4 = (bf16[4,128,384]{2,1,0:T(8,128)(2,1)S(1)}, bf16[4,128,384]{2,1,0:T(8,128)(2,1)S(1)}, u32[]{:S(2)}, u32[]{:S(2)}) collective-permute-start(bf16[4,128,384]{2,1,0:T(8,128)(2,1)S(1)} %all_to_all.16.mine), channel_id=1, source_target_pairs={{0,256},{256,0},{1,257},{257,1},{2,258},{258,2},{3,259},{259,3},{4... | collective-permute-start | bytes 1179656 | tf_op jit(solution)/shard_map/ppermute | solution.py:19
  99.0 10.0 %copy-start.16 = (bf16[4,128,384]{2,1,0:T(8,128)(2,1)}, bf16[4,128,384]{2,1,0:T(8,128)(2,1)S(1)}, u32[]{:S(2)}) copy-start(bf16[4,128,384]{2,1,0:T(8,128)(2,1)S(1)} %collective-permute-done.4.theirs) | copy-start | bytes 1179652
  116.8 3.9 %collective-permute-start.5 = (f32[2,128,128]{2,1,0:T(8,128)}, f32[2,128,128]{2,1,0:T(8,128)S(1)}, u32[]{:S(2)}, u32[]{:S(2)}) collective-permute-start(f32[2,128,128]{2,1,0:T(8,128)} %get-tuple-element.13.mine), channel_id=1, source_target_pairs={{0,256},{256,0},{1,257},{257,1},{2,258},{258,2},{3,259},{259,3},{4... | collective-permute-start | bytes 393224 | tf_op jit(solution)/shard_map/ppermute | solution.py:19
  120.7 0.9 copy-start.4
  121.6 0.7 copy-start.9
  122.3 0.7 copy-start.10
Sparse Core Ops, SparseCore 0:
  10.5 98.4 all-gather.1

commit v3 on v2

--- a/solution.py
+++ b/solution.py
@@ -10,7 +10,7 @@
 SPAN_MOST = 8
 FULL_WIDTH = 3072
 ROW = 4
-STEPS = 6
+STEPS = 3
 LOG2E = 1.4426950408889634
 NT = (((1,), (1,)), ((), ()))
 
@@ -128,10 +128,60 @@
     )(where, spans, text_len, q, far_l, near_l, own, near_r, far_r)
 
 
-def project_kernel(
-    where, spans, mine, theirs, w_ref, hidden, gate, final_t, sums, colsum, weight, state, arrived
+def prepare_kernel(
+    where, spans, on, scales, strides, hidden, gate, final_t, latent_t, h_out, g_out, f_out, aux
 ):
     place, half = where[0], where[1]
+    _, _, request, switch, factor, stride = request_of(
+        place, spans, [lambda r: on[r], lambda r: scales[r], lambda r: strides[r]]
+    )
+    channels, width = f_out.shape
+    base = pl.multiple_of(half * width, 128)
+    for side, which in enumerate((half, 1 - half)):
+        lanes = slice(side * TILE, (side + 1) * TILE)
+        row = jnp.zeros((1, width), jnp.float32)
+        for r in range(gate.shape[1]):
+            new = gate[which, r : r + 1, pl.ds(base, width)].astype(jnp.float32)
+            row = jnp.where(request == r, new, row)
+        g_out[:, lanes] = jnp.broadcast_to(row, (TILE, width)).T.astype(jnp.bfloat16)
+        h_out[:, lanes] = hidden[which].astype(jnp.float32).T.astype(jnp.bfloat16)
+    weights = final_t[:, pl.ds(base, width)]
+    others = final_t[:, pl.ds(pl.multiple_of((1 - half) * width, 128), width)]
+    f_out[...] = weights
+    ones = jnp.ones((width, TILE), jnp.bfloat16)
+    aux[:channels] = latent_t[...]
+    aux[channels : 2 * channels] = jnp.dot(
+        weights, ones, preferred_element_type=jnp.float32
+    ) - jnp.dot(others, ones, preferred_element_type=jnp.float32)
+    line = lax.broadcasted_iota(jnp.int32, (8, TILE), 0)
+    scalars = jnp.where(line == 1, factor, jnp.where(line == 2, stride, 0.0))
+    aux[2 * channels :] = jnp.where(line == 0, switch.astype(jnp.float32), scalars)
+
+
+def prepare(where, spans, on, scales, strides, hidden, gate, final_t, latent_t):
+    width, channels = hidden.shape[2], final_t.shape[0]
+    smem = pl.BlockSpec(memory_space=pltpu.SMEM)
+    vmem = pl.BlockSpec(memory_space=pltpu.VMEM)
+    turned = jax.ShapeDtypeStruct((width, 2 * TILE), jnp.bfloat16)
+    return pl.pallas_call(
+        prepare_kernel,
+        out_shape=(
+            turned,
+            turned,
+            jax.ShapeDtypeStruct((channels, width), jnp.bfloat16),
+            jax.ShapeDtypeStruct((2 * channels + 8, TILE), jnp.float32),
+        ),
+        in_specs=[smem] * 5 + [vmem] * 4,
+        out_specs=(vmem,) * 4,
+        compiler_params=pltpu.CompilerParams(vmem_limit_bytes=20 << 20),
+        name="prepare",
+    )(where, spans, on, scales, strides, hidden, gate, final_t, latent_t)
+
+
+def project_kernel(
+    where, mine, theirs, w_ref, hidden, gate, final, sums, weight, attn, state, arrived
+):
+    half = where[1]
     width = weight.shape[0]
     block = width // STEPS
     copies = [
@@ -142,113 +192,90 @@
     ]
     for copy in copies:
         copy.start()
-
-    _, _, request = request_of(place, spans, [])
-    base = pl.multiple_of(half * width, 128)
-    groups = mine.shape[0]
-    attn = jnp.concatenate(
-        [jnp.concatenate([source[j] for j in range(groups)], axis=1) for source in (mine, theirs)],
-        axis=0,
-    )
-    weights = final_t[:, pl.ds(base, width)]
-    others = final_t[:, pl.ds(pl.multiple_of((1 - half) * width, 128), width)]
-    ones = jnp.ones((8, width), jnp.bfloat16)
-    colsum[...] = lax.dot_general(
-        ones, weights, NT, preferred_element_type=jnp.float32
-    ) - lax.dot_general(ones, others, NT, preferred_element_type=jnp.float32)
-    scales = []
-    for which in (half, 1 - half):
-        scale = jnp.zeros((1, width), jnp.float32)
-        for r in range(gate.shape[1]):
-            row = gate[which, r : r + 1, pl.ds(base, width)].astype(jnp.float32)
-            scale = jnp.where(request == r, row, scale)
-        scales.append(scale)
-
+    groups, _, depth = mine.shape
+    for side, source in enumerate((mine, theirs)):
+        for j in range(groups):
+            attn[j * depth : (j + 1) * depth, side * TILE : (side + 1) * TILE] = source[j].T
+
+    added = jnp.zeros((1, 2 * TILE), jnp.float32)
     for c in range(STEPS):
         copies[c].wait()
         here = slice(c * block, (c + 1) * block)
-        total = lax.dot_general(attn, weight[here, :], NT, preferred_element_type=jnp.float32)
-        for side, which in enumerate((half, 1 - half)):
-            state[side, :, here] = (
-                hidden[which, :, here].astype(jnp.float32)
-                + scales[side][:, here] * total[side * TILE : (side + 1) * TILE]
-            )
-
-    channels = weights.shape[0]
-    lane = lax.broadcasted_iota(jnp.int32, (TILE, sums.shape[2] - channels), 1)
-    for side, which in enumerate((half, 1 - half)):
-        rows = state[side]
-        mean = jnp.mean(rows, axis=-1, keepdims=True)
-        centre = rows - mean
-        squares = jnp.sum(centre * centre, axis=-1, keepdims=True)
+        total = jnp.dot(weight[here, :], attn[...], preferred_element_type=jnp.float32)
+        new = hidden[here, :].astype(jnp.float32) + gate[here, :].astype(jnp.float32) * total
+        state[here, :] = new
+        added += jnp.sum(new, axis=0, keepdims=True)
+    mean = added / width
+    channels = final.shape[0]
+    squares = jnp.zeros((1, 2 * TILE), jnp.float32)
+    speed = jnp.zeros((channels, 2 * TILE), jnp.float32)
+    for c in range(STEPS):
+        here = slice(c * block, (c + 1) * block)
+        centre = state[here, :] - mean
+        squares += jnp.sum(centre * centre, axis=0, keepdims=True)
         high = centre.astype(jnp.bfloat16)
         low = (centre - high.astype(jnp.float32)).astype(jnp.bfloat16)
-        speed = lax.dot_general(high, weights, NT, preferred_element_type=jnp.float32)
-        speed += lax.dot_general(low, weights, NT, preferred_element_type=jnp.float32)
-        sums[which, :, :channels] = speed
-        sums[which, :, channels:] = jnp.where(
-            lane == 0, mean, jnp.where(lane == 1, squares, 0.0)
-        )
-
-
-def project(where, spans, mine, theirs, weight_t, hidden, gate, final_t):
-    depth, width = weight_t.shape[1], weight_t.shape[0]
-    channels = final_t.shape[0]
+        speed += jnp.dot(final[:, here], high, preferred_element_type=jnp.float32)
+        speed += jnp.dot(final[:, here], low, preferred_element_type=jnp.float32)
+    line = lax.broadcasted_iota(jnp.int32, (8, 2 * TILE), 0)
+    extra = jnp.where(line == 0, mean, jnp.where(line == 1, squares, 0.0))
+    for side, which in enumerate((half, 1 - half)):
+        lanes = slice(side * TILE, (side + 1) * TILE)
+        sums[which, :channels] = speed[:, lanes]
+        sums[which, channels:] = extra[:, lanes]
+
+
+def project(where, mine, theirs, weight_t, hidden, gate, final):
+    width, depth = weight_t.shape
     smem = pl.BlockSpec(memory_space=pltpu.SMEM)
     vmem = pl.BlockSpec(memory_space=pltpu.VMEM)
     return pl.pallas_call(
         project_kernel,
-        out_shape=(
-            jax.ShapeDtypeStruct((2, TILE, 2 * channels), jnp.float32),
-            jax.ShapeDtypeStruct((8, channels), jnp.float32),
-        ),
-        in_specs=[smem, smem, vmem, vmem, pl.BlockSpec(memory_space=pl.ANY), vmem, vmem, vmem],
-        out_specs=(vmem, vmem),
+        out_shape=jax.ShapeDtypeStruct((2, final.shape[0] + 8, TILE), jnp.float32),
+        in_specs=[smem, vmem, vmem, pl.BlockSpec(memory_space=pl.ANY), vmem, vmem, vmem],
+        out_specs=vmem,
         scratch_shapes=[
             pltpu.VMEM((width, depth), jnp.bfloat16),
-            pltpu.VMEM((2, TILE, width), jnp.float32),
+            pltpu.VMEM((depth, 2 * TILE), jnp.bfloat16),
+            pltpu.VMEM((width, 2 * TILE), jnp.float32),
             pltpu.SemaphoreType.DMA((STEPS,)),
         ],
-        compiler_params=pltpu.CompilerParams(vmem_limit_bytes=56 << 20),
+        compiler_params=pltpu.CompilerParams(vmem_limit_bytes=52 << 20),
         cost_estimate=pl.CostEstimate(
             flops=4 * TILE * depth * width, bytes_accessed=8 << 20, transcendentals=0
         ),
         name="project",
-    )(where, spans, mine, theirs, weight_t, hidden, gate, final_t)
-
-
-def finish_kernel(where, spans, on, scales, strides, mine, theirs, colsum, latent_t, out_t):
-    _, _, _, switch, factor, stride = request_of(
-        where[0], spans, [lambda r: on[r], lambda r: scales[r], lambda r: strides[r]]
-    )
-    channels = latent_t.shape[0]
-    full = FULL_WIDTH
+    )(where, mine, theirs, weight_t, hidden, gate, final)
+
+
+def finish_kernel(a_ref, b_ref, aux, out_t):
+    channels = out_t.shape[0]
+    switch, factor, stride = (aux[2 * channels + i : 2 * channels + i + 1, :] for i in range(3))
     speeds = []
     for which in range(2):
-        a, b = mine[which], theirs[which]
-        gap = a[:, channels : channels + 1] - b[:, channels : channels + 1]
-        squares = a[:, channels + 1 : channels + 2] + b[:, channels + 1 : channels + 2]
-        spread_of = squares + gap * gap * (full / 4)
-        raw = a[:, :channels] + b[:, :channels] + (0.5 * gap) * colsum[0:1, :]
-        speeds.append(raw * lax.rsqrt(spread_of / full + 1e-06))
+        a, b = a_ref[which], b_ref[which]
+        gap = a[channels : channels + 1] - b[channels : channels + 1]
+        squares = a[channels + 1 : channels + 2] + b[channels + 1 : channels + 2]
+        squares = squares + gap * gap * (FULL_WIDTH / 4)
+        raw = a[:channels] + b[:channels] + (0.5 * gap) * aux[channels : 2 * channels, :]
+        speeds.append(raw * lax.rsqrt(squares / FULL_WIDTH + 1e-06))
     cond, uncond = speeds
     blend = jnp.where(switch > 0, uncond + factor * (cond - uncond), cond)
-    upper = jnp.sqrt(jnp.mean(cond * cond, axis=-1, keepdims=True) + 1e-06)
-    lower = jnp.sqrt(jnp.mean(blend * blend, axis=-1, keepdims=True) + 1e-06)
-    out_t[...] = latent_t[...] + (stride * (blend * (upper / lower))).T
-
-
-def finish(where, spans, on, scales, strides, mine, theirs, colsum, latent_t):
-    smem = pl.BlockSpec(memory_space=pltpu.SMEM)
+    upper = jnp.sqrt(jnp.mean(cond * cond, axis=0, keepdims=True) + 1e-06)
+    lower = jnp.sqrt(jnp.mean(blend * blend, axis=0, keepdims=True) + 1e-06)
+    out_t[...] = aux[:channels, :] + stride * (blend * (upper / lower))
+
+
+def finish(mine, theirs, aux, channels):
     vmem = pl.BlockSpec(memory_space=pltpu.VMEM)
     return pl.pallas_call(
         finish_kernel,
-        out_shape=jax.ShapeDtypeStruct(latent_t.shape, jnp.float32),
-        in_specs=[smem] * 5 + [vmem] * 4,
+        out_shape=jax.ShapeDtypeStruct((channels, TILE), jnp.float32),
+        in_specs=[vmem] * 3,
         out_specs=vmem,
         compiler_params=pltpu.CompilerParams(vmem_limit_bytes=4 << 20),
         name="finish",
-    )(where, spans, on, scales, strides, mine, theirs, colsum, latent_t)
+    )(mine, theirs, aux)
 
 
 def shards(
@@ -275,19 +302,25 @@
     own = spread(kv_sent)
     near_l = along_z(own, 1)
     near_r = along_z(own, -1)
-    q_sent, _ = lax.optimization_barrier((q_sent, own))
+    q_sent, hidden_in, _ = lax.optimization_barrier((q_sent, hidden_in, own))
     q = spread(q_sent)
     far_l = along_z(near_l[1:], 1)
     far_r = along_z(near_r[:-1], -1)
+    turned = prepare(
+        where,
+        span_tiles,
+        guide_on,
+        guide_scale,
+        step_size,
+        hidden_in,
+        gate_mod,
+        final_weight.T,
+        latent.T,
+    )
+    q, (hidden, gate, final, aux) = lax.optimization_barrier((q, turned))
     attn = spread(attend(where, span_tiles, text_len, q, far_l, near_l, own, near_r, far_r))
-    theirs = swapped(attn)
-    sums, colsum = project(
-        where, span_tiles, attn, theirs, weight_t, hidden_in, gate_mod, final_weight.T
-    )
-    out_t = finish(
-        where, span_tiles, guide_on, guide_scale, step_size, sums, swapped(sums), colsum, latent.T
-    )
-    return out_t.T
+    sums = project(where, attn, swapped(attn), weight_t, hidden, gate, final)
+    return finish(sums, swapped(sums), aux, latent.shape[1]).T
 
 
 def solution(mesh):

time: 132 us -> 128 us (0.970)
  waiting for transfers between devices: 40.8 us -> 32.9 us
  local copies, waits for them, and re-layouts: 7.75 us -> 12.1 us
    all_to_all x1, waiting for transfers between devices: 6.11 us -> 0.01 us  [spread(): return lax.all_to_all(value, 'seq', 0, 0, axis_index_groups=groups)]
    unnamed x37 -> x35, local copies, waits for them, and re-layouts: 5.96 us -> 10.4 us
    ppermute x4, waiting for transfers between devices: 22.1 us -> 19.5 us  [along_z(): return lax.ppermute(value, 'seq', pairs)]
    pallas_call x2 -> x3, Pallas kernels: 9.3 us -> 7.77 us  [the longest x1 5.95 us: project(): pl.pallas_call(project_kernel, out_shape=jax.ShapeDtypeStruct((2, final.s...]
  transfers between devices with their start and end apart: 8 -> 8, of which waited for: 6 -> 5; matrix products, arithmetic and copies ran while one was open for 2% -> 1% of each run, Pallas kernels for 4% -> 6%
where the time goes in v3:
time: 128 us; the launch traced here: 127 us
  waiting for transfers between devices  32.9 us (26%)
  starting transfers between devices  27.4 us (21%)
  blocking collectives  26.5 us (21%)
  Pallas kernels  14.6 us (11%)
  between operations  13.5 us (11%)
  local copies, waits for them, and re-layouts  12.1 us (9%)
    all_to_all x2, blocking collectives, spread(): return lax.all_to_all(value, 'seq', 0, 0, axis_index_groups=groups)  26.5 us
    ppermute x4, waiting for transfers between devices, along_z(): return lax.ppermute(value, 'seq', pairs)  19.5 us
    ppermute x4, starting transfers between devices, along_z(): return lax.ppermute(value, 'seq', pairs)  15.3 us
    all_gather x1, waiting for transfers between devices, shards(): weight_t = lax.all_gather(out_weight.T, 'seq', axis=0, tiled=True)  10.5 us
    unnamed x35, local copies, waits for them, and re-layouts  10.4 us
    ppermute x2, starting transfers between devices, swapped(): return lax.ppermute(value, 'guide', [(0, 1), (1, 0)])  8.56 us
    pallas_call x1, Pallas kernels, project(): pl.pallas_call(project_kernel, out_shape=jax.ShapeDtypeStruct((2, final.s...  5.95 us
    pallas_call x1, Pallas kernels, attend(): pl.pallas_call(attend_kernel, out_shape=jax.ShapeDtypeStruct(q.shape, jnp...  5.91 us
  transfers between devices with their start and end apart: 8, of which 5 were waited for; matrix products, arithmetic and copies ran while one was open for 1% of the time, Pallas kernels for 6%

profile of v3, /device:TPU:1, one launch (start us, length us, event | category | flops | bytes accessed | tf_op | source)
XLA Modules:
  0.0 127.1 jit_solution(13882705833067095436)
XLA Ops:
  6.6 0.7 all-gather.2.cloned.1.call-update
  7.3 1.0 copy-done.2
  8.3 1.0 copy-done.3
  9.3 1.0 copy-done.4
  10.3 0.9 pack.1
  11.1 13.0 %all_to_all.15.own = bf16[4,2,128,384]{3,2,1,0:T(8,128)(2,1)S(1)} all-to-all(bf16[4,2,128,384]{3,2,1,0:T(8,128)(2,1)S(1)} %get-tuple-element.19), channel_id=1, replica_groups={{0,8,16,24},{32,40,48,56},{64,72,80,88},{96,104,112,120},{128,136,144,1..., dimensions={0} | all-to-all | bytes 1572864 | tf_op jit(solution)/shard_map/all_to_all | solution.py:32
  24.1 7.1 %collective-permute-start = (bf16[4,2,128,384]{3,2,1,0:T(8,128)(2,1)S(1)}, bf16[4,2,128,384]{3,2,1,0:T(8,128)(2,1)S(1)}, u32[]{:S(2)}, u32[]{:S(2)}) collective-permute-start(bf16[4,2,128,384]{3,2,1,0:T(8,128)(2,1)S(1)} %all_to_all.15.own), channel_id=1, source_target_pairs={{0,32},{8,40},{16,48},{24,56},{32,64},{40,72},{48,80},{56,88},{64,... | collective-permute-start | bytes 2359304 | tf_op jit(solution)/shard_map/ppermute | solution.py:26
  31.2 1.3 %collective-permute-start.2 = (bf16[4,2,128,384]{3,2,1,0:T(8,128)(2,1)S(1)}, bf16[4,2,128,384]{3,2,1,0:T(8,128)(2,1)S(1)}, u32[]{:S(2)}, u32[]{:S(2)}) collective-permute-start(bf16[4,2,128,384]{3,2,1,0:T(8,128)(2,1)S(1)} %all_to_all.15.own), channel_id=1, source_target_pairs={{32,0},{40,8},{48,16},{56,24},{64,32},{72,40},{80,48},{88,56},{96,... | collective-permute-start | bytes 2359304 | tf_op jit(solution)/shard_map/ppermute | solution.py:26
  32.5 17.9 %collective-permute-done.near_l = bf16[4,2,128,384]{3,2,1,0:T(8,128)(2,1)S(1)} collective-permute-done((bf16[4,2,128,384]{3,2,1,0:T(8,128)(2,1)S(1)}, bf16[4,2,128,384]{3,2,1,0:T(8,128)(2,1)S(1)}, u32[]{:S(2)}, u32[]{:S(2)}) %collective-permute-start) | collective-permute-done | bytes 786464 | tf_op jit(solution)/shard_map/ppermute | solution.py:26
  50.4 0.9 slice.8
  51.2 5.7 %collective-permute-start.1 = (bf16[3,2,128,384]{3,2,1,0:T(8,128)(2,1)}, bf16[3,2,128,384]{3,2,1,0:T(8,128)(2,1)}, u32[]{:S(2)}, u32[]{:S(2)}) collective-permute-start(bf16[3,2,128,384]{3,2,1,0:T(8,128)(2,1)} %slice.8), channel_id=1, source_target_pairs={{0,32},{8,40},{16,48},{24,56},{32,64},{40,72},{48,80},{56,88},{64,... | collective-permute-start | bytes 1769480 | tf_op jit(solution)/shard_map/ppermute | solution.py:26
  56.9 0.9 slice.9
  57.8 1.3 %collective-permute-start.3 = (bf16[3,2,128,384]{3,2,1,0:T(8,128)(2,1)}, bf16[3,2,128,384]{3,2,1,0:T(8,128)(2,1)}, u32[]{:S(2)}, u32[]{:S(2)}) collective-permute-start(bf16[3,2,128,384]{3,2,1,0:T(8,128)(2,1)} %slice.9), channel_id=1, source_target_pairs={{32,0},{40,8},{48,16},{56,24},{64,32},{72,40},{80,48},{88,56},{96,... | collective-permute-start | bytes 1769480 | tf_op jit(solution)/shard_map/ppermute | solution.py:26
  59.1 3.5 %all-to-all-start.1 = ((bf16[4,128,384]{2,1,0:T(8,128)(2,1)}), bf16[4,128,384]{2,1,0:T(8,128)(2,1)S(1)}, u32[]{:S(2)}, u32[]{:S(2)}) async-start(bf16[4,128,384]{2,1,0:T(8,128)(2,1)} %get-tuple-element.20), calls=%async_computation.1 | async-start | bytes 786432 | tf_op jit(solution)/shard_map/all_to_all | solution.py:32
  62.7 1.1 copy-done.1
  63.9 1.0 copy-done.5
  64.9 0.8 copy-done.10
  65.6 0.7 copy-done.14
  66.9 1.1 prepare.1
  68.1 0.9 copy-done
  69.0 0.7 copy-done.6
  70.3 1.7 %collective-permute-done.3.far_r = bf16[3,2,128,384]{3,2,1,0:T(8,128)(2,1)} collective-permute-done((bf16[3,2,128,384]{3,2,1,0:T(8,128)(2,1)}, bf16[3,2,128,384]{3,2,1,0:T(8,128)(2,1)}, u32[]{:S(2)}, u32[]{:S(2)}) %collective-permute-start.3) | collective-permute-done | bytes 589856 | tf_op jit(solution)/shard_map/ppermute | solution.py:26
  72.0 5.9 %attend.1 = bf16[4,128,384]{2,1,0:T(8,128)(2,1)S(1)} custom-call(s32[2]{0:T(128)S(1)} %pad_add_fusion.where, s32[5]{0:T(128)S(1)} %copy-done.11, s32[2,5]{1,0:T(2,128)S(1)} %copy-done.12, bf16[4,128,384]{2,1,0:T(8,128)(2,1)S(1)} %all-to-all-done.1.q_ref, bf16[3,2,128,384]{3,2,1,0:T(8,128)(2,1)} %collective-permute-done.1.far_l, ...), custom_call_target="tpu_custom_call" | custom-call | flops 805306368 | bytes 8388608 | tf_op jit(solution)/shard_map/attend/pallas_call | solution.py:114
  77.9 13.5 %all_to_all.16.mine = bf16[4,128,384]{2,1,0:T(8,128)(2,1)S(1)} all-to-all(bf16[4,128,384]{2,1,0:T(8,128)(2,1)S(1)} %attend.1), channel_id=1, replica_groups={{0,8,16,24},{32,40,48,56},{64,72,80,88},{96,104,112,120},{128,136,144,1..., dimensions={0} | all-to-all | bytes 786432 | tf_op jit(solution)/shard_map/all_to_all | solution.py:32
  91.4 5.8 %collective-permute-start.4 = (bf16[4,128,384]{2,1,0:T(8,128)(2,1)S(1)}, bf16[4,128,384]{2,1,0:T(8,128)(2,1)S(1)}, u32[]{:S(2)}, u32[]{:S(2)}) collective-permute-start(bf16[4,128,384]{2,1,0:T(8,128)(2,1)S(1)} %all_to_all.16.mine), channel_id=1, source_target_pairs={{0,256},{256,0},{1,257},{257,1},{2,258},{258,2},{3,259},{259,3},{4... | collective-permute-start | bytes 1179656 | tf_op jit(solution)/shard_map/ppermute | solution.py:19
  97.2 1.3 %collective-permute-done.4.theirs = bf16[4,128,384]{2,1,0:T(8,128)(2,1)S(1)} collective-permute-done((bf16[4,128,384]{2,1,0:T(8,128)(2,1)S(1)}, bf16[4,128,384]{2,1,0:T(8,128)(2,1)S(1)}, u32[]{:S(2)}, u32[]{:S(2)}) %collective-permute-start.4) | collective-permute-done | bytes 393248 | tf_op jit(solution)/shard_map/ppermute | solution.py:19
  98.5 10.5 %all-gather.2.cloned.1.call-done.w_ref = bf16[1536,1536]{1,0:T(8,128)(2,1)} async-done(((bf16[48,1536]{1,0:T(8,128)(2,1)}), bf16[1536,1536]{1,0:T(8,128)(2,1)}) %all-gather.2.cloned.1.call-update) | async-done | bytes 4718608 | tf_op jit(solution)/shard_map/all_gather | solution.py:299
  109.0 0.9 copy-done.7
  109.9 6.0 %project.1.a_ref = f32[2,72,128]{2,1,0:T(8,128)S(1)} custom-call(s32[2]{0:T(128)S(1)} %pad_add_fusion.where, bf16[4,128,384]{2,1,0:T(8,128)(2,1)S(1)} %all_to_all.16.mine, bf16[4,128,384]{2,1,0:T(8,128)(2,1)S(1)} %collective-permute-done.4.theirs, bf16[1536,1536]{1,0:T(8,128)(2,1)} %all-gather.2.cloned.1.call-done.w_ref, ...), custom_call_target="tpu_custom_call" | custom-call | flops 1207959552 | bytes 8388608 | tf_op jit(solution)/shard_map/project/pallas_call | solution.py:232
  115.9 2.8 %collective-permute-start.5 = (f32[2,72,128]{2,1,0:T(8,128)S(1)}, f32[2,72,128]{2,1,0:T(8,128)S(1)}, u32[]{:S(2)}, u32[]{:S(2)}) collective-permute-start(f32[2,72,128]{2,1,0:T(8,128)S(1)} %project.1.a_ref), channel_id=1, source_target_pairs={{0,256},{256,0},{1,257},{257,1},{2,258},{258,2},{3,259},{259,3},{4... | collective-permute-start | bytes 221192 | tf_op jit(solution)/shard_map/ppermute | solution.py:19
  118.7 0.9 collective-permute-done.5.b_ref
  119.6 0.7 finish.1
  (30 shorter events, 1.5 us)
Async XLA Ops:
  6.5 56.1 %copy-start.16 = (bf16[2,5,3072]{2,0,1:T(2,128)(2,1)S(1)}, bf16[2,5,3072]{2,0,1:T(2,128)(2,1)}, u32[]{:S(2)}) copy-start(bf16[2,5,3072]{2,0,1:T(2,128)(2,1)} %param.19) | copy-start | bytes 184324
  6.5 56.2 %copy-start.11 = (s32[5]{0:T(128)S(1)}, s32[5]{0:T(128)}, u32[]{:S(2)}) copy-start(s32[5]{0:T(128)} %spans.3) | copy-start | bytes 64
  6.5 56.2 %copy-start.13 = (s32[5]{0:T(128)S(1)}, s32[5]{0:T(128)}, u32[]{:S(2)}) copy-start(s32[5]{0:T(128)} %on.1) | copy-start | bytes 64
  6.5 65.4 %copy-start.12 = (s32[2,5]{1,0:T(2,128)S(1)}, s32[2,5]{1,0:T(2,128)}, u32[]{:S(2)}) copy-start(s32[2,5]{1,0:T(2,128)} %text_len.1) | copy-start | bytes 124
  6.5 102.4 %all-gather.2.cloned.1.call-start = ((), (), s32[]{:S(2)}) async-start(), calls=%async_computation.3 | async-start | bytes 4866048 | tf_op jit(solution)/shard_map/all_gather | solution.py:299
  7.3 1.0 copy-start.2
  8.3 1.0 copy-start.3
  9.3 1.0 copy-start.4
  24.1 26.2 %collective-permute-start = (bf16[4,2,128,384]{3,2,1,0:T(8,128)(2,1)S(1)}, bf16[4,2,128,384]{3,2,1,0:T(8,128)(2,1)S(1)}, u32[]{:S(2)}, u32[]{:S(2)}) collective-permute-start(bf16[4,2,128,384]{3,2,1,0:T(8,128)(2,1)S(1)} %all_to_all.15.own), channel_id=1, source_target_pairs={{0,32},{8,40},{16,48},{24,56},{32,64},{40,72},{48,80},{56,88},{64,... | collective-permute-start | bytes 2359304 | tf_op jit(solution)/shard_map/ppermute | solution.py:26
  31.2 25.7 %collective-permute-start.2 = (bf16[4,2,128,384]{3,2,1,0:T(8,128)(2,1)S(1)}, bf16[4,2,128,384]{3,2,1,0:T(8,128)(2,1)S(1)}, u32[]{:S(2)}, u32[]{:S(2)}) collective-permute-start(bf16[4,2,128,384]{3,2,1,0:T(8,128)(2,1)S(1)} %all_to_all.15.own), channel_id=1, source_target_pairs={{32,0},{40,8},{48,16},{56,24},{64,32},{72,40},{80,48},{88,56},{96,... | collective-permute-start | bytes 2359304 | tf_op jit(solution)/shard_map/ppermute | solution.py:26
  51.2 19.1 %collective-permute-start.1 = (bf16[3,2,128,384]{3,2,1,0:T(8,128)(2,1)}, bf16[3,2,128,384]{3,2,1,0:T(8,128)(2,1)}, u32[]{:S(2)}, u32[]{:S(2)}) collective-permute-start(bf16[3,2,128,384]{3,2,1,0:T(8,128)(2,1)} %slice.8), channel_id=1, source_target_pairs={{0,32},{8,40},{16,48},{24,56},{32,64},{40,72},{48,80},{56,88},{64,... | collective-permute-start | bytes 1769480 | tf_op jit(solution)/shard_map/ppermute | solution.py:26
  57.8 14.1 %collective-permute-start.3 = (bf16[3,2,128,384]{3,2,1,0:T(8,128)(2,1)}, bf16[3,2,128,384]{3,2,1,0:T(8,128)(2,1)}, u32[]{:S(2)}, u32[]{:S(2)}) collective-permute-start(bf16[3,2,128,384]{3,2,1,0:T(8,128)(2,1)} %slice.9), channel_id=1, source_target_pairs={{32,0},{40,8},{48,16},{56,24},{64,32},{72,40},{80,48},{88,56},{96,... | collective-permute-start | bytes 1769480 | tf_op jit(solution)/shard_map/ppermute | solution.py:26
  59.1 11.2 %all-to-all-start.1 = ((bf16[4,128,384]{2,1,0:T(8,128)(2,1)}), bf16[4,128,384]{2,1,0:T(8,128)(2,1)S(1)}, u32[]{:S(2)}, u32[]{:S(2)}) async-start(bf16[4,128,384]{2,1,0:T(8,128)(2,1)} %get-tuple-element.20), calls=%async_computation.1 | async-start | bytes 786432 | tf_op jit(solution)/shard_map/all_to_all | solution.py:32
  62.7 1.1 copy-start.1
  63.9 1.0 copy-start.5
  64.9 0.8 copy-start.10
  65.6 0.7 copy-start.14
  66.3 0.7 copy-start.15
  68.1 0.9 copy-start
  69.0 0.7 copy-start.6
  69.7 0.6 copy-start.8
  77.9 41.7 %copy-start.9 = (f32[136,128]{1,0:T(8,128)S(1)}, f32[136,128]{1,0:T(8,128)}, u32[]{:S(2)}) copy-start(f32[136,128]{1,0:T(8,128)} %copy-done.8) | copy-start | bytes 208900
  91.4 7.1 %collective-permute-start.4 = (bf16[4,128,384]{2,1,0:T(8,128)(2,1)S(1)}, bf16[4,128,384]{2,1,0:T(8,128)(2,1)S(1)}, u32[]{:S(2)}, u32[]{:S(2)}) collective-permute-start(bf16[4,128,384]{2,1,0:T(8,128)(2,1)S(1)} %all_to_all.16.mine), channel_id=1, source_target_pairs={{0,256},{256,0},{1,257},{257,1},{2,258},{258,2},{3,259},{259,3},{4... | collective-permute-start | bytes 1179656 | tf_op jit(solution)/shard_map/ppermute | solution.py:19
  109.0 0.9 copy-start.7
  115.9 3.7 %collective-permute-start.5 = (f32[2,72,128]{2,1,0:T(8,128)S(1)}, f32[2,72,128]{2,1,0:T(8,128)S(1)}, u32[]{:S(2)}, u32[]{:S(2)}) collective-permute-start(f32[2,72,128]{2,1,0:T(8,128)S(1)} %project.1.a_ref), channel_id=1, source_target_pairs={{0,256},{256,0},{1,257},{257,1},{2,258},{258,2},{3,259},{259,3},{4... | collective-permute-start | bytes 221192 | tf_op jit(solution)/shard_map/ppermute | solution.py:19
Sparse Core Ops, SparseCore 0:
  10.5 98.4 all-gather.1

commit v4 on v3

--- a/solution.py
+++ b/solution.py
@@ -10,7 +10,7 @@
 SPAN_MOST = 8
 FULL_WIDTH = 3072
 ROW = 4
-STEPS = 3
+STEPS = 4
 LOG2E = 1.4426950408889634
 NT = (((1,), (1,)), ((), ()))
 
@@ -32,13 +32,21 @@
     return lax.all_to_all(value, "seq", 0, 0, axis_index_groups=groups)
 
 
-def pack_kernel(k_ref, v_ref, q_ref, kv_out, q_out):
+def pack_kernel(k_ref, v_ref, q_ref, kv_out, q_out, sems):
     width = q_out.shape[2]
+    copies = []
     for j in range(ROW):
-        lanes = slice(j * width, (j + 1) * width)
-        kv_out[j, 0] = k_ref[0, :, lanes]
-        kv_out[j, 1] = v_ref[0, :, lanes]
-        q_out[j] = q_ref[0, :, lanes]
+        lanes = pl.ds(j * width, width)
+        for source, target in (
+            (k_ref, kv_out.at[j, 0]), (v_ref, kv_out.at[j, 1]), (q_ref, q_out.at[j])
+        ):
+            copies.append(
+                pltpu.make_async_copy(source.at[0, :, lanes], target, sems.at[len(copies)])
+            )
+    for copy in copies:
+        copy.start()
+    for copy in copies:
+        copy.wait()
 
 
 def pack(keys, values, queries):
@@ -50,9 +58,10 @@
             jax.ShapeDtypeStruct((ROW, 2, rows, width // ROW), keys.dtype),
             jax.ShapeDtypeStruct((ROW, rows, width // ROW), queries.dtype),
         ),
-        in_specs=[vmem] * 3,
+        in_specs=[pl.BlockSpec(memory_space=pl.ANY)] * 3,
         out_specs=(vmem, vmem),
-        compiler_params=pltpu.CompilerParams(vmem_limit_bytes=8 << 20),
+        scratch_shapes=[pltpu.SemaphoreType.DMA((3 * ROW,))],
+        compiler_params=pltpu.CompilerParams(vmem_limit_bytes=56 << 20),
         name="pack",
     )(keys, values, queries)
 
@@ -120,7 +129,7 @@
             pltpu.VMEM((rows, width), jnp.bfloat16),
             pltpu.VMEM((rows, width), jnp.bfloat16),
         ],
-        compiler_params=pltpu.CompilerParams(vmem_limit_bytes=40 << 20),
+        compiler_params=pltpu.CompilerParams(vmem_limit_bytes=16 << 20),
         cost_estimate=pl.CostEstimate(
             flops=4 * pairs * HEAD_WIDTH, bytes_accessed=8 << 20, transcendentals=pairs
         ),
@@ -173,7 +182,7 @@
         ),
         in_specs=[smem] * 5 + [vmem] * 4,
         out_specs=(vmem,) * 4,
-        compiler_params=pltpu.CompilerParams(vmem_limit_bytes=20 << 20),
+        compiler_params=pltpu.CompilerParams(vmem_limit_bytes=16 << 20),
         name="prepare",
     )(where, spans, on, scales, strides, hidden, gate, final_t, latent_t)
 

time: 128 us -> 127 us (level)
  local copies, waits for them, and re-layouts: 12.1 us -> 9.14 us
  Pallas kernels: 14.6 us -> 16.1 us
    unnamed x35 -> x29, local copies, waits for them, and re-layouts: 10.4 us -> 7.37 us
    pallas_call x1, Pallas kernels: 0.88 us -> 2.54 us  [pack(): pl.pallas_call(pack_kernel, out_shape=(jax.ShapeDtypeStruct((ROW, 2, rows...]
  transfers between devices with their start and end apart: 8 -> 8, of which waited for: 5 -> 5; matrix products, arithmetic and copies ran while one was open for 1% -> 1% of each run, Pallas kernels for 6% -> 8%
where the time goes in v4:
time: 127 us; the launch traced here: 126 us
  waiting for transfers between devices  32.2 us (25%)
  starting transfers between devices  28.2 us (22%)
  blocking collectives  26.9 us (21%)
  Pallas kernels  16.1 us (13%)
  between operations  13.5 us (11%)
  local copies, waits for them, and re-layouts  9.14 us (7%)
    all_to_all x2, blocking collectives, spread(): return lax.all_to_all(value, 'seq', 0, 0, axis_index_groups=groups)  26.9 us
    ppermute x4, waiting for transfers between devices, along_z(): return lax.ppermute(value, 'seq', pairs)  19.7 us
    ppermute x4, starting transfers between devices, along_z(): return lax.ppermute(value, 'seq', pairs)  15.4 us
    all_gather x1, waiting for transfers between devices, shards(): weight_t = lax.all_gather(out_weight.T, 'seq', axis=0, tiled=True)  9.57 us
    ppermute x2, starting transfers between devices, swapped(): return lax.ppermute(value, 'guide', [(0, 1), (1, 0)])  9.26 us
    unnamed x29, local copies, waits for them, and re-layouts  7.37 us
    pallas_call x1, Pallas kernels, project(): pl.pallas_call(project_kernel, out_shape=jax.ShapeDtypeStruct((2, final.s...  5.98 us
    pallas_call x1, Pallas kernels, attend(): pl.pallas_call(attend_kernel, out_shape=jax.ShapeDtypeStruct(q.shape, jnp...  5.8 us
  transfers between devices with their start and end apart: 8, of which 5 were waited for; matrix products, arithmetic and copies ran while one was open for 1% of the time, Pallas kernels for 8%

profile of v4, /device:TPU:1, one launch (start us, length us, event | category | flops | bytes accessed | tf_op | source)
XLA Modules:
  0.0 126.1 jit_solution(5334817638951166677)
XLA Ops:
  6.6 0.7 all-gather.2.cloned.1.call-update
  7.3 2.5 %pack.1 = (bf16[4,2,128,384]{3,2,1,0:T(8,128)(2,1)}, bf16[4,128,384]{2,1,0:T(8,128)(2,1)}) custom-call(bf16[1,128,1536]{2,1,0:T(8,128)(2,1)} %k_ref.1, bf16[1,128,1536]{2,1,0:T(8,128)(2,1)} %v_ref.1, bf16[1,128,1536]{2,1,0:T(8,128)(2,1)} %q_ref.1), custom_call_target="tpu_custom_call" | custom-call | tf_op jit(solution)/shard_map/pack/pallas_call | solution.py:55
  9.8 13.2 %all_to_all.15.own = bf16[4,2,128,384]{3,2,1,0:T(8,128)(2,1)S(1)} all-to-all(bf16[4,2,128,384]{3,2,1,0:T(8,128)(2,1)} %get-tuple-element.19), channel_id=1, replica_groups={{0,8,16,24},{32,40,48,56},{64,72,80,88},{96,104,112,120},{128,136,144,1..., dimensions={0} | all-to-all | bytes 1572864 | tf_op jit(solution)/shard_map/all_to_all | solution.py:32
  23.0 7.1 %collective-permute-start = (bf16[4,2,128,384]{3,2,1,0:T(8,128)(2,1)S(1)}, bf16[4,2,128,384]{3,2,1,0:T(8,128)(2,1)S(1)}, u32[]{:S(2)}, u32[]{:S(2)}) collective-permute-start(bf16[4,2,128,384]{3,2,1,0:T(8,128)(2,1)S(1)} %all_to_all.15.own), channel_id=1, source_target_pairs={{0,32},{8,40},{16,48},{24,56},{32,64},{40,72},{48,80},{56,88},{64,... | collective-permute-start | bytes 2359304 | tf_op jit(solution)/shard_map/ppermute | solution.py:26
  30.1 1.3 %collective-permute-start.2 = (bf16[4,2,128,384]{3,2,1,0:T(8,128)(2,1)S(1)}, bf16[4,2,128,384]{3,2,1,0:T(8,128)(2,1)S(1)}, u32[]{:S(2)}, u32[]{:S(2)}) collective-permute-start(bf16[4,2,128,384]{3,2,1,0:T(8,128)(2,1)S(1)} %all_to_all.15.own), channel_id=1, source_target_pairs={{32,0},{40,8},{48,16},{56,24},{64,32},{72,40},{80,48},{88,56},{96,... | collective-permute-start | bytes 2359304 | tf_op jit(solution)/shard_map/ppermute | solution.py:26
  31.4 17.7 %collective-permute-done.near_l = bf16[4,2,128,384]{3,2,1,0:T(8,128)(2,1)S(1)} collective-permute-done((bf16[4,2,128,384]{3,2,1,0:T(8,128)(2,1)S(1)}, bf16[4,2,128,384]{3,2,1,0:T(8,128)(2,1)S(1)}, u32[]{:S(2)}, u32[]{:S(2)}) %collective-permute-start) | collective-permute-done | bytes 786464 | tf_op jit(solution)/shard_map/ppermute | solution.py:26
  49.1 0.9 slice.8
  50.0 5.8 %collective-permute-start.1 = (bf16[3,2,128,384]{3,2,1,0:T(8,128)(2,1)}, bf16[3,2,128,384]{3,2,1,0:T(8,128)(2,1)}, u32[]{:S(2)}, u32[]{:S(2)}) collective-permute-start(bf16[3,2,128,384]{3,2,1,0:T(8,128)(2,1)} %slice.8), channel_id=1, source_target_pairs={{0,32},{8,40},{16,48},{24,56},{32,64},{40,72},{48,80},{56,88},{64,... | collective-permute-start | bytes 1769480 | tf_op jit(solution)/shard_map/ppermute | solution.py:26
  55.7 0.9 slice.9
  56.6 1.3 %collective-permute-start.3 = (bf16[3,2,128,384]{3,2,1,0:T(8,128)(2,1)}, bf16[3,2,128,384]{3,2,1,0:T(8,128)(2,1)}, u32[]{:S(2)}, u32[]{:S(2)}) collective-permute-start(bf16[3,2,128,384]{3,2,1,0:T(8,128)(2,1)} %slice.9), channel_id=1, source_target_pairs={{32,0},{40,8},{48,16},{56,24},{64,32},{72,40},{80,48},{88,56},{96,... | collective-permute-start | bytes 1769480 | tf_op jit(solution)/shard_map/ppermute | solution.py:26
  57.9 3.5 %all-to-all-start.1 = ((bf16[4,128,384]{2,1,0:T(8,128)(2,1)}), bf16[4,128,384]{2,1,0:T(8,128)(2,1)S(1)}, u32[]{:S(2)}, u32[]{:S(2)}) async-start(bf16[4,128,384]{2,1,0:T(8,128)(2,1)} %get-tuple-element.20), calls=%async_computation.1 | async-start | bytes 786432 | tf_op jit(solution)/shard_map/all_to_all | solution.py:32
  61.4 0.1 pad_add_fusion.where
  61.5 1.1 copy-done.1
  62.6 1.0 copy-done.2
  63.6 0.8 copy-done.7
  64.4 0.7 copy-done.11
  65.0 0.7 copy-done.12
  65.7 1.1 prepare.1
  66.9 0.9 copy-done
  67.8 0.7 copy-done.3
  68.4 0.6 copy-done.5
  69.1 2.0 %collective-permute-done.3.far_r = bf16[3,2,128,384]{3,2,1,0:T(8,128)(2,1)} collective-permute-done((bf16[3,2,128,384]{3,2,1,0:T(8,128)(2,1)}, bf16[3,2,128,384]{3,2,1,0:T(8,128)(2,1)}, u32[]{:S(2)}, u32[]{:S(2)}) %collective-permute-start.3) | collective-permute-done | bytes 589856 | tf_op jit(solution)/shard_map/ppermute | solution.py:26
  71.1 5.8 %attend.1 = bf16[4,128,384]{2,1,0:T(8,128)(2,1)S(1)} custom-call(s32[2]{0:T(128)S(1)} %pad_add_fusion.where, s32[5]{0:T(128)S(1)} %copy-done.8, s32[2,5]{1,0:T(2,128)S(1)} %copy-done.9, bf16[4,128,384]{2,1,0:T(8,128)(2,1)S(1)} %all-to-all-done.1.q_ref, bf16[3,2,128,384]{3,2,1,0:T(8,128)(2,1)} %collective-permute-done.1.far_l, ...), custom_call_target="tpu_custom_call" | custom-call | flops 805306368 | bytes 8388608 | tf_op jit(solution)/shard_map/attend/pallas_call | solution.py:123
  76.9 13.7 %all_to_all.16.mine = bf16[4,128,384]{2,1,0:T(8,128)(2,1)S(1)} all-to-all(bf16[4,128,384]{2,1,0:T(8,128)(2,1)S(1)} %attend.1), channel_id=1, replica_groups={{0,8,16,24},{32,40,48,56},{64,72,80,88},{96,104,112,120},{128,136,144,1..., dimensions={0} | all-to-all | bytes 786432 | tf_op jit(solution)/shard_map/all_to_all | solution.py:32
  90.6 6.5 %collective-permute-start.4 = (bf16[4,128,384]{2,1,0:T(8,128)(2,1)S(1)}, bf16[4,128,384]{2,1,0:T(8,128)(2,1)S(1)}, u32[]{:S(2)}, u32[]{:S(2)}) collective-permute-start(bf16[4,128,384]{2,1,0:T(8,128)(2,1)S(1)} %all_to_all.16.mine), channel_id=1, source_target_pairs={{0,256},{256,0},{1,257},{257,1},{2,258},{258,2},{3,259},{259,3},{4... | collective-permute-start | bytes 1179656 | tf_op jit(solution)/shard_map/ppermute | solution.py:19
  97.1 1.3 %collective-permute-done.4.theirs = bf16[4,128,384]{2,1,0:T(8,128)(2,1)S(1)} collective-permute-done((bf16[4,128,384]{2,1,0:T(8,128)(2,1)S(1)}, bf16[4,128,384]{2,1,0:T(8,128)(2,1)S(1)}, u32[]{:S(2)}, u32[]{:S(2)}) %collective-permute-start.4) | collective-permute-done | bytes 393248 | tf_op jit(solution)/shard_map/ppermute | solution.py:19
  98.5 9.6 %all-gather.2.cloned.1.call-done.w_ref = bf16[1536,1536]{1,0:T(8,128)(2,1)} async-done(((bf16[48,1536]{1,0:T(8,128)(2,1)}), bf16[1536,1536]{1,0:T(8,128)(2,1)}) %all-gather.2.cloned.1.call-update) | async-done | bytes 4718608 | tf_op jit(solution)/shard_map/all_gather | solution.py:308
  108.0 0.9 copy-done.4
  109.0 6.0 %project.1.a_ref = f32[2,72,128]{2,1,0:T(8,128)S(1)} custom-call(s32[2]{0:T(128)S(1)} %pad_add_fusion.where, bf16[4,128,384]{2,1,0:T(8,128)(2,1)S(1)} %all_to_all.16.mine, bf16[4,128,384]{2,1,0:T(8,128)(2,1)S(1)} %collective-permute-done.4.theirs, bf16[1536,1536]{1,0:T(8,128)(2,1)} %all-gather.2.cloned.1.call-done.w_ref, ...), custom_call_target="tpu_custom_call" | custom-call | flops 1207959552 | bytes 8388608 | tf_op jit(solution)/shard_map/project/pallas_call | solution.py:241
  115.0 2.7 %collective-permute-start.5 = (f32[2,72,128]{2,1,0:T(8,128)S(1)}, f32[2,72,128]{2,1,0:T(8,128)S(1)}, u32[]{:S(2)}, u32[]{:S(2)}) collective-permute-start(f32[2,72,128]{2,1,0:T(8,128)S(1)} %project.1.a_ref), channel_id=1, source_target_pairs={{0,256},{256,0},{1,257},{257,1},{2,258},{258,2},{3,259},{259,3},{4... | collective-permute-start | bytes 221192 | tf_op jit(solution)/shard_map/ppermute | solution.py:19
  117.7 0.9 collective-permute-done.5.b_ref
  118.6 0.7 finish.1
  (24 shorter events, 0.1 us)
Async XLA Ops:
  6.5 54.8 %copy-start.13 = (bf16[2,5,3072]{2,0,1:T(2,128)(2,1)S(1)}, bf16[2,5,3072]{2,0,1:T(2,128)(2,1)}, u32[]{:S(2)}) copy-start(bf16[2,5,3072]{2,0,1:T(2,128)(2,1)} %param.19) | copy-start | bytes 184324
  6.5 55.0 %copy-start.8 = (s32[5]{0:T(128)S(1)}, s32[5]{0:T(128)}, u32[]{:S(2)}) copy-start(s32[5]{0:T(128)} %spans.3) | copy-start | bytes 64
  6.5 55.0 %copy-start.10 = (s32[5]{0:T(128)S(1)}, s32[5]{0:T(128)}, u32[]{:S(2)}) copy-start(s32[5]{0:T(128)} %on.1) | copy-start | bytes 64
  6.5 64.6 %copy-start.9 = (s32[2,5]{1,0:T(2,128)S(1)}, s32[2,5]{1,0:T(2,128)}, u32[]{:S(2)}) copy-start(s32[2,5]{1,0:T(2,128)} %text_len.1) | copy-start | bytes 124
  6.5 101.5 %all-gather.2.cloned.1.call-start = ((), (), s32[]{:S(2)}) async-start(), calls=%async_computation.3 | async-start | bytes 4866048 | tf_op jit(solution)/shard_map/all_gather | solution.py:308
  23.0 26.1 %collective-permute-start = (bf16[4,2,128,384]{3,2,1,0:T(8,128)(2,1)S(1)}, bf16[4,2,128,384]{3,2,1,0:T(8,128)(2,1)S(1)}, u32[]{:S(2)}, u32[]{:S(2)}) collective-permute-start(bf16[4,2,128,384]{3,2,1,0:T(8,128)(2,1)S(1)} %all_to_all.15.own), channel_id=1, source_target_pairs={{0,32},{8,40},{16,48},{24,56},{32,64},{40,72},{48,80},{56,88},{64,... | collective-permute-start | bytes 2359304 | tf_op jit(solution)/shard_map/ppermute | solution.py:26
  30.1 25.6 %collective-permute-start.2 = (bf16[4,2,128,384]{3,2,1,0:T(8,128)(2,1)S(1)}, bf16[4,2,128,384]{3,2,1,0:T(8,128)(2,1)S(1)}, u32[]{:S(2)}, u32[]{:S(2)}) collective-permute-start(bf16[4,2,128,384]{3,2,1,0:T(8,128)(2,1)S(1)} %all_to_all.15.own), channel_id=1, source_target_pairs={{32,0},{40,8},{48,16},{56,24},{64,32},{72,40},{80,48},{88,56},{96,... | collective-permute-start | bytes 2359304 | tf_op jit(solution)/shard_map/ppermute | solution.py:26
  50.0 19.1 %collective-permute-start.1 = (bf16[3,2,128,384]{3,2,1,0:T(8,128)(2,1)}, bf16[3,2,128,384]{3,2,1,0:T(8,128)(2,1)}, u32[]{:S(2)}, u32[]{:S(2)}) collective-permute-start(bf16[3,2,128,384]{3,2,1,0:T(8,128)(2,1)} %slice.8), channel_id=1, source_target_pairs={{0,32},{8,40},{16,48},{24,56},{32,64},{40,72},{48,80},{56,88},{64,... | collective-permute-start | bytes 1769480 | tf_op jit(solution)/shard_map/ppermute | solution.py:26
  56.6 14.5 %collective-permute-start.3 = (bf16[3,2,128,384]{3,2,1,0:T(8,128)(2,1)}, bf16[3,2,128,384]{3,2,1,0:T(8,128)(2,1)}, u32[]{:S(2)}, u32[]{:S(2)}) collective-permute-start(bf16[3,2,128,384]{3,2,1,0:T(8,128)(2,1)} %slice.9), channel_id=1, source_target_pairs={{32,0},{40,8},{48,16},{56,24},{64,32},{72,40},{80,48},{88,56},{96,... | collective-permute-start | bytes 1769480 | tf_op jit(solution)/shard_map/ppermute | solution.py:26
  57.9 11.2 %all-to-all-start.1 = ((bf16[4,128,384]{2,1,0:T(8,128)(2,1)}), bf16[4,128,384]{2,1,0:T(8,128)(2,1)S(1)}, u32[]{:S(2)}, u32[]{:S(2)}) async-start(bf16[4,128,384]{2,1,0:T(8,128)(2,1)} %get-tuple-element.20), calls=%async_computation.1 | async-start | bytes 786432 | tf_op jit(solution)/shard_map/all_to_all | solution.py:32
  61.5 1.1 copy-start.1
  62.6 1.0 copy-start.2
  63.6 0.8 copy-start.7
  64.4 0.7 copy-start.11
  65.0 0.7 copy-start.12
  66.8 0.9 copy-start
  67.8 0.7 copy-start.3
  68.4 0.6 copy-start.5
  76.9 41.7 %copy-start.6 = (f32[136,128]{1,0:T(8,128)S(1)}, f32[136,128]{1,0:T(8,128)}, u32[]{:S(2)}) copy-start(f32[136,128]{1,0:T(8,128)} %copy-done.5) | copy-start | bytes 208900
  90.6 7.9 %collective-permute-start.4 = (bf16[4,128,384]{2,1,0:T(8,128)(2,1)S(1)}, bf16[4,128,384]{2,1,0:T(8,128)(2,1)S(1)}, u32[]{:S(2)}, u32[]{:S(2)}) collective-permute-start(bf16[4,128,384]{2,1,0:T(8,128)(2,1)S(1)} %all_to_all.16.mine), channel_id=1, source_target_pairs={{0,256},{256,0},{1,257},{257,1},{2,258},{258,2},{3,259},{259,3},{4... | collective-permute-start | bytes 1179656 | tf_op jit(solution)/shard_map/ppermute | solution.py:19
  108.0 0.9 copy-start.4
  115.0 3.6 %collective-permute-start.5 = (f32[2,72,128]{2,1,0:T(8,128)S(1)}, f32[2,72,128]{2,1,0:T(8,128)S(1)}, u32[]{:S(2)}, u32[]{:S(2)}) collective-permute-start(f32[2,72,128]{2,1,0:T(8,128)S(1)} %project.1.a_ref), channel_id=1, source_target_pairs={{0,256},{256,0},{1,257},{257,1},{2,258},{258,2},{3,259},{259,3},{4... | collective-permute-start | bytes 221192 | tf_op jit(solution)/shard_map/ppermute | solution.py:19
Sparse Core Ops, SparseCore 0:
  10.5 97.4 all-gather.1

commit v5 on v4

v5 whole, which is shorter than its diff:
```python
import jax
import jax.numpy as jnp
from jax import lax
from jax.experimental import pallas as pl
from jax.experimental.pallas import tpu as pltpu
from jax.sharding import PartitionSpec as P

HEAD_WIDTH = 128
TILE = 128
SPAN_MOST = 8
FULL_WIDTH = 3072
SHARD = 48
ROW = 4
LOG2E = 1.4426950408889634
NT = (((1,), (1,)), ((), ()))


def swapped(value):
    return lax.ppermute(value, "guide", [(0, 1), (1, 0)])


def along_z(value, by):
    count = lax.axis_size("seq")
    step = by * ROW
    pairs = [(i, i + step) for i in range(count) if 0 <= i + step < count]
    return lax.ppermute(value, "seq", pairs)


def spread_wide(value):
    count = lax.axis_size("seq")
    groups = [
        [g * count + z * ROW + x for g in range(2) for x in range(ROW)]
        for z in range(count // ROW)
    ]
    return lax.all_to_all(value, ("guide", "seq"), 0, 0, axis_index_groups=groups)


def along_x(value, by):
    count = lax.axis_size("seq")
    pairs = [(i, i // ROW * ROW + (i + by) % ROW) for i in range(count)]
    return lax.ppermute(value, "seq", pairs)


def all_of_row(own):
    middle = own.shape[0] // 2
    return (
        own,
        along_x(own, 1),
        along_x(own, -1),
        along_x(own[:middle], 2),
        along_x(own[middle:], -2),
    )


def spread(value):
    count = lax.axis_size("seq")
    groups = [[z * ROW + x for x in range(ROW)] for z in range(count // ROW)]
    return lax.all_to_all(value, "seq", 0, 0, axis_index_groups=groups)


def gather_weight(copies):
    count = lax.axis_size("seq")
    columns = [[z * ROW + x for z in range(count // ROW)] for x in range(ROW)]
    return lax.all_to_all(copies, "seq", 0, 0, axis_index_groups=columns).reshape(
        -1, copies.shape[2]
    )


def pack_kernel(k_ref, v_ref, kv_out, sems):
    width = kv_out.shape[3]
    copies = []
    for j in range(ROW):
        lanes = pl.ds(j * width, width)
        for i, source in enumerate((k_ref, v_ref)):
            copies.append(
                pltpu.make_async_copy(
                    source.at[0, :, lanes], kv_out.at[j, i], sems.at[len(copies)]
                )
            )
    for copy in copies:
        copy.start()
    for copy in copies:
        copy.wait()


def pack(keys, values):
    _, rows, width = keys.shape
    return pl.pallas_call(
        pack_kernel,
        out_shape=jax.ShapeDtypeStruct((ROW, 2, rows, width // ROW), keys.dtype),
        in_specs=[pl.BlockSpec(memory_space=pl.ANY)] * 2,
        out_specs=pl.BlockSpec(memory_space=pltpu.VMEM),
        scratch_shapes=[pltpu.SemaphoreType.DMA((2 * ROW,))],
        compiler_params=pltpu.CompilerParams(vmem_limit_bytes=56 << 20),
        name="pack",
    )(keys, values)


def request_of(tile, spans, tables):
    start = jnp.int32(0)
    found = [jnp.int32(0) for _ in range(len(tables) + 3)]
    for r in range(spans.shape[0]):
        span = spans[r]
        here = (tile >= start) & (tile < start + span)
        row = [start, span, jnp.int32(r)] + [table(r) for table in tables]
        found = [jnp.where(here, new, old) for new, old in zip(row, found)]
        start = start + span
    return found


def attend_kernel(
    where, spans, text_len, q_ref, far_l, one_l, near_l, own, near_r, one_r, far_r, o_ref, k_all, v_all
):
    place, half = where[0], where[1]
    first = (place // ROW) * ROW
    heads = q_ref.shape[3] // HEAD_WIDTH
    at = 0
    for ref in (far_l, one_l, near_l, own, near_r, one_r, far_r):
        for i in range(ref.shape[0]):
            k_all[at * TILE : (at + 1) * TILE, :] = ref[i, 0]
            v_all[at * TILE : (at + 1) * TILE, :] = ref[i, 1]
            at += 1
    keys = SPAN_MOST * TILE
    column = lax.broadcasted_iota(jnp.int32, (1, keys), 1)
    factor = HEAD_WIDTH**-0.5 * LOG2E
    for t in range(ROW):
        start, span, _, live = request_of(first + t, spans, [lambda r: text_len[half, r]])
        begin = jnp.clip(start - (first - (SPAN_MOST - 1)), 0, SPAN_MOST + ROW - 2)
        begin = pl.multiple_of(begin * TILE, TILE)
        allowed = ((column < live) | (column >= TILE)) & (column < span * TILE)
        bias = jnp.where(allowed, 0.0, -1e30)
        for h in range(heads):
            lanes = slice(h * HEAD_WIDTH, (h + 1) * HEAD_WIDTH)
            key = k_all[pl.ds(begin, keys), lanes]
            value = v_all[pl.ds(begin, keys), lanes]
            score = lax.dot_general(
                q_ref[t, 0, :, lanes], key, NT, preferred_element_type=jnp.float32
            )
            score = score + bias
            top = jnp.max(score, axis=-1, keepdims=True)
            weight = jnp.exp2((score - top) * factor)
            total = jnp.sum(weight, axis=-1, keepdims=True)
            mixed = jnp.dot(weight.astype(jnp.bfloat16), value, preferred_element_type=jnp.float32)
            out = (mixed / total).astype(jnp.bfloat16)
            o_ref[t, :, lanes] = out


def attend(where, spans, text_len, q, parts):
    rows = (SPAN_MOST * 2 + ROW - 2) * TILE
    width = q.shape[3]
    smem = pl.BlockSpec(memory_space=pltpu.SMEM)
    vmem = pl.BlockSpec(memory_space=pltpu.VMEM)
    pairs = ROW * TILE * SPAN_MOST * TILE * (width // HEAD_WIDTH)
    return pl.pallas_call(
        attend_kernel,
        out_shape=jax.ShapeDtypeStruct((ROW, TILE, width), jnp.bfloat16),
        in_specs=[smem] * 3 + [vmem] * 8,
        out_specs=vmem,
        scratch_shapes=[
            pltpu.VMEM((rows, width), jnp.bfloat16),
            pltpu.VMEM((rows, width), jnp.bfloat16),
        ],
        compiler_params=pltpu.CompilerParams(vmem_limit_bytes=58 << 20),
        cost_estimate=pl.CostEstimate(
            flops=4 * pairs * HEAD_WIDTH, bytes_accessed=8 << 20, transcendentals=pairs
        ),
        name="attend",
    )(where, spans, text_len, q, *parts)


def regroup(source, x):
    count = source.shape[0] // SHARD
    starts = [(z * ROW + x) * SHARD for z in range(count // ROW)]
    return jnp.concatenate(
        [source[pl.ds(pl.multiple_of(start, 16), SHARD), :] for start in starts], axis=0
    )


def prepare_kernel(
    where, spans, on, scales, strides, queries, hidden, brought, gate, final_t, latent_t,
    sent, cols, aux, order,
):
    place, half = where[0], where[1]
    x = lax.rem(place, ROW)
    _, _, _, switch, factor, stride = request_of(
        place, spans, [lambda r: on[r], lambda r: scales[r], lambda r: strides[r]]
    )
    channels, width = final_t.shape[0], hidden.shape[2]
    for d in range(ROW):
        sent[d, 0] = queries[0, :, d * width // ROW : (d + 1) * width // ROW]
    for side, rows in enumerate((hidden[half], brought[...])):
        order[...] = rows.astype(jnp.float32).T
        for d in range(ROW):
            sent[d, 1 + side] = regroup(order, d).T.astype(jnp.bfloat16)
    requests = gate.shape[1]
    rest = jnp.zeros((TILE - channels - requests, width), jnp.float32)
    for side, which in enumerate((half, 1 - half)):
        lanes = pl.ds(pl.multiple_of(which * width, 128), width)
        rows = [final_t[:, lanes].astype(jnp.float32)]
        rows += [gate[half, r : r + 1, lanes].astype(jnp.float32) for r in range(requests)]
        order[...] = jnp.concatenate(rows + [rest], axis=0).T
        cols[side] = regroup(order, x).T
    number = lax.broadcasted_iota(jnp.int32, (FULL_WIDTH, TILE), 0).astype(jnp.float32)
    shard = jnp.floor((number + 0.5) * (1.0 / SHARD))
    ring = shard - ROW * jnp.floor((shard + 0.5) * (1.0 / ROW))
    aux[:channels] = latent_t[...]
    for d in range(ROW):
        chosen = jnp.where(ring == d, 1.0, 0.0).astype(jnp.bfloat16)
        aux[(d + 1) * channels : (d + 2) * channels] = jnp.dot(
            final_t[...], chosen, preferred_element_type=jnp.float32
        )
    line = lax.broadcasted_iota(jnp.int32, (8, TILE), 0)
    scalars = jnp.where(line == 1, factor, jnp.where(line == 2, stride, 0.0))
    aux[(ROW + 1) * channels :] = jnp.where(line == 0, switch.astype(jnp.float32), scalars)


def prepare(where, spans, on, scales, strides, queries, hidden, brought, gate, final_t, latent_t):
    width, channels = hidden.shape[2], final_t.shape[0]
    smem = pl.BlockSpec(memory_space=pltpu.SMEM)
    vmem = pl.BlockSpec(memory_space=pltpu.VMEM)
    return pl.pallas_call(
        prepare_kernel,
        out_shape=(
            jax.ShapeDtypeStruct((ROW, 3, TILE, width // ROW), jnp.bfloat16),
            jax.ShapeDtypeStruct((2, TILE, width // ROW), jnp.float32),
            jax.ShapeDtypeStruct(((ROW + 1) * channels + 8, TILE), jnp.float32),
        ),
        in_specs=[smem] * 5 + [vmem] * 6,
        out_specs=(vmem,) * 3,
        scratch_shapes=[pltpu.VMEM((width, TILE), jnp.float32)],
        compiler_params=pltpu.CompilerParams(vmem_limit_bytes=16 << 20),
        name="prepare",
    )(where, spans, on, scales, strides, queries, hidden, brought, gate, final_t, latent_t)


def project_kernel(
    where, spans, own, behind, ahead, far_a, far_b, w_mine, w_other, hidden, cols,
    out, attn, state,
):
    first = where[0] // ROW * ROW
    x = where[0] - first
    tiles, _, depth = own.shape
    middle = far_a.shape[0]
    for ref, step, begin in (
        (own, 0, 0), (behind, ROW - 1, 0), (ahead, 1, 0), (far_a, 2, 0), (far_b, 2, middle)
    ):
        lanes = pl.ds(pl.multiple_of(lax.rem(x + step, ROW) * depth, 128), depth)
        for i in range(ref.shape[0]):
            attn[(begin + i) * TILE : (begin + i + 1) * TILE, lanes] = ref[i]
    channels = out.shape[1] - 8
    block = cols.shape[2]
    for side, weight in enumerate((w_mine, w_other)):
        total = lax.dot_general(attn[...], weight[...], NT, preferred_element_type=jnp.float32)
        for t in range(tiles):
            _, _, request = request_of(first + t, spans, [])
            scale = jnp.zeros((1, block), jnp.float32)
            for r in range(spans.shape[0]):
                row = cols[side, channels + r : channels + r + 1, :]
                scale = jnp.where(request == r, row, scale)
            rows = slice(t * TILE, (t + 1) * TILE)
            state[side, rows] = (
                hidden[t, 1 + side].astype(jnp.float32) + scale * total[rows]
            )
    mean = jnp.sum(state[0], axis=-1, keepdims=True) + jnp.sum(state[1], axis=-1, keepdims=True)
    mean = mean * (1.0 / (2 * block))
    squares = jnp.zeros_like(mean)
    speed = jnp.zeros((tiles * TILE, channels), jnp.float32)
    for side in range(2):
        centre = state[side] - mean
        squares += jnp.sum(centre * centre, axis=-1, keepdims=True)
        high = centre.astype(jnp.bfloat16)
        low = (centre - high.astype(jnp.float32)).astype(jnp.bfloat16)
        final = cols[side, :channels, :].astype(jnp.bfloat16)
        speed += lax.dot_general(high, final, NT, preferred_element_type=jnp.float32)
        speed += lax.dot_general(low, final, NT, preferred_element_type=jnp.float32)
    lane = lax.broadcasted_iota(jnp.int32, (tiles * TILE, TILE - channels), 1)
    extra = jnp.where(lane == 0, mean, jnp.where(lane == 1, squares, 0.0))
    sums = jnp.concatenate([speed, extra], axis=1)
    for t in range(tiles):
        turned = sums[t * TILE : (t + 1) * TILE].T[: channels + 8]
        out[t] = turned
        out[tiles + t] = turned


def project(where, spans, attn, weights, hidden, cols, channels):
    block, depth = weights[0].shape
    tokens = attn[0].shape[0] * TILE
    smem = pl.BlockSpec(memory_space=pltpu.SMEM)
    vmem = pl.BlockSpec(memory_space=pltpu.VMEM)
    return pl.pallas_call(
        project_kernel,
        out_shape=jax.ShapeDtypeStruct((2 * ROW, channels + 8, TILE), jnp.float32),
        in_specs=[smem] * 2 + [vmem] * 9,
        out_specs=vmem,
        scratch_shapes=[
            pltpu.VMEM((tokens, depth), jnp.bfloat16),
            pltpu.VMEM((2, tokens, block), jnp.float32),
        ],
        compiler_params=pltpu.CompilerParams(vmem_limit_bytes=58 << 20),
        cost_estimate=pl.CostEstimate(
            flops=4 * tokens * depth * block, bytes_accessed=8 << 20, transcendentals=0
        ),
        name="project",
    )(where, spans, *attn, *weights, hidden, cols)


def finish_kernel(parts, aux, out_t):
    channels = out_t.shape[0]
    tables = [aux[(d + 1) * channels : (d + 2) * channels, :] for d in range(ROW)]
    last = (ROW + 1) * channels
    switch, factor, stride = (aux[last + i : last + i + 1, :] for i in range(3))
    speeds = []
    for which in range(2):
        four = [parts[which * ROW + d] for d in range(ROW)]
        means = [p[channels : channels + 1] for p in four]
        mean = sum(means) / ROW
        gaps = [m - mean for m in means]
        squares = sum(
            p[channels + 1 : channels + 2] + gap * gap * (FULL_WIDTH / ROW)
            for p, gap in zip(four, gaps)
        )
        raw = sum(p[:channels] + gap * table for p, gap, table in zip(four, gaps, tables))
        speeds.append(raw * lax.rsqrt(squares / FULL_WIDTH + 1e-06))
    cond, uncond = speeds
    blend = jnp.where(switch > 0, uncond + factor * (cond - uncond), cond)
    upper = jnp.sqrt(jnp.mean(cond * cond, axis=0, keepdims=True) + 1e-06)
    lower = jnp.sqrt(jnp.mean(blend * blend, axis=0, keepdims=True) + 1e-06)
    out_t[...] = aux[:channels, :] + stride * (blend * (upper / lower))


def finish(parts, aux, channels):
    vmem = pl.BlockSpec(memory_space=pltpu.VMEM)
    return pl.pallas_call(
        finish_kernel,
        out_shape=jax.ShapeDtypeStruct((channels, TILE), jnp.float32),
        in_specs=[vmem] * 2,
        out_specs=vmem,
        compiler_params=pltpu.CompilerParams(vmem_limit_bytes=4 << 20),
        name="finish",
    )(parts, aux)


def shards(
    queries,
    keys,
    values,
    hidden_in,
    out_weight,
    final_weight,
    gate_mod,
    span_tiles,
    text_len,
    guide_on,
    guide_scale,
    step_size,
    latent,
):
    place = lax.axis_index("seq")
    half = lax.axis_index("guide")
    where = jnp.stack([place, half]).astype(jnp.int32)
    away = lax.dynamic_index_in_dim(hidden_in, 1 - half, 0, keepdims=False)
    brought = swapped(away)
    own = spread(pack(keys, values))
    queries, gate_mod, _ = lax.optimization_barrier((queries, gate_mod, own))
    near_l = along_z(own[1:], 1)
    near_r = along_z(own[:-1], -1)
    one_l = along_z(own[:1], 1)
    one_r = along_z(own[-1:], -1)
    far_l = along_z(near_l, 1)
    far_r = along_z(near_r, -1)
    sent, cols, aux = prepare(
        where,
        span_tiles,
        guide_on,
        guide_scale,
        step_size,
        queries,
        hidden_in,
        brought,
        gate_mod,
        final_weight.T,
        latent.T,
    )
    local = spread(sent)
    parts = (far_l, one_l, near_l, own, near_r, one_r, far_r)
    shard = jnp.broadcast_to(out_weight.T, (lax.axis_size("seq") // ROW, *out_weight.T.shape))
    shard, queries = lax.optimization_barrier((shard, queries))
    shard, *_ = lax.optimization_barrier((shard, *parts))
    weight = gather_weight(shard)
    attn = all_of_row(attend(where, span_tiles, text_len, local, parts))
    weight, attn = lax.optimization_barrier((weight, attn))
    weights = [weight, swapped(weight)]
    channels = latent.shape[1]
    sums = project(where, span_tiles, attn, weights, local, cols, channels)
    return finish(spread_wide(sums), aux, channels).T


def solution(mesh):
    in_specs = (
        P("guide", ("rep", "seq"), None),
        P("guide", ("rep", "seq"), None),
        P("guide", ("rep", "seq"), None),
        P(None, ("rep", "seq"), "guide"),
        P(None, ("guide", "seq")),
        P(),
        P(None, "rep", None),
        P("rep"),
        P(None, "rep"),
        P("rep"),
        P("rep"),
        P("rep"),
        P(("rep", "seq"), None),
    )
    out_specs = P(("rep", "seq"), None)
    return jax.shard_map(shards, mesh=mesh, in_specs=in_specs, out_specs=out_specs, check_vma=False)
```

time: 127 us -> 127 us (level)
  starting transfers between devices: 28.2 us -> 69.4 us
  blocking collectives: 26.9 us -> 11.1 us
  waiting for transfers between devices: 32.2 us -> 17.8 us
  between operations: 13.5 us -> 0.35 us
  Pallas kernels: 16.1 us -> 19.9 us
  local copies, waits for them, and re-layouts: 9.14 us -> 7.77 us
    all_to_all x2 -> x1, blocking collectives: 26.9 us -> 11.1 us  [spread_wide(): lax.all_to_all(value, ('guide', 'seq'), 0, 0, axis_index_groups=groups)]
    ppermute x4 -> x6, waiting for transfers between devices: 19.7 us -> 6.6 us  [along_z(): return lax.ppermute(value, 'seq', pairs)]
    ppermute x0 -> x4, starting transfers between devices: none -> 12.1 us  [along_x(): return lax.ppermute(value, 'seq', pairs)]
    all_to_all x0 -> x1, starting transfers between devices: none -> 11.6 us  [gather_weight(): lax.all_to_all(copies, 'seq', 0, 0, axis_index_groups=columns)]
    all_gather x1 -> x0, waiting for transfers between devices: 9.57 us -> none  [shards(): weight_t = lax.all_gather(out_weight.T, 'seq', axis=0, tiled=True)]
    ppermute x0 -> x4, waiting for transfers between devices: none -> 7.65 us  [along_x(): return lax.ppermute(value, 'seq', pairs)]
    ppermute x4 -> x6, starting transfers between devices: 15.4 us -> 23 us  [along_z(): return lax.ppermute(value, 'seq', pairs)]
    all_to_all x1 -> x2, starting transfers between devices: 3.47 us -> 8.51 us  [spread(): return lax.all_to_all(value, 'seq', 0, 0, axis_index_groups=groups)]
  transfers between devices with their start and end apart: 8 -> 15, of which waited for: 5 -> 8; matrix products, arithmetic and copies ran while one was open for 1% -> 4% of each run, Pallas kernels for 8% -> 9%
where the time goes in v5:
time: 127 us; the launch traced here: 126 us
  starting transfers between devices  69.4 us (55%)
  Pallas kernels  19.9 us (16%)
  waiting for transfers between devices  17.8 us (14%)
  blocking collectives  11.1 us (9%)
  local copies, waits for them, and re-layouts  7.77 us (6%)
    ppermute x6, starting transfers between devices, along_z(): return lax.ppermute(value, 'seq', pairs)  23 us
    ppermute x2, starting transfers between devices, swapped(): return lax.ppermute(value, 'guide', [(0, 1), (1, 0)])  14.2 us
    ppermute x4, starting transfers between devices, along_x(): return lax.ppermute(value, 'seq', pairs)  12.1 us
    all_to_all x1, starting transfers between devices, gather_weight(): lax.all_to_all(copies, 'seq', 0, 0, axis_index_groups=columns)  11.6 us
    all_to_all x1, blocking collectives, spread_wide(): lax.all_to_all(value, ('guide', 'seq'), 0, 0, axis_index_groups=groups)  11.1 us
    all_to_all x2, starting transfers between devices, spread(): return lax.all_to_all(value, 'seq', 0, 0, axis_index_groups=groups)  8.51 us
    ppermute x4, waiting for transfers between devices, along_x(): return lax.ppermute(value, 'seq', pairs)  7.65 us
    pallas_call x1, Pallas kernels, attend(): pl.pallas_call(attend_kernel, out_shape=jax.ShapeDtypeStruct((ROW, TILE,...  7.64 us
  transfers between devices with their start and end apart: 15, of which 8 were waited for; matrix products, arithmetic and copies ran while one was open for 4% of the time, Pallas kernels for 9%

profile of v5, /device:TPU:1, one launch (start us, length us, event | category | flops | bytes accessed | tf_op | source)
XLA Modules:
  0.0 126.4 jit_solution(7971946922288095562)
XLA Ops:
  0.0 2.2 %pack.1 = bf16[4,2,128,384]{3,2,1,0:T(8,128)(2,1)} custom-call(bf16[1,128,1536]{2,1,0:T(8,128)(2,1)} %k_ref.1, bf16[1,128,1536]{2,1,0:T(8,128)(2,1)} %v_ref.1), custom_call_target="tpu_custom_call" | custom-call | tf_op jit(solution)/shard_map/pack/pallas_call | solution.py:88
  2.2 5.0 %all-to-all-start = ((bf16[4,2,128,384]{3,2,1,0:T(8,128)(2,1)}), bf16[4,2,128,384]{3,2,1,0:T(8,128)(2,1)S(1)}, u32[]{:S(2)}, u32[]{:S(2)}) async-start(bf16[4,2,128,384]{3,2,1,0:T(8,128)(2,1)} %pack.1), calls=%async_computation | async-start | bytes 1572864 | tf_op jit(solution)/shard_map/all_to_all | solution.py:58
  7.3 7.6 %collective-permute-start.6 = (bf16[128,1536]{1,0:T(8,128)(2,1)S(1)}, bf16[128,1536]{1,0:T(8,128)(2,1)S(1)}, u32[]{:S(2)}, u32[]{:S(2)}) collective-permute-start(bf16[128,1536]{1,0:T(8,128)(2,1)S(1)} %dynamic-slice_bitcast_fusion), channel_id=1, source_target_pairs={{0,256},{256,0},{1,257},{257,1},{2,258},{258,2},{3,259},{259,3},{4... | collective-permute-start | bytes 1179656 | tf_op jit(solution)/shard_map/ppermute | solution.py:19
  15.5 1.3 %fusion.1 = (bf16[3,2,128,384]{3,2,1,0:T(8,128)(2,1)}, bf16[3,2,128,384]{3,2,1,0:T(8,128)(2,1)}) fusion(bf16[4,2,128,384]{3,2,1,0:T(8,128)(2,1)S(1)} %all-to-all-done.own), kind=kLoop, calls=%fused_computation.3 | loop fusion | bytes 2359296 | tf_op jit(solution)/shard_map/slice | solution.py:366
  16.8 1.3 %collective-permute-start.3 = (bf16[3,2,128,384]{3,2,1,0:T(8,128)(2,1)}, bf16[3,2,128,384]{3,2,1,0:T(8,128)(2,1)}, u32[]{:S(2)}, u32[]{:S(2)}) collective-permute-start(bf16[3,2,128,384]{3,2,1,0:T(8,128)(2,1)} %get-tuple-element.33), channel_id=1, source_target_pairs={{32,0},{40,8},{48,16},{56,24},{64,32},{72,40},{80,48},{88,56},{96,... | collective-permute-start | bytes 1769480 | tf_op jit(solution)/shard_map/ppermute | solution.py:26
  18.1 8.5 %collective-permute-start = (bf16[3,2,128,384]{3,2,1,0:T(8,128)(2,1)}, bf16[3,2,128,384]{3,2,1,0:T(8,128)(2,1)}, u32[]{:S(2)}, u32[]{:S(2)}) collective-permute-start(bf16[3,2,128,384]{3,2,1,0:T(8,128)(2,1)} %get-tuple-element.34), channel_id=1, source_target_pairs={{0,32},{8,40},{16,48},{24,56},{32,64},{40,72},{48,80},{56,88},{64,... | collective-permute-start | bytes 1769480 | tf_op jit(solution)/shard_map/ppermute | solution.py:26
  26.8 3.3 %prepare.1 = (bf16[4,3,128,384]{3,2,1,0:T(8,128)(2,1)}, f32[2,128,384]{2,1,0:T(8,128)S(1)}, f32[328,128]{1,0:T(8,128)S(1)}) custom-call(s32[2]{0:T(128)S(1)} %pad_add_fusion.where, s32[5]{0:T(128)S(1)} %copy-done.5, s32[5]{0:T(128)S(1)} %copy-done.7, f32[5]{0:T(128)S(1)} %copy-done.8, f32[5]{0:T(128)S(1)} %copy-done.9, bf16[1,128,1536]{2,1,0:T(8,128)(2,1)S(1)} %copy-done.2, ...), custom_call_target="tpu_custom_call" | custom-call | tf_op jit(solution)/shard_map/prepare/pallas_call | solution.py:221
  30.1 0.8 copy-done.1
  30.9 3.5 %all-to-all-start.2 = ((bf16[4,3,128,384]{3,2,1,0:T(8,128)(2,1)}), bf16[4,3,128,384]{3,2,1,0:T(8,128)(2,1)S(1)}, u32[]{:S(2)}, u32[]{:S(2)}) async-start(bf16[4,3,128,384]{3,2,1,0:T(8,128)(2,1)} %get-tuple-element.22), calls=%async_computation.2 | async-start | bytes 2359296 | tf_op jit(solution)/shard_map/all_to_all | solution.py:58
  34.5 1.3 %collective-permute-start.5 = (bf16[3,2,128,384]{3,2,1,0:T(8,128)(2,1)}, bf16[3,2,128,384]{3,2,1,0:T(8,128)(2,1)S(1)}, u32[]{:S(2)}, u32[]{:S(2)}) collective-permute-start(bf16[3,2,128,384]{3,2,1,0:T(8,128)(2,1)} %collective-permute-done.3.near_r), channel_id=1, source_target_pairs={{32,0},{40,8},{48,16},{56,24},{64,32},{72,40},{80,48},{88,56},{96,... | collective-permute-start | bytes 1769480 | tf_op jit(solution)/shard_map/ppermute | solution.py:26
  35.8 6.0 %collective-permute-start.1 = (bf16[3,2,128,384]{3,2,1,0:T(8,128)(2,1)}, bf16[3,2,128,384]{3,2,1,0:T(8,128)(2,1)S(1)}, u32[]{:S(2)}, u32[]{:S(2)}) collective-permute-start(bf16[3,2,128,384]{3,2,1,0:T(8,128)(2,1)} %collective-permute-done.near_l), channel_id=1, source_target_pairs={{0,32},{8,40},{16,48},{24,56},{32,64},{40,72},{48,80},{56,88},{64,... | collective-permute-start | bytes 1769480 | tf_op jit(solution)/shard_map/ppermute | solution.py:26
  42.0 1.3 %collective-permute-start.4 = (bf16[1,2,128,384]{3,2,1,0:T(8,128)(2,1)S(1)}, bf16[1,2,128,384]{3,2,1,0:T(8,128)(2,1)S(1)}, u32[]{:S(2)}, u32[]{:S(2)}) collective-permute-start(bf16[1,2,128,384]{3,2,1,0:T(8,128)(2,1)S(1)} %get-tuple-element.31), channel_id=1, source_target_pairs={{32,0},{40,8},{48,16},{56,24},{64,32},{72,40},{80,48},{88,56},{96,... | collective-permute-start | bytes 589832 | tf_op jit(solution)/shard_map/ppermute | solution.py:26
  43.3 4.6 %collective-permute-start.2 = (bf16[1,2,128,384]{3,2,1,0:T(8,128)(2,1)S(1)}, bf16[1,2,128,384]{3,2,1,0:T(8,128)(2,1)S(1)}, u32[]{:S(2)}, u32[]{:S(2)}) collective-permute-start(bf16[1,2,128,384]{3,2,1,0:T(8,128)(2,1)S(1)} %get-tuple-element.32), channel_id=1, source_target_pairs={{0,32},{8,40},{16,48},{24,56},{32,64},{40,72},{48,80},{56,88},{64,... | collective-permute-start | bytes 589832 | tf_op jit(solution)/shard_map/ppermute | solution.py:26
  47.9 2.0 %broadcast_in_dim.3 = bf16[8,48,1536]{2,1,0:T(8,128)(2,1)} broadcast(bf16[48,1536]{1,0:T(8,128)(2,1)} %bitcast.13), dimensions={1,2} | broadcast | bytes 1327104 | tf_op jit(solution)/shard_map/broadcast_in_dim | solution.py:386
  49.9 5.5 %collective-permute-done.4.one_r = bf16[1,2,128,384]{3,2,1,0:T(8,128)(2,1)S(1)} collective-permute-done((bf16[1,2,128,384]{3,2,1,0:T(8,128)(2,1)S(1)}, bf16[1,2,128,384]{3,2,1,0:T(8,128)(2,1)S(1)}, u32[]{:S(2)}, u32[]{:S(2)}) %collective-permute-start.4) | collective-permute-done | bytes 196640 | tf_op jit(solution)/shard_map/ppermute | solution.py:26
  55.5 0.9 collective-permute-done.2.one_l
  56.4 0.8 copy-done.21
  57.9 11.6 %all-to-all-start.1 = ((bf16[8,48,1536]{2,1,0:T(8,128)(2,1)}), bf16[8,48,1536]{2,1,0:T(8,128)(2,1)S(1)}, u32[]{:S(2)}, u32[]{:S(2)}) async-start(bf16[8,48,1536]{2,1,0:T(8,128)(2,1)} %broadcast_in_dim.3), calls=%async_computation.1 | async-start | bytes 2359296 | tf_op jit(solution)/shard_map/all_to_all | solution.py:64
  69.5 7.6 %attend.1.own = bf16[4,128,384]{2,1,0:T(8,128)(2,1)} custom-call(s32[2]{0:T(128)} %copy-done.6, s32[5]{0:T(128)} %spans.5, s32[2,5]{1,0:T(2,128)} %text_len.1, bf16[4,3,128,384]{3,2,1,0:T(8,128)(2,1)} %copy-done.11, bf16[3,2,128,384]{3,2,1,0:T(8,128)(2,1)} %copy-done.15, bf16[1,2,128,384]{3,2,1,0:T(8,128)(2,1)} %copy-done.21, ...), custom_call_target="tpu_custom_call" | custom-call | flops 805306368 | bytes 8388608 | tf_op jit(solution)/shard_map/attend/pallas_call | solution.py:154
  77.1 2.8 %collective-permute-start.8 = (bf16[4,128,384]{2,1,0:T(8,128)(2,1)}, bf16[4,128,384]{2,1,0:T(8,128)(2,1)S(1)}, u32[]{:S(2)}, u32[]{:S(2)}) collective-permute-start(bf16[4,128,384]{2,1,0:T(8,128)(2,1)} %attend.1.own), channel_id=1, source_target_pairs={{0,24},{8,0},{16,8},{24,16},{32,56},{40,32},{48,40},{56,48},{64,88... | collective-permute-start | bytes 1179656 | tf_op jit(solution)/shard_map/ppermute | solution.py:41
  79.9 2.5 %collective-permute-start.7 = (bf16[4,128,384]{2,1,0:T(8,128)(2,1)}, bf16[4,128,384]{2,1,0:T(8,128)(2,1)S(1)}, u32[]{:S(2)}, u32[]{:S(2)}) collective-permute-start(bf16[4,128,384]{2,1,0:T(8,128)(2,1)} %attend.1.own), channel_id=1, source_target_pairs={{0,8},{8,16},{16,24},{24,0},{32,40},{40,48},{48,56},{56,32},{64,72... | collective-permute-start | bytes 1179656 | tf_op jit(solution)/shard_map/ppermute | solution.py:41
  82.4 1.1 fusion.2
  83.5 2.6 %collective-permute-start.10 = (bf16[2,128,384]{2,1,0:T(8,128)(2,1)S(1)}, bf16[2,128,384]{2,1,0:T(8,128)(2,1)S(1)}, u32[]{:S(2)}, u32[]{:S(2)}) collective-permute-start(bf16[2,128,384]{2,1,0:T(8,128)(2,1)S(1)} %get-tuple-element.35), channel_id=1, source_target_pairs={{0,16},{8,24},{16,0},{24,8},{32,48},{40,56},{48,32},{56,40},{64,80... | collective-permute-start | bytes 589832 | tf_op jit(solution)/shard_map/ppermute | solution.py:41
  86.1 4.2 %collective-permute-start.9 = (bf16[2,128,384]{2,1,0:T(8,128)(2,1)S(1)}, bf16[2,128,384]{2,1,0:T(8,128)(2,1)S(1)}, u32[]{:S(2)}, u32[]{:S(2)}) collective-permute-start(bf16[2,128,384]{2,1,0:T(8,128)(2,1)S(1)} %get-tuple-element.36), channel_id=1, source_target_pairs={{0,16},{8,24},{16,0},{24,8},{32,48},{40,56},{48,32},{56,40},{64,80... | collective-permute-start | bytes 589832 | tf_op jit(solution)/shard_map/ppermute | solution.py:41
  90.3 3.3 %collective-permute-done.10.far_b = bf16[2,128,384]{2,1,0:T(8,128)(2,1)S(1)} collective-permute-done((bf16[2,128,384]{2,1,0:T(8,128)(2,1)S(1)}, bf16[2,128,384]{2,1,0:T(8,128)(2,1)S(1)}, u32[]{:S(2)}, u32[]{:S(2)}) %collective-permute-start.10) | collective-permute-done | bytes 196640 | tf_op jit(solution)/shard_map/ppermute | solution.py:41
  93.6 4.4 %collective-permute-done.9.far_a = bf16[2,128,384]{2,1,0:T(8,128)(2,1)S(1)} collective-permute-done((bf16[2,128,384]{2,1,0:T(8,128)(2,1)S(1)}, bf16[2,128,384]{2,1,0:T(8,128)(2,1)S(1)}, u32[]{:S(2)}, u32[]{:S(2)}) %collective-permute-start.9) | collective-permute-done | bytes 196640 | tf_op jit(solution)/shard_map/ppermute | solution.py:41
  98.5 6.6 %collective-permute-start.11 = (bf16[384,1536]{1,0:T(8,128)(2,1)S(1)}, bf16[384,1536]{1,0:T(8,128)(2,1)S(1)}, u32[]{:S(2)}, u32[]{:S(2)}) collective-permute-start(bf16[384,1536]{1,0:T(8,128)(2,1)S(1)} %bitcast.11), channel_id=1, source_target_pairs={{0,256},{256,0},{1,257},{257,1},{2,258},{258,2},{3,259},{259,3},{4... | collective-permute-start | bytes 3538952 | tf_op jit(solution)/shard_map/ppermute | solution.py:19
  105.1 2.5 %collective-permute-done.11.w_other = bf16[384,1536]{1,0:T(8,128)(2,1)S(1)} collective-permute-done((bf16[384,1536]{1,0:T(8,128)(2,1)S(1)}, bf16[384,1536]{1,0:T(8,128)(2,1)S(1)}, u32[]{:S(2)}, u32[]{:S(2)}) %collective-permute-start.11) | collective-permute-done | bytes 1179680 | tf_op jit(solution)/shard_map/ppermute | solution.py:19
  107.6 1.0 copy-done.13
  108.6 6.0 %project.1 = f32[8,72,128]{2,1,0:T(8,128)} custom-call(s32[2]{0:T(128)} %copy-done.6, s32[5]{0:T(128)} %spans.5, bf16[4,128,384]{2,1,0:T(8,128)(2,1)} %attend.1.own, bf16[4,128,384]{2,1,0:T(8,128)(2,1)} %copy-done.17, bf16[4,128,384]{2,1,0:T(8,128)(2,1)} %copy-done.16, bf16[2,128,384]{2,1,0:T(8,128)(2,1)} %copy-done.20, bf16[2,128,384]{2,1,0:T(8,128)(2,1)} %copy-done.18, ...), custom_call_target="tpu_custom_call" | custom-call | flops 1207959552 | bytes 8388608 | tf_op jit(solution)/shard_map/project/pallas_call | solution.py:290
  114.6 11.1 %all_to_all.20.parts = f32[8,72,128]{2,1,0:T(8,128)S(1)} all-to-all(f32[8,72,128]{2,1,0:T(8,128)} %project.1), channel_id=1, replica_groups={{0,8,16,24,256,264,272,280},{32,40,48,56,288,296,304,312},{64,72,80,88,..., dimensions={0} | all-to-all | bytes 589824 | tf_op jit(solution)/shard_map/all_to_all | solution.py:35
  125.7 0.7 finish.1
  (57 shorter events, 2.1 us)
Async XLA Ops:
  2.2 5.0 %copy-start = (bf16[2,128,1536]{2,1,0:T(8,128)(2,1)S(1)}, bf16[2,128,1536]{2,1,0:T(8,128)(2,1)}, u32[]{:S(2)}) copy-start(bf16[2,128,1536]{2,1,0:T(8,128)(2,1)} %hidden.1) | copy-start | bytes 2359300
  2.2 13.3 %all-to-all-start = ((bf16[4,2,128,384]{3,2,1,0:T(8,128)(2,1)}), bf16[4,2,128,384]{3,2,1,0:T(8,128)(2,1)S(1)}, u32[]{:S(2)}, u32[]{:S(2)}) async-start(bf16[4,2,128,384]{3,2,1,0:T(8,128)(2,1)} %pack.1), calls=%async_computation | async-start | bytes 1572864 | tf_op jit(solution)/shard_map/all_to_all | solution.py:58
  7.2 19.5 %copy-start.22 = (bf16[2,5,3072]{2,0,1:T(2,128)(2,1)S(1)}, bf16[2,5,3072]{2,0,1:T(2,128)(2,1)}, u32[]{:S(2)}) copy-start(bf16[2,5,3072]{2,0,1:T(2,128)(2,1)} %param.19) | copy-start | bytes 184324
  7.2 19.5 %copy-start.2 = (bf16[1,128,1536]{2,1,0:T(8,128)(2,1)S(1)}, bf16[1,128,1536]{2,1,0:T(8,128)(2,1)}, u32[]{:S(2)}) copy-start(bf16[1,128,1536]{2,1,0:T(8,128)(2,1)} %queries) | copy-start | bytes 1179652
  7.2 19.5 %copy-start.3 = (bf16[3072,64]{0,1:T(8,128)(2,1)S(1)}, bf16[3072,64]{0,1:T(8,128)(2,1)}, u32[]{:S(2)}) copy-start(bf16[3072,64]{0,1:T(8,128)(2,1)} %param.18) | copy-start | bytes 1179652
  7.3 19.5 %copy-start.4 = (f32[128,64]{0,1:T(8,128)S(1)}, f32[128,64]{0,1:T(8,128)}, u32[]{:S(2)}) copy-start(f32[128,64]{0,1:T(8,128)} %param.25) | copy-start | bytes 98308
  7.3 19.5 %copy-start.5 = (s32[5]{0:T(128)S(1)}, s32[5]{0:T(128)}, u32[]{:S(2)}) copy-start(s32[5]{0:T(128)} %spans.5) | copy-start | bytes 64
  7.3 19.5 %copy-start.7 = (s32[5]{0:T(128)S(1)}, s32[5]{0:T(128)}, u32[]{:S(2)}) copy-start(s32[5]{0:T(128)} %on.1) | copy-start | bytes 64
  7.3 19.5 %copy-start.8 = (f32[5]{0:T(128)S(1)}, f32[5]{0:T(128)}, u32[]{:S(2)}) copy-start(f32[5]{0:T(128)} %scales.1) | copy-start | bytes 64
  7.3 19.5 %copy-start.9 = (f32[5]{0:T(128)S(1)}, f32[5]{0:T(128)}, u32[]{:S(2)}) copy-start(f32[5]{0:T(128)} %strides.1) | copy-start | bytes 64
  7.3 19.4 %collective-permute-start.6 = (bf16[128,1536]{1,0:T(8,128)(2,1)S(1)}, bf16[128,1536]{1,0:T(8,128)(2,1)S(1)}, u32[]{:S(2)}, u32[]{:S(2)}) collective-permute-start(bf16[128,1536]{1,0:T(8,128)(2,1)S(1)} %dynamic-slice_bitcast_fusion), channel_id=1, source_target_pairs={{0,256},{256,0},{1,257},{257,1},{2,258},{258,2},{3,259},{259,3},{4... | collective-permute-start | bytes 1179656 | tf_op jit(solution)/shard_map/ppermute | solution.py:19
  15.5 26.4 %copy-start.10 = (bf16[4,2,128,384]{3,2,1,0:T(8,128)(2,1)}, bf16[4,2,128,384]{3,2,1,0:T(8,128)(2,1)S(1)}, u32[]{:S(2)}) copy-start(bf16[4,2,128,384]{3,2,1,0:T(8,128)(2,1)S(1)} %all-to-all-done.own) | copy-start | bytes 2359300
  16.8 17.7 %collective-permute-start.3 = (bf16[3,2,128,384]{3,2,1,0:T(8,128)(2,1)}, bf16[3,2,128,384]{3,2,1,0:T(8,128)(2,1)}, u32[]{:S(2)}, u32[]{:S(2)}) collective-permute-start(bf16[3,2,128,384]{3,2,1,0:T(8,128)(2,1)} %get-tuple-element.33), channel_id=1, source_target_pairs={{32,0},{40,8},{48,16},{56,24},{64,32},{72,40},{80,48},{88,56},{96,... | collective-permute-start | bytes 1769480 | tf_op jit(solution)/shard_map/ppermute | solution.py:26
  18.1 17.7 %collective-permute-start = (bf16[3,2,128,384]{3,2,1,0:T(8,128)(2,1)}, bf16[3,2,128,384]{3,2,1,0:T(8,128)(2,1)}, u32[]{:S(2)}, u32[]{:S(2)}) collective-permute-start(bf16[3,2,128,384]{3,2,1,0:T(8,128)(2,1)} %get-tuple-element.34), channel_id=1, source_target_pairs={{0,32},{8,40},{16,48},{24,56},{32,64},{40,72},{48,80},{56,88},{64,... | collective-permute-start | bytes 1769480 | tf_op jit(solution)/shard_map/ppermute | solution.py:26
  26.7 4.2 %copy-start.6 = (s32[2]{0:T(128)}, s32[2]{0:T(128)S(1)}, u32[]{:S(2)}) copy-start(s32[2]{0:T(128)S(1)} %pad_add_fusion.where) | copy-start | bytes 28
  30.9 25.5 %all-to-all-start.2 = ((bf16[4,3,128,384]{3,2,1,0:T(8,128)(2,1)}), bf16[4,3,128,384]{3,2,1,0:T(8,128)(2,1)S(1)}, u32[]{:S(2)}, u32[]{:S(2)}) async-start(bf16[4,3,128,384]{3,2,1,0:T(8,128)(2,1)} %get-tuple-element.22), calls=%async_computation.2 | async-start | bytes 2359296 | tf_op jit(solution)/shard_map/all_to_all | solution.py:58
  34.5 21.8 %collective-permute-start.5 = (bf16[3,2,128,384]{3,2,1,0:T(8,128)(2,1)}, bf16[3,2,128,384]{3,2,1,0:T(8,128)(2,1)S(1)}, u32[]{:S(2)}, u32[]{:S(2)}) collective-permute-start(bf16[3,2,128,384]{3,2,1,0:T(8,128)(2,1)} %collective-permute-done.3.near_r), channel_id=1, source_target_pairs={{32,0},{40,8},{48,16},{56,24},{64,32},{72,40},{80,48},{88,56},{96,... | collective-permute-start | bytes 1769480 | tf_op jit(solution)/shard_map/ppermute | solution.py:26
  35.8 20.6 %collective-permute-start.1 = (bf16[3,2,128,384]{3,2,1,0:T(8,128)(2,1)}, bf16[3,2,128,384]{3,2,1,0:T(8,128)(2,1)S(1)}, u32[]{:S(2)}, u32[]{:S(2)}) collective-permute-start(bf16[3,2,128,384]{3,2,1,0:T(8,128)(2,1)} %collective-permute-done.near_l), channel_id=1, source_target_pairs={{0,32},{8,40},{16,48},{24,56},{32,64},{40,72},{48,80},{56,88},{64,... | collective-permute-start | bytes 1769480 | tf_op jit(solution)/shard_map/ppermute | solution.py:26
  42.0 13.5 %collective-permute-start.4 = (bf16[1,2,128,384]{3,2,1,0:T(8,128)(2,1)S(1)}, bf16[1,2,128,384]{3,2,1,0:T(8,128)(2,1)S(1)}, u32[]{:S(2)}, u32[]{:S(2)}) collective-permute-start(bf16[1,2,128,384]{3,2,1,0:T(8,128)(2,1)S(1)} %get-tuple-element.31), channel_id=1, source_target_pairs={{32,0},{40,8},{48,16},{56,24},{64,32},{72,40},{80,48},{88,56},{96,... | collective-permute-start | bytes 589832 | tf_op jit(solution)/shard_map/ppermute | solution.py:26
  43.3 13.1 %collective-permute-start.2 = (bf16[1,2,128,384]{3,2,1,0:T(8,128)(2,1)S(1)}, bf16[1,2,128,384]{3,2,1,0:T(8,128)(2,1)S(1)}, u32[]{:S(2)}, u32[]{:S(2)}) collective-permute-start(bf16[1,2,128,384]{3,2,1,0:T(8,128)(2,1)S(1)} %get-tuple-element.32), channel_id=1, source_target_pairs={{0,32},{8,40},{16,48},{24,56},{32,64},{40,72},{48,80},{56,88},{64,... | collective-permute-start | bytes 589832 | tf_op jit(solution)/shard_map/ppermute | solution.py:26
  55.5 14.0 %copy-start.19 = (bf16[1,2,128,384]{3,2,1,0:T(8,128)(2,1)}, bf16[1,2,128,384]{3,2,1,0:T(8,128)(2,1)S(1)}, u32[]{:S(2)}) copy-start(bf16[1,2,128,384]{3,2,1,0:T(8,128)(2,1)S(1)} %collective-permute-done.4.one_r) | copy-start | bytes 589828
  57.9 40.6 %all-to-all-start.1 = ((bf16[8,48,1536]{2,1,0:T(8,128)(2,1)}), bf16[8,48,1536]{2,1,0:T(8,128)(2,1)S(1)}, u32[]{:S(2)}, u32[]{:S(2)}) async-start(bf16[8,48,1536]{2,1,0:T(8,128)(2,1)} %broadcast_in_dim.3), calls=%async_computation.1 | async-start | bytes 2359296 | tf_op jit(solution)/shard_map/all_to_all | solution.py:64
  77.1 20.8 %collective-permute-start.8 = (bf16[4,128,384]{2,1,0:T(8,128)(2,1)}, bf16[4,128,384]{2,1,0:T(8,128)(2,1)S(1)}, u32[]{:S(2)}, u32[]{:S(2)}) collective-permute-start(bf16[4,128,384]{2,1,0:T(8,128)(2,1)} %attend.1.own), channel_id=1, source_target_pairs={{0,24},{8,0},{16,8},{24,16},{32,56},{40,32},{48,40},{56,48},{64,88... | collective-permute-start | bytes 1179656 | tf_op jit(solution)/shard_map/ppermute | solution.py:41
  79.9 18.0 %collective-permute-start.7 = (bf16[4,128,384]{2,1,0:T(8,128)(2,1)}, bf16[4,128,384]{2,1,0:T(8,128)(2,1)S(1)}, u32[]{:S(2)}, u32[]{:S(2)}) collective-permute-start(bf16[4,128,384]{2,1,0:T(8,128)(2,1)} %attend.1.own), channel_id=1, source_target_pairs={{0,8},{8,16},{16,24},{24,0},{32,40},{40,48},{48,56},{56,32},{64,72... | collective-permute-start | bytes 1179656 | tf_op jit(solution)/shard_map/ppermute | solution.py:41
  83.5 10.1 %collective-permute-start.10 = (bf16[2,128,384]{2,1,0:T(8,128)(2,1)S(1)}, bf16[2,128,384]{2,1,0:T(8,128)(2,1)S(1)}, u32[]{:S(2)}, u32[]{:S(2)}) collective-permute-start(bf16[2,128,384]{2,1,0:T(8,128)(2,1)S(1)} %get-tuple-element.35), channel_id=1, source_target_pairs={{0,16},{8,24},{16,0},{24,8},{32,48},{40,56},{48,32},{56,40},{64,80... | collective-permute-start | bytes 589832 | tf_op jit(solution)/shard_map/ppermute | solution.py:41
  86.1 11.8 %collective-permute-start.9 = (bf16[2,128,384]{2,1,0:T(8,128)(2,1)S(1)}, bf16[2,128,384]{2,1,0:T(8,128)(2,1)S(1)}, u32[]{:S(2)}, u32[]{:S(2)}) collective-permute-start(bf16[2,128,384]{2,1,0:T(8,128)(2,1)S(1)} %get-tuple-element.36), channel_id=1, source_target_pairs={{0,16},{8,24},{16,0},{24,8},{32,48},{40,56},{48,32},{56,40},{64,80... | collective-permute-start | bytes 589832 | tf_op jit(solution)/shard_map/ppermute | solution.py:41
  93.6 14.0 %copy-start.18 = (bf16[2,128,384]{2,1,0:T(8,128)(2,1)}, bf16[2,128,384]{2,1,0:T(8,128)(2,1)S(1)}, u32[]{:S(2)}) copy-start(bf16[2,128,384]{2,1,0:T(8,128)(2,1)S(1)} %collective-permute-done.10.far_b) | copy-start | bytes 589828
  97.9 9.6 %copy-start.20 = (bf16[2,128,384]{2,1,0:T(8,128)(2,1)}, bf16[2,128,384]{2,1,0:T(8,128)(2,1)S(1)}, u32[]{:S(2)}) copy-start(bf16[2,128,384]{2,1,0:T(8,128)(2,1)S(1)} %collective-permute-done.9.far_a) | copy-start | bytes 589828
  97.9 9.6 %copy-start.16 = (bf16[4,128,384]{2,1,0:T(8,128)(2,1)}, bf16[4,128,384]{2,1,0:T(8,128)(2,1)S(1)}, u32[]{:S(2)}) copy-start(bf16[4,128,384]{2,1,0:T(8,128)(2,1)S(1)} %collective-permute-done.8.ahead) | copy-start | bytes 1179652
  97.9 9.6 %copy-start.17 = (bf16[4,128,384]{2,1,0:T(8,128)(2,1)}, bf16[4,128,384]{2,1,0:T(8,128)(2,1)S(1)}, u32[]{:S(2)}) copy-start(bf16[4,128,384]{2,1,0:T(8,128)(2,1)S(1)} %collective-permute-done.7.behind) | copy-start | bytes 1179652
  98.5 9.1 %copy-start.12 = (bf16[8,48,1536]{2,1,0:T(8,128)(2,1)}, bf16[8,48,1536]{2,1,0:T(8,128)(2,1)S(1)}, u32[]{:S(2)}) copy-start(bf16[8,48,1536]{2,1,0:T(8,128)(2,1)S(1)} %all-to-all-done.1) | copy-start | bytes 3538948
  98.5 9.1 %collective-permute-start.11 = (bf16[384,1536]{1,0:T(8,128)(2,1)S(1)}, bf16[384,1536]{1,0:T(8,128)(2,1)S(1)}, u32[]{:S(2)}, u32[]{:S(2)}) collective-permute-start(bf16[384,1536]{1,0:T(8,128)(2,1)S(1)} %bitcast.11), channel_id=1, source_target_pairs={{0,256},{256,0},{1,257},{257,1},{2,258},{258,2},{3,259},{259,3},{4... | collective-permute-start | bytes 3538952 | tf_op jit(solution)/shard_map/ppermute | solution.py:19
  (6 other events, 6.1 us)

commit v6 on v5

--- a/solution.py
+++ b/solution.py
@@ -109,17 +109,24 @@
 
 
 def attend_kernel(
-    where, spans, text_len, q_ref, far_l, one_l, near_l, own, near_r, one_r, far_r, o_ref, k_all, v_all
+    where, spans, text_len, q_ref, far_l, one_l, near_l, own, near_r, one_r, far_r, o_ref,
+    k_all, v_all, q_all, arrived,
 ):
     place, half = where[0], where[1]
     first = (place // ROW) * ROW
     heads = q_ref.shape[3] // HEAD_WIDTH
-    at = 0
+    copies, at = [], 0
     for ref in (far_l, one_l, near_l, own, near_r, one_r, far_r):
         for i in range(ref.shape[0]):
-            k_all[at * TILE : (at + 1) * TILE, :] = ref[i, 0]
-            v_all[at * TILE : (at + 1) * TILE, :] = ref[i, 1]
+            for j, whole in enumerate((k_all, v_all)):
+                copies.append((ref.at[i, j], whole.at[pl.ds(at * TILE, TILE)]))
             at += 1
+    copies += [(q_ref.at[i, 0], q_all.at[i]) for i in range(ROW)]
+    copies = [pltpu.make_async_copy(*pair, arrived.at[n]) for n, pair in enumerate(copies)]
+    for copy in copies:
+        copy.start()
+    for copy in copies:
+        copy.wait()
     keys = SPAN_MOST * TILE
     column = lax.broadcasted_iota(jnp.int32, (1, keys), 1)
     factor = HEAD_WIDTH**-0.5 * LOG2E
@@ -134,7 +141,7 @@
             key = k_all[pl.ds(begin, keys), lanes]
             value = v_all[pl.ds(begin, keys), lanes]
             score = lax.dot_general(
-                q_ref[t, 0, :, lanes], key, NT, preferred_element_type=jnp.float32
+                q_all[t, :, lanes], key, NT, preferred_element_type=jnp.float32
             )
             score = score + bias
             top = jnp.max(score, axis=-1, keepdims=True)
@@ -154,11 +161,13 @@
     return pl.pallas_call(
         attend_kernel,
         out_shape=jax.ShapeDtypeStruct((ROW, TILE, width), jnp.bfloat16),
-        in_specs=[smem] * 3 + [vmem] * 8,
+        in_specs=[smem] * 3 + [pl.BlockSpec(memory_space=pl.ANY)] * 8,
         out_specs=vmem,
         scratch_shapes=[
             pltpu.VMEM((rows, width), jnp.bfloat16),
             pltpu.VMEM((rows, width), jnp.bfloat16),
+            pltpu.VMEM((ROW, TILE, width), jnp.bfloat16),
+            pltpu.SemaphoreType.DMA((2 * rows // TILE + ROW,)),
         ],
         compiler_params=pltpu.CompilerParams(vmem_limit_bytes=58 << 20),
         cost_estimate=pl.CostEstimate(

time: 127 us -> 128 us (level)
  transfers between devices with their start and end apart: 15 -> 15, of which waited for: 8 -> 7; matrix products, arithmetic and copies ran while one was open for 4% -> 4% of each run, Pallas kernels for 9% -> 9%
where the time goes in v6:
time: 128 us; the launch traced here: 127 us
  starting transfers between devices  69.9 us (55%)
  Pallas kernels  20.6 us (16%)
  waiting for transfers between devices  17.3 us (14%)
  blocking collectives  11.1 us (9%)
  local copies, waits for them, and re-layouts  7.77 us (6%)
    ppermute x6, starting transfers between devices, along_z(): return lax.ppermute(value, 'seq', pairs)  23 us
    ppermute x2, starting transfers between devices, swapped(): return lax.ppermute(value, 'guide', [(0, 1), (1, 0)])  14.7 us
    ppermute x4, starting transfers between devices, along_x(): return lax.ppermute(value, 'seq', pairs)  12.1 us
    all_to_all x1, starting transfers between devices, gather_weight(): lax.all_to_all(copies, 'seq', 0, 0, axis_index_groups=columns)  11.6 us
    all_to_all x1, blocking collectives, spread_wide(): lax.all_to_all(value, ('guide', 'seq'), 0, 0, axis_index_groups=groups)  11.1 us
    all_to_all x2, starting transfers between devices, spread(): return lax.all_to_all(value, 'seq', 0, 0, axis_index_groups=groups)  8.51 us
    pallas_call x1, Pallas kernels, attend(): pl.pallas_call(attend_kernel, out_shape=jax.ShapeDtypeStruct((ROW, TILE,...  8.34 us
    ppermute x4, waiting for transfers between devices, along_x(): return lax.ppermute(value, 'seq', pairs)  7.65 us
  transfers between devices with their start and end apart: 15, of which 7 were waited for; matrix products, arithmetic and copies ran while one was open for 4% of the time, Pallas kernels for 9%

profile of v6, /device:TPU:1, one launch (start us, length us, event | category | flops | bytes accessed | tf_op | source)
XLA Modules:
  0.0 127.1 jit_solution(15766430394558168246)
XLA Ops:
  0.0 2.2 %pack.1 = bf16[4,2,128,384]{3,2,1,0:T(8,128)(2,1)} custom-call(bf16[1,128,1536]{2,1,0:T(8,128)(2,1)} %k_ref.1, bf16[1,128,1536]{2,1,0:T(8,128)(2,1)} %v_ref.1), custom_call_target="tpu_custom_call" | custom-call | tf_op jit(solution)/shard_map/pack/pallas_call | solution.py:88
  2.2 5.0 %all-to-all-start = ((bf16[4,2,128,384]{3,2,1,0:T(8,128)(2,1)}), bf16[4,2,128,384]{3,2,1,0:T(8,128)(2,1)S(1)}, u32[]{:S(2)}, u32[]{:S(2)}) async-start(bf16[4,2,128,384]{3,2,1,0:T(8,128)(2,1)} %pack.1), calls=%async_computation | async-start | bytes 1572864 | tf_op jit(solution)/shard_map/all_to_all | solution.py:58
  7.3 7.6 %collective-permute-start.6 = (bf16[128,1536]{1,0:T(8,128)(2,1)S(1)}, bf16[128,1536]{1,0:T(8,128)(2,1)S(1)}, u32[]{:S(2)}, u32[]{:S(2)}) collective-permute-start(bf16[128,1536]{1,0:T(8,128)(2,1)S(1)} %dynamic-slice_bitcast_fusion), channel_id=1, source_target_pairs={{0,256},{256,0},{1,257},{257,1},{2,258},{258,2},{3,259},{259,3},{4... | collective-permute-start | bytes 1179656 | tf_op jit(solution)/shard_map/ppermute | solution.py:19
  15.5 1.3 %fusion.1 = (bf16[3,2,128,384]{3,2,1,0:T(8,128)(2,1)}, bf16[3,2,128,384]{3,2,1,0:T(8,128)(2,1)}) fusion(bf16[4,2,128,384]{3,2,1,0:T(8,128)(2,1)S(1)} %all-to-all-done.own), kind=kLoop, calls=%fused_computation.3 | loop fusion | bytes 2359296 | tf_op jit(solution)/shard_map/slice | solution.py:375
  16.8 1.3 %collective-permute-start.3 = (bf16[3,2,128,384]{3,2,1,0:T(8,128)(2,1)}, bf16[3,2,128,384]{3,2,1,0:T(8,128)(2,1)}, u32[]{:S(2)}, u32[]{:S(2)}) collective-permute-start(bf16[3,2,128,384]{3,2,1,0:T(8,128)(2,1)} %get-tuple-element.33), channel_id=1, source_target_pairs={{32,0},{40,8},{48,16},{56,24},{64,32},{72,40},{80,48},{88,56},{96,... | collective-permute-start | bytes 1769480 | tf_op jit(solution)/shard_map/ppermute | solution.py:26
  18.1 8.5 %collective-permute-start = (bf16[3,2,128,384]{3,2,1,0:T(8,128)(2,1)}, bf16[3,2,128,384]{3,2,1,0:T(8,128)(2,1)}, u32[]{:S(2)}, u32[]{:S(2)}) collective-permute-start(bf16[3,2,128,384]{3,2,1,0:T(8,128)(2,1)} %get-tuple-element.34), channel_id=1, source_target_pairs={{0,32},{8,40},{16,48},{24,56},{32,64},{40,72},{48,80},{56,88},{64,... | collective-permute-start | bytes 1769480 | tf_op jit(solution)/shard_map/ppermute | solution.py:26
  26.8 3.3 %prepare.1 = (bf16[4,3,128,384]{3,2,1,0:T(8,128)(2,1)}, f32[2,128,384]{2,1,0:T(8,128)S(1)}, f32[328,128]{1,0:T(8,128)S(1)}) custom-call(s32[2]{0:T(128)S(1)} %pad_add_fusion.where, s32[5]{0:T(128)S(1)} %copy-done.5, s32[5]{0:T(128)S(1)} %copy-done.7, f32[5]{0:T(128)S(1)} %copy-done.8, f32[5]{0:T(128)S(1)} %copy-done.9, bf16[1,128,1536]{2,1,0:T(8,128)(2,1)S(1)} %copy-done.2, ...), custom_call_target="tpu_custom_call" | custom-call | tf_op jit(solution)/shard_map/prepare/pallas_call | solution.py:230
  30.1 0.8 copy-done.1
  30.9 3.5 %all-to-all-start.2 = ((bf16[4,3,128,384]{3,2,1,0:T(8,128)(2,1)}), bf16[4,3,128,384]{3,2,1,0:T(8,128)(2,1)S(1)}, u32[]{:S(2)}, u32[]{:S(2)}) async-start(bf16[4,3,128,384]{3,2,1,0:T(8,128)(2,1)} %get-tuple-element.22), calls=%async_computation.2 | async-start | bytes 2359296 | tf_op jit(solution)/shard_map/all_to_all | solution.py:58
  34.5 1.3 %collective-permute-start.5 = (bf16[3,2,128,384]{3,2,1,0:T(8,128)(2,1)}, bf16[3,2,128,384]{3,2,1,0:T(8,128)(2,1)S(1)}, u32[]{:S(2)}, u32[]{:S(2)}) collective-permute-start(bf16[3,2,128,384]{3,2,1,0:T(8,128)(2,1)} %collective-permute-done.3.near_r), channel_id=1, source_target_pairs={{32,0},{40,8},{48,16},{56,24},{64,32},{72,40},{80,48},{88,56},{96,... | collective-permute-start | bytes 1769480 | tf_op jit(solution)/shard_map/ppermute | solution.py:26
  35.8 6.0 %collective-permute-start.1 = (bf16[3,2,128,384]{3,2,1,0:T(8,128)(2,1)}, bf16[3,2,128,384]{3,2,1,0:T(8,128)(2,1)S(1)}, u32[]{:S(2)}, u32[]{:S(2)}) collective-permute-start(bf16[3,2,128,384]{3,2,1,0:T(8,128)(2,1)} %collective-permute-done.near_l), channel_id=1, source_target_pairs={{0,32},{8,40},{16,48},{24,56},{32,64},{40,72},{48,80},{56,88},{64,... | collective-permute-start | bytes 1769480 | tf_op jit(solution)/shard_map/ppermute | solution.py:26
  42.0 1.3 %collective-permute-start.4 = (bf16[1,2,128,384]{3,2,1,0:T(8,128)(2,1)S(1)}, bf16[1,2,128,384]{3,2,1,0:T(8,128)(2,1)S(1)}, u32[]{:S(2)}, u32[]{:S(2)}) collective-permute-start(bf16[1,2,128,384]{3,2,1,0:T(8,128)(2,1)S(1)} %get-tuple-element.31), channel_id=1, source_target_pairs={{32,0},{40,8},{48,16},{56,24},{64,32},{72,40},{80,48},{88,56},{96,... | collective-permute-start | bytes 589832 | tf_op jit(solution)/shard_map/ppermute | solution.py:26
  43.3 4.6 %collective-permute-start.2 = (bf16[1,2,128,384]{3,2,1,0:T(8,128)(2,1)S(1)}, bf16[1,2,128,384]{3,2,1,0:T(8,128)(2,1)S(1)}, u32[]{:S(2)}, u32[]{:S(2)}) collective-permute-start(bf16[1,2,128,384]{3,2,1,0:T(8,128)(2,1)S(1)} %get-tuple-element.32), channel_id=1, source_target_pairs={{0,32},{8,40},{16,48},{24,56},{32,64},{40,72},{48,80},{56,88},{64,... | collective-permute-start | bytes 589832 | tf_op jit(solution)/shard_map/ppermute | solution.py:26
  47.9 2.0 %broadcast_in_dim.3 = bf16[8,48,1536]{2,1,0:T(8,128)(2,1)} broadcast(bf16[48,1536]{1,0:T(8,128)(2,1)} %bitcast.13), dimensions={1,2} | broadcast | bytes 1327104 | tf_op jit(solution)/shard_map/broadcast_in_dim | solution.py:395
  49.9 5.5 %collective-permute-done.4.one_r = bf16[1,2,128,384]{3,2,1,0:T(8,128)(2,1)S(1)} collective-permute-done((bf16[1,2,128,384]{3,2,1,0:T(8,128)(2,1)S(1)}, bf16[1,2,128,384]{3,2,1,0:T(8,128)(2,1)S(1)}, u32[]{:S(2)}, u32[]{:S(2)}) %collective-permute-start.4) | collective-permute-done | bytes 196640 | tf_op jit(solution)/shard_map/ppermute | solution.py:26
  55.5 0.9 collective-permute-done.2.one_l
  56.4 0.8 copy-done.21
  57.9 11.6 %all-to-all-start.1 = ((bf16[8,48,1536]{2,1,0:T(8,128)(2,1)}), bf16[8,48,1536]{2,1,0:T(8,128)(2,1)S(1)}, u32[]{:S(2)}, u32[]{:S(2)}) async-start(bf16[8,48,1536]{2,1,0:T(8,128)(2,1)} %broadcast_in_dim.3), calls=%async_computation.1 | async-start | bytes 2359296 | tf_op jit(solution)/shard_map/all_to_all | solution.py:64
  69.5 8.3 %attend.1.own = bf16[4,128,384]{2,1,0:T(8,128)(2,1)} custom-call(s32[2]{0:T(128)} %copy-done.6, s32[5]{0:T(128)} %spans.5, s32[2,5]{1,0:T(2,128)} %text_len.1, bf16[4,3,128,384]{3,2,1,0:T(8,128)(2,1)} %copy-done.11, bf16[3,2,128,384]{3,2,1,0:T(8,128)(2,1)} %copy-done.15, bf16[1,2,128,384]{3,2,1,0:T(8,128)(2,1)} %copy-done.21, ...), custom_call_target="tpu_custom_call" | custom-call | flops 805306368 | bytes 8388608 | tf_op jit(solution)/shard_map/attend/pallas_call | solution.py:161
  77.8 2.8 %collective-permute-start.8 = (bf16[4,128,384]{2,1,0:T(8,128)(2,1)}, bf16[4,128,384]{2,1,0:T(8,128)(2,1)S(1)}, u32[]{:S(2)}, u32[]{:S(2)}) collective-permute-start(bf16[4,128,384]{2,1,0:T(8,128)(2,1)} %attend.1.own), channel_id=1, source_target_pairs={{0,24},{8,0},{16,8},{24,16},{32,56},{40,32},{48,40},{56,48},{64,88... | collective-permute-start | bytes 1179656 | tf_op jit(solution)/shard_map/ppermute | solution.py:41
  80.6 2.5 %collective-permute-start.7 = (bf16[4,128,384]{2,1,0:T(8,128)(2,1)}, bf16[4,128,384]{2,1,0:T(8,128)(2,1)S(1)}, u32[]{:S(2)}, u32[]{:S(2)}) collective-permute-start(bf16[4,128,384]{2,1,0:T(8,128)(2,1)} %attend.1.own), channel_id=1, source_target_pairs={{0,8},{8,16},{16,24},{24,0},{32,40},{40,48},{48,56},{56,32},{64,72... | collective-permute-start | bytes 1179656 | tf_op jit(solution)/shard_map/ppermute | solution.py:41
  83.1 1.1 fusion.2
  84.2 2.6 %collective-permute-start.10 = (bf16[2,128,384]{2,1,0:T(8,128)(2,1)S(1)}, bf16[2,128,384]{2,1,0:T(8,128)(2,1)S(1)}, u32[]{:S(2)}, u32[]{:S(2)}) collective-permute-start(bf16[2,128,384]{2,1,0:T(8,128)(2,1)S(1)} %get-tuple-element.35), channel_id=1, source_target_pairs={{0,16},{8,24},{16,0},{24,8},{32,48},{40,56},{48,32},{56,40},{64,80... | collective-permute-start | bytes 589832 | tf_op jit(solution)/shard_map/ppermute | solution.py:41
  86.8 4.2 %collective-permute-start.9 = (bf16[2,128,384]{2,1,0:T(8,128)(2,1)S(1)}, bf16[2,128,384]{2,1,0:T(8,128)(2,1)S(1)}, u32[]{:S(2)}, u32[]{:S(2)}) collective-permute-start(bf16[2,128,384]{2,1,0:T(8,128)(2,1)S(1)} %get-tuple-element.36), channel_id=1, source_target_pairs={{0,16},{8,24},{16,0},{24,8},{32,48},{40,56},{48,32},{56,40},{64,80... | collective-permute-start | bytes 589832 | tf_op jit(solution)/shard_map/ppermute | solution.py:41
  91.0 3.1 %collective-permute-done.10.far_b = bf16[2,128,384]{2,1,0:T(8,128)(2,1)S(1)} collective-permute-done((bf16[2,128,384]{2,1,0:T(8,128)(2,1)S(1)}, bf16[2,128,384]{2,1,0:T(8,128)(2,1)S(1)}, u32[]{:S(2)}, u32[]{:S(2)}) %collective-permute-start.10) | collective-permute-done | bytes 196640 | tf_op jit(solution)/shard_map/ppermute | solution.py:41
  94.1 4.5 %collective-permute-done.9.far_a = bf16[2,128,384]{2,1,0:T(8,128)(2,1)S(1)} collective-permute-done((bf16[2,128,384]{2,1,0:T(8,128)(2,1)S(1)}, bf16[2,128,384]{2,1,0:T(8,128)(2,1)S(1)}, u32[]{:S(2)}, u32[]{:S(2)}) %collective-permute-start.9) | collective-permute-done | bytes 196640 | tf_op jit(solution)/shard_map/ppermute | solution.py:41
  98.7 7.1 %collective-permute-start.11 = (bf16[384,1536]{1,0:T(8,128)(2,1)S(1)}, bf16[384,1536]{1,0:T(8,128)(2,1)S(1)}, u32[]{:S(2)}, u32[]{:S(2)}) collective-permute-start(bf16[384,1536]{1,0:T(8,128)(2,1)S(1)} %bitcast.11), channel_id=1, source_target_pairs={{0,256},{256,0},{1,257},{257,1},{2,258},{258,2},{3,259},{259,3},{4... | collective-permute-start | bytes 3538952 | tf_op jit(solution)/shard_map/ppermute | solution.py:19
  105.8 2.5 %collective-permute-done.11.w_other = bf16[384,1536]{1,0:T(8,128)(2,1)S(1)} collective-permute-done((bf16[384,1536]{1,0:T(8,128)(2,1)S(1)}, bf16[384,1536]{1,0:T(8,128)(2,1)S(1)}, u32[]{:S(2)}, u32[]{:S(2)}) %collective-permute-start.11) | collective-permute-done | bytes 1179680 | tf_op jit(solution)/shard_map/ppermute | solution.py:19
  108.3 1.0 copy-done.13
  109.3 6.0 %project.1 = f32[8,72,128]{2,1,0:T(8,128)} custom-call(s32[2]{0:T(128)} %copy-done.6, s32[5]{0:T(128)} %spans.5, bf16[4,128,384]{2,1,0:T(8,128)(2,1)} %attend.1.own, bf16[4,128,384]{2,1,0:T(8,128)(2,1)} %copy-done.17, bf16[4,128,384]{2,1,0:T(8,128)(2,1)} %copy-done.16, bf16[2,128,384]{2,1,0:T(8,128)(2,1)} %copy-done.20, bf16[2,128,384]{2,1,0:T(8,128)(2,1)} %copy-done.18, ...), custom_call_target="tpu_custom_call" | custom-call | flops 1207959552 | bytes 8388608 | tf_op jit(solution)/shard_map/project/pallas_call | solution.py:299
  115.3 11.1 %all_to_all.20.parts = f32[8,72,128]{2,1,0:T(8,128)S(1)} all-to-all(f32[8,72,128]{2,1,0:T(8,128)} %project.1), channel_id=1, replica_groups={{0,8,16,24,256,264,272,280},{32,40,48,56,288,296,304,312},{64,72,80,88,..., dimensions={0} | all-to-all | bytes 589824 | tf_op jit(solution)/shard_map/all_to_all | solution.py:35
  126.4 0.7 finish.1
  (57 shorter events, 1.6 us)
Async XLA Ops:
  2.2 5.0 %copy-start = (bf16[2,128,1536]{2,1,0:T(8,128)(2,1)S(1)}, bf16[2,128,1536]{2,1,0:T(8,128)(2,1)}, u32[]{:S(2)}) copy-start(bf16[2,128,1536]{2,1,0:T(8,128)(2,1)} %hidden.1) | copy-start | bytes 2359300
  2.2 13.3 %all-to-all-start = ((bf16[4,2,128,384]{3,2,1,0:T(8,128)(2,1)}), bf16[4,2,128,384]{3,2,1,0:T(8,128)(2,1)S(1)}, u32[]{:S(2)}, u32[]{:S(2)}) async-start(bf16[4,2,128,384]{3,2,1,0:T(8,128)(2,1)} %pack.1), calls=%async_computation | async-start | bytes 1572864 | tf_op jit(solution)/shard_map/all_to_all | solution.py:58
  7.2 19.5 %copy-start.22 = (bf16[2,5,3072]{2,0,1:T(2,128)(2,1)S(1)}, bf16[2,5,3072]{2,0,1:T(2,128)(2,1)}, u32[]{:S(2)}) copy-start(bf16[2,5,3072]{2,0,1:T(2,128)(2,1)} %param.19) | copy-start | bytes 184324
  7.2 19.5 %copy-start.2 = (bf16[1,128,1536]{2,1,0:T(8,128)(2,1)S(1)}, bf16[1,128,1536]{2,1,0:T(8,128)(2,1)}, u32[]{:S(2)}) copy-start(bf16[1,128,1536]{2,1,0:T(8,128)(2,1)} %queries) | copy-start | bytes 1179652
  7.2 19.5 %copy-start.3 = (bf16[3072,64]{0,1:T(8,128)(2,1)S(1)}, bf16[3072,64]{0,1:T(8,128)(2,1)}, u32[]{:S(2)}) copy-start(bf16[3072,64]{0,1:T(8,128)(2,1)} %param.18) | copy-start | bytes 1179652
  7.3 19.5 %copy-start.4 = (f32[128,64]{0,1:T(8,128)S(1)}, f32[128,64]{0,1:T(8,128)}, u32[]{:S(2)}) copy-start(f32[128,64]{0,1:T(8,128)} %param.25) | copy-start | bytes 98308
  7.3 19.5 %copy-start.5 = (s32[5]{0:T(128)S(1)}, s32[5]{0:T(128)}, u32[]{:S(2)}) copy-start(s32[5]{0:T(128)} %spans.5) | copy-start | bytes 64
  7.3 19.5 %copy-start.7 = (s32[5]{0:T(128)S(1)}, s32[5]{0:T(128)}, u32[]{:S(2)}) copy-start(s32[5]{0:T(128)} %on.1) | copy-start | bytes 64
  7.3 19.5 %copy-start.8 = (f32[5]{0:T(128)S(1)}, f32[5]{0:T(128)}, u32[]{:S(2)}) copy-start(f32[5]{0:T(128)} %scales.1) | copy-start | bytes 64
  7.3 19.5 %copy-start.9 = (f32[5]{0:T(128)S(1)}, f32[5]{0:T(128)}, u32[]{:S(2)}) copy-start(f32[5]{0:T(128)} %strides.1) | copy-start | bytes 64
  7.3 19.4 %collective-permute-start.6 = (bf16[128,1536]{1,0:T(8,128)(2,1)S(1)}, bf16[128,1536]{1,0:T(8,128)(2,1)S(1)}, u32[]{:S(2)}, u32[]{:S(2)}) collective-permute-start(bf16[128,1536]{1,0:T(8,128)(2,1)S(1)} %dynamic-slice_bitcast_fusion), channel_id=1, source_target_pairs={{0,256},{256,0},{1,257},{257,1},{2,258},{258,2},{3,259},{259,3},{4... | collective-permute-start | bytes 1179656 | tf_op jit(solution)/shard_map/ppermute | solution.py:19
  15.5 26.4 %copy-start.10 = (bf16[4,2,128,384]{3,2,1,0:T(8,128)(2,1)}, bf16[4,2,128,384]{3,2,1,0:T(8,128)(2,1)S(1)}, u32[]{:S(2)}) copy-start(bf16[4,2,128,384]{3,2,1,0:T(8,128)(2,1)S(1)} %all-to-all-done.own) | copy-start | bytes 2359300
  16.8 17.7 %collective-permute-start.3 = (bf16[3,2,128,384]{3,2,1,0:T(8,128)(2,1)}, bf16[3,2,128,384]{3,2,1,0:T(8,128)(2,1)}, u32[]{:S(2)}, u32[]{:S(2)}) collective-permute-start(bf16[3,2,128,384]{3,2,1,0:T(8,128)(2,1)} %get-tuple-element.33), channel_id=1, source_target_pairs={{32,0},{40,8},{48,16},{56,24},{64,32},{72,40},{80,48},{88,56},{96,... | collective-permute-start | bytes 1769480 | tf_op jit(solution)/shard_map/ppermute | solution.py:26
  18.1 17.7 %collective-permute-start = (bf16[3,2,128,384]{3,2,1,0:T(8,128)(2,1)}, bf16[3,2,128,384]{3,2,1,0:T(8,128)(2,1)}, u32[]{:S(2)}, u32[]{:S(2)}) collective-permute-start(bf16[3,2,128,384]{3,2,1,0:T(8,128)(2,1)} %get-tuple-element.34), channel_id=1, source_target_pairs={{0,32},{8,40},{16,48},{24,56},{32,64},{40,72},{48,80},{56,88},{64,... | collective-permute-start | bytes 1769480 | tf_op jit(solution)/shard_map/ppermute | solution.py:26
  26.7 4.2 %copy-start.6 = (s32[2]{0:T(128)}, s32[2]{0:T(128)S(1)}, u32[]{:S(2)}) copy-start(s32[2]{0:T(128)S(1)} %pad_add_fusion.where) | copy-start | bytes 28
  30.9 25.5 %all-to-all-start.2 = ((bf16[4,3,128,384]{3,2,1,0:T(8,128)(2,1)}), bf16[4,3,128,384]{3,2,1,0:T(8,128)(2,1)S(1)}, u32[]{:S(2)}, u32[]{:S(2)}) async-start(bf16[4,3,128,384]{3,2,1,0:T(8,128)(2,1)} %get-tuple-element.22), calls=%async_computation.2 | async-start | bytes 2359296 | tf_op jit(solution)/shard_map/all_to_all | solution.py:58
  34.5 21.8 %collective-permute-start.5 = (bf16[3,2,128,384]{3,2,1,0:T(8,128)(2,1)}, bf16[3,2,128,384]{3,2,1,0:T(8,128)(2,1)S(1)}, u32[]{:S(2)}, u32[]{:S(2)}) collective-permute-start(bf16[3,2,128,384]{3,2,1,0:T(8,128)(2,1)} %collective-permute-done.3.near_r), channel_id=1, source_target_pairs={{32,0},{40,8},{48,16},{56,24},{64,32},{72,40},{80,48},{88,56},{96,... | collective-permute-start | bytes 1769480 | tf_op jit(solution)/shard_map/ppermute | solution.py:26
  35.8 20.6 %collective-permute-start.1 = (bf16[3,2,128,384]{3,2,1,0:T(8,128)(2,1)}, bf16[3,2,128,384]{3,2,1,0:T(8,128)(2,1)S(1)}, u32[]{:S(2)}, u32[]{:S(2)}) collective-permute-start(bf16[3,2,128,384]{3,2,1,0:T(8,128)(2,1)} %collective-permute-done.near_l), channel_id=1, source_target_pairs={{0,32},{8,40},{16,48},{24,56},{32,64},{40,72},{48,80},{56,88},{64,... | collective-permute-start | bytes 1769480 | tf_op jit(solution)/shard_map/ppermute | solution.py:26
  42.0 13.5 %collective-permute-start.4 = (bf16[1,2,128,384]{3,2,1,0:T(8,128)(2,1)S(1)}, bf16[1,2,128,384]{3,2,1,0:T(8,128)(2,1)S(1)}, u32[]{:S(2)}, u32[]{:S(2)}) collective-permute-start(bf16[1,2,128,384]{3,2,1,0:T(8,128)(2,1)S(1)} %get-tuple-element.31), channel_id=1, source_target_pairs={{32,0},{40,8},{48,16},{56,24},{64,32},{72,40},{80,48},{88,56},{96,... | collective-permute-start | bytes 589832 | tf_op jit(solution)/shard_map/ppermute | solution.py:26
  43.3 13.1 %collective-permute-start.2 = (bf16[1,2,128,384]{3,2,1,0:T(8,128)(2,1)S(1)}, bf16[1,2,128,384]{3,2,1,0:T(8,128)(2,1)S(1)}, u32[]{:S(2)}, u32[]{:S(2)}) collective-permute-start(bf16[1,2,128,384]{3,2,1,0:T(8,128)(2,1)S(1)} %get-tuple-element.32), channel_id=1, source_target_pairs={{0,32},{8,40},{16,48},{24,56},{32,64},{40,72},{48,80},{56,88},{64,... | collective-permute-start | bytes 589832 | tf_op jit(solution)/shard_map/ppermute | solution.py:26
  55.5 14.0 %copy-start.19 = (bf16[1,2,128,384]{3,2,1,0:T(8,128)(2,1)}, bf16[1,2,128,384]{3,2,1,0:T(8,128)(2,1)S(1)}, u32[]{:S(2)}) copy-start(bf16[1,2,128,384]{3,2,1,0:T(8,128)(2,1)S(1)} %collective-permute-done.4.one_r) | copy-start | bytes 589828
  57.9 40.8 %all-to-all-start.1 = ((bf16[8,48,1536]{2,1,0:T(8,128)(2,1)}), bf16[8,48,1536]{2,1,0:T(8,128)(2,1)S(1)}, u32[]{:S(2)}, u32[]{:S(2)}) async-start(bf16[8,48,1536]{2,1,0:T(8,128)(2,1)} %broadcast_in_dim.3), calls=%async_computation.1 | async-start | bytes 2359296 | tf_op jit(solution)/shard_map/all_to_all | solution.py:64
  77.8 20.8 %collective-permute-start.8 = (bf16[4,128,384]{2,1,0:T(8,128)(2,1)}, bf16[4,128,384]{2,1,0:T(8,128)(2,1)S(1)}, u32[]{:S(2)}, u32[]{:S(2)}) collective-permute-start(bf16[4,128,384]{2,1,0:T(8,128)(2,1)} %attend.1.own), channel_id=1, source_target_pairs={{0,24},{8,0},{16,8},{24,16},{32,56},{40,32},{48,40},{56,48},{64,88... | collective-permute-start | bytes 1179656 | tf_op jit(solution)/shard_map/ppermute | solution.py:41
  80.6 18.0 %collective-permute-start.7 = (bf16[4,128,384]{2,1,0:T(8,128)(2,1)}, bf16[4,128,384]{2,1,0:T(8,128)(2,1)S(1)}, u32[]{:S(2)}, u32[]{:S(2)}) collective-permute-start(bf16[4,128,384]{2,1,0:T(8,128)(2,1)} %attend.1.own), channel_id=1, source_target_pairs={{0,8},{8,16},{16,24},{24,0},{32,40},{40,48},{48,56},{56,32},{64,72... | collective-permute-start | bytes 1179656 | tf_op jit(solution)/shard_map/ppermute | solution.py:41
  84.2 9.9 %collective-permute-start.10 = (bf16[2,128,384]{2,1,0:T(8,128)(2,1)S(1)}, bf16[2,128,384]{2,1,0:T(8,128)(2,1)S(1)}, u32[]{:S(2)}, u32[]{:S(2)}) collective-permute-start(bf16[2,128,384]{2,1,0:T(8,128)(2,1)S(1)} %get-tuple-element.35), channel_id=1, source_target_pairs={{0,16},{8,24},{16,0},{24,8},{32,48},{40,56},{48,32},{56,40},{64,80... | collective-permute-start | bytes 589832 | tf_op jit(solution)/shard_map/ppermute | solution.py:41
  86.8 11.8 %collective-permute-start.9 = (bf16[2,128,384]{2,1,0:T(8,128)(2,1)S(1)}, bf16[2,128,384]{2,1,0:T(8,128)(2,1)S(1)}, u32[]{:S(2)}, u32[]{:S(2)}) collective-permute-start(bf16[2,128,384]{2,1,0:T(8,128)(2,1)S(1)} %get-tuple-element.36), channel_id=1, source_target_pairs={{0,16},{8,24},{16,0},{24,8},{32,48},{40,56},{48,32},{56,40},{64,80... | collective-permute-start | bytes 589832 | tf_op jit(solution)/shard_map/ppermute | solution.py:41
  94.1 14.1 %copy-start.18 = (bf16[2,128,384]{2,1,0:T(8,128)(2,1)}, bf16[2,128,384]{2,1,0:T(8,128)(2,1)S(1)}, u32[]{:S(2)}) copy-start(bf16[2,128,384]{2,1,0:T(8,128)(2,1)S(1)} %collective-permute-done.10.far_b) | copy-start | bytes 589828
  98.6 9.6 %copy-start.20 = (bf16[2,128,384]{2,1,0:T(8,128)(2,1)}, bf16[2,128,384]{2,1,0:T(8,128)(2,1)S(1)}, u32[]{:S(2)}) copy-start(bf16[2,128,384]{2,1,0:T(8,128)(2,1)S(1)} %collective-permute-done.9.far_a) | copy-start | bytes 589828
  98.6 9.6 %copy-start.16 = (bf16[4,128,384]{2,1,0:T(8,128)(2,1)}, bf16[4,128,384]{2,1,0:T(8,128)(2,1)S(1)}, u32[]{:S(2)}) copy-start(bf16[4,128,384]{2,1,0:T(8,128)(2,1)S(1)} %collective-permute-done.8.ahead) | copy-start | bytes 1179652
  98.7 9.6 %copy-start.17 = (bf16[4,128,384]{2,1,0:T(8,128)(2,1)}, bf16[4,128,384]{2,1,0:T(8,128)(2,1)S(1)}, u32[]{:S(2)}) copy-start(bf16[4,128,384]{2,1,0:T(8,128)(2,1)S(1)} %collective-permute-done.7.behind) | copy-start | bytes 1179652
  98.7 9.6 %copy-start.12 = (bf16[8,48,1536]{2,1,0:T(8,128)(2,1)}, bf16[8,48,1536]{2,1,0:T(8,128)(2,1)S(1)}, u32[]{:S(2)}) copy-start(bf16[8,48,1536]{2,1,0:T(8,128)(2,1)S(1)} %all-to-all-done.1) | copy-start | bytes 3538948
  98.7 9.6 %collective-permute-start.11 = (bf16[384,1536]{1,0:T(8,128)(2,1)S(1)}, bf16[384,1536]{1,0:T(8,128)(2,1)S(1)}, u32[]{:S(2)}, u32[]{:S(2)}) collective-permute-start(bf16[384,1536]{1,0:T(8,128)(2,1)S(1)} %bitcast.11), channel_id=1, source_target_pairs={{0,256},{256,0},{1,257},{257,1},{2,258},{258,2},{3,259},{259,3},{4... | collective-permute-start | bytes 3538952 | tf_op jit(solution)/shard_map/ppermute | solution.py:19
  (6 other events, 6.1 us)
